TPU v7x, 32 devices: a whole 2x2x4 slice. The times are simulated.
32 devices in a mesh: dp: 16 (over z, y, x), fsdp: 2 (over core).
Axes of the slice: x: 2, y: 2, z: 4, core: 2. Of those that a mesh axis runs over, the one named last changes fastest.
Arguments:
- tokens: bfloat16 [8192, 768], P(('dp', 'fsdp')), may hold values from -6 to 6
- cotangent: bfloat16 [8192, 768], P(('dp', 'fsdp')), may hold values from -6 to 6
- lengths: int32 [32, 6], P(('dp', 'fsdp')), may hold values from 1 to 160, 256 in all within a row
- mix_weight: float32 [768, 2304], P(None, ('dp', 'fsdp')), may hold values from -0.21875 to 0.21875
- out_weight: float32 [768, 768], P(('dp', 'fsdp')), may hold values from -0.875 to 0.875
- up_weight: float32 [768, 3072], P(None, ('dp', 'fsdp')), may hold values from -0.21875 to 0.21875
- down_weight: float32 [3072, 768], P(('dp', 'fsdp')), may hold values from -0.109375 to 0.109375
- norm_params: float32 [4, 768], replicated, may hold values from 0.5 to 1.5
- mix_first: float32 [768, 2304], P(None, ('dp', 'fsdp')), may hold values from -0.00061035156 to 0.00061035156
- out_first: float32 [768, 768], P(('dp', 'fsdp')), may hold values from -0.00061035156 to 0.00061035156
- up_first: float32 [768, 3072], P(None, ('dp', 'fsdp')), may hold values from -0.00061035156 to 0.00061035156
- down_first: float32 [3072, 768], P(('dp', 'fsdp')), may hold values from -0.00061035156 to 0.00061035156
- norm_first: float32 [4, 768], replicated, may hold values from -0.0029296875 to 0.0029296875
- mix_second: float32 [768, 2304], P(None, ('dp', 'fsdp')), may hold values from 7.4283713e-09 to 2.9656995e-08
- out_second: float32 [768, 768], P(('dp', 'fsdp')), may hold values from 7.4283713e-09 to 2.9656995e-08
- up_second: float32 [768, 3072], P(None, ('dp', 'fsdp')), may hold values from 7.4283713e-09 to 2.9656995e-08
- down_second: float32 [3072, 768], P(('dp', 'fsdp')), may hold values from 7.4283713e-09 to 2.9656995e-08
- norm_second: float32 [4, 768], replicated, may hold values from 1.8359093e-07 to 7.4848606e-07
Outputs:
- output: bfloat16 [8192, 768], P(('dp', 'fsdp'))
- grad_tokens: float32 [8192, 768], P(('dp', 'fsdp'))
- global_norm: float32 [], replicated
- new_mix: float32 [768, 2304], P(None, ('dp', 'fsdp'))
- new_out: float32 [768, 768], P(('dp', 'fsdp'))
- new_up: float32 [768, 3072], P(None, ('dp', 'fsdp'))
- new_down: float32 [3072, 768], P(('dp', 'fsdp'))
- new_norm: float32 [4, 768], replicated
- mix_first_new: float32 [768, 2304], P(None, ('dp', 'fsdp'))
- out_first_new: float32 [768, 768], P(('dp', 'fsdp'))
- up_first_new: float32 [768, 3072], P(None, ('dp', 'fsdp'))
- down_first_new: float32 [3072, 768], P(('dp', 'fsdp'))
- norm_first_new: float32 [4, 768], replicated
- mix_second_new: float32 [768, 2304], P(None, ('dp', 'fsdp'))
- out_second_new: float32 [768, 768], P(('dp', 'fsdp'))
- up_second_new: float32 [768, 3072], P(None, ('dp', 'fsdp'))
- down_second_new: float32 [3072, 768], P(('dp', 'fsdp'))
- norm_second_new: float32 [4, 768], replicated
Inputs may be any that keep to these rules, and one draw needn't show every extreme that they name: In each row the first 5 entries are sequence lengths and the last is the padding at the buffer's end; the row sums to 256.
All inputs are finite; a program needn't handle non-finite values.
Results may differ from a plain program's by a relative error of at most 0.007.
Values may be sent and summed in bfloat16 or wider, within the bound.
No kernel may reach another device: no remote copies, remote signals or barrier semaphores. Data moves between devices by JAX's collectives and lax.ppermute only.
A program may use at most 192 MiB of HBM per device.

v0:
```python
import math

import jax
import jax.numpy as jnp
from jax import lax
from jax.sharding import PartitionSpec as P

DH = 64
STEP = 10


HIGH = lax.Precision.HIGHEST
RATES = (0.01, 0.08, 0.01, 0.01, 0.2)
DECAYS = (0.1, 0.1, 0.1, 0.1, 0.0)


def segment_tables(lengths, rows):
    ends = jnp.cumsum(lengths)
    starts = ends - lengths
    places = jnp.arange(rows, dtype=jnp.int32)
    inside = (places[None, :] >= starts[:, None]) & (places[None, :] < ends[:, None])
    member = inside[:-1].astype(jnp.float32)
    live = jnp.sum(member, axis=0)
    offset = places.astype(jnp.float32) - jnp.sum(
        member * starts[:-1, None].astype(jnp.float32), axis=0
    )
    extent = jnp.sum(member * lengths[:-1, None].astype(jnp.float32), axis=0) + (1.0 - live)
    angle = 0.5 * math.pi * offset / extent
    return (member, live, angle)


def cos_attention(queries, keys, values, member, live, angle):
    rows = queries.shape[0]
    feat_q = jax.nn.softplus(queries).reshape(rows, -1, DH)
    feat_k = jax.nn.softplus(keys).reshape(rows, -1, DH)
    vals = values.reshape(rows, -1, DH)
    phases = jnp.stack([jnp.cos(angle), jnp.sin(angle)])
    weighted = member[None] * phases[:, None, :]
    scaled = jnp.einsum("psr,rhd->psrhd", weighted, feat_k)
    state = jnp.einsum("psrhd,rhe->pshde", scaled, vals, precision=HIGH)
    normal = jnp.sum(scaled, axis=2)
    query_side = feat_q[None] * phases[:, :, None, None]
    per_slot = jnp.einsum("prhd,pshde->rshe", query_side, state, precision=HIGH)
    numer = jnp.einsum("sr,rshe->rhe", member, per_slot, precision=HIGH)
    slot_den = jnp.einsum("prhd,pshd->rsh", query_side, normal, precision=HIGH)
    denom = jnp.einsum("sr,rsh->rh", member, slot_den, precision=HIGH) + (1.0 - live)[:, None]
    return (numer / denom[:, :, None]).reshape(rows, -1)


def layer_norm(hidden, gain, shift):
    centered = hidden - jnp.mean(hidden, axis=-1, keepdims=True)
    spread = jnp.mean(centered * centered, axis=-1, keepdims=True)
    return centered * lax.rsqrt(spread + 1e-05) * gain + shift


def gelu_tanh(values):
    return jax.nn.gelu(values, approximate=True)


def inner_rows(left, right):
    return lax.dot_general(
        left, right, (((0,), (0,)), ((), ())), preferred_element_type=jnp.float32
    )


def times_transpose(left, right):
    return lax.dot_general(
        left, right, (((1,), (1,)), ((), ())), preferred_element_type=jnp.float32
    )


def by_owner_rows(grad, owners):
    return grad.reshape(owners, -1, 128)


def by_owner_columns(grad, owners):
    height, across = grad.shape
    split = grad.reshape(height, owners, across // owners)
    return jnp.transpose(split, (1, 0, 2)).reshape(owners, -1, 128)


def unpack_owned(packed, shapes):
    pieces = []
    offset = 0
    for shape in shapes:
        blocks = shape[0] * shape[1] // 128
        pieces.append(packed[0, offset : offset + blocks].reshape(shape))
        offset = offset + blocks
    return pieces


def adamw(weight, grad, first, second, rate, decay):
    first_new = 0.9 * first + 0.1 * grad
    second_new = 0.95 * second + 0.05 * grad * grad
    step_dir = first_new / (1.0 - 0.9**STEP) / (jnp.sqrt(second_new / (1.0 - 0.95**STEP)) + 1e-08)
    return (weight - rate * (step_dir + decay * weight), first_new, second_new)


def on_device(
    tokens,
    cotangent,
    lengths,
    mix_weight,
    out_weight,
    up_weight,
    down_weight,
    norm_params,
    mix_first,
    out_first,
    up_first,
    down_first,
    norm_first,
    mix_second,
    out_second,
    up_second,
    down_second,
    norm_second,
):
    rows, width = tokens.shape
    owners = lax.axis_size(("dp", "fsdp"))
    rounded = (
        mix_weight.astype(jnp.bfloat16),
        out_weight.astype(jnp.bfloat16),
        up_weight.astype(jnp.bfloat16),
        down_weight.astype(jnp.bfloat16),
    )
    mix_full, out_full, up_full, down_full = (
        lax.all_gather(rounded[0], ("dp", "fsdp"), axis=1, tiled=True),
        lax.all_gather(rounded[1], ("dp", "fsdp"), axis=0, tiled=True),
        lax.all_gather(rounded[2], ("dp", "fsdp"), axis=1, tiled=True),
        lax.all_gather(rounded[3], ("dp", "fsdp"), axis=0, tiled=True),
    )
    member, live, angle = segment_tables(lengths[0], rows)
    mixed = jnp.dot(tokens, mix_full, preferred_element_type=jnp.float32)

    def attend(queries, keys, values):
        return cos_attention(queries, keys, values, member, live, angle)

    attended, attention_pull = jax.vjp(
        attend, mixed[:, :width], mixed[:, width : 2 * width], mixed[:, 2 * width :]
    )
    attended_low = attended.astype(jnp.bfloat16)
    branch = jnp.dot(attended_low, out_full, preferred_element_type=jnp.float32)
    first, first_pull = jax.vjp(
        layer_norm, tokens.astype(jnp.float32) + branch, norm_params[0], norm_params[1]
    )
    first_low = first.astype(jnp.bfloat16)
    upper = jnp.dot(first_low, up_full, preferred_element_type=jnp.float32)
    hidden, gelu_pull = jax.vjp(gelu_tanh, upper)
    hidden_low = hidden.astype(jnp.bfloat16)
    second = jnp.dot(hidden_low, down_full, preferred_element_type=jnp.float32)
    final, final_pull = jax.vjp(layer_norm, first + second, norm_params[2], norm_params[3])
    output = (final * live[:, None]).astype(jnp.bfloat16)
    mix_full, out_full, up_full, down_full = (
        lax.all_gather(rounded[0], ("dp", "fsdp"), axis=1, tiled=True),
        lax.all_gather(rounded[1], ("dp", "fsdp"), axis=0, tiled=True),
        lax.all_gather(rounded[2], ("dp", "fsdp"), axis=1, tiled=True),
        lax.all_gather(rounded[3], ("dp", "fsdp"), axis=0, tiled=True),
    )
    grad_final = cotangent.astype(jnp.float32) * live[:, None]
    grad_sum_two, grad_gain_two, grad_bias_two = final_pull(grad_final)
    grad_second = grad_sum_two.astype(jnp.bfloat16)
    grad_down = inner_rows(hidden_low, grad_second)
    grad_hidden = times_transpose(grad_second, down_full)
    (grad_upper,) = gelu_pull(grad_hidden)
    grad_upper_low = grad_upper.astype(jnp.bfloat16)
    grad_up = inner_rows(first_low, grad_upper_low)
    grad_first = grad_sum_two + times_transpose(grad_upper_low, up_full)
    grad_sum_one, grad_gain_one, grad_bias_one = first_pull(grad_first)
    grad_branch = grad_sum_one.astype(jnp.bfloat16)
    grad_out = inner_rows(attended_low, grad_branch)
    grad_attended = times_transpose(grad_branch, out_full)
    grad_q, grad_k, grad_v = attention_pull(grad_attended)
    grad_mixed = jnp.concatenate([grad_q, grad_k, grad_v], axis=1).astype(jnp.bfloat16)
    grad_mix = inner_rows(tokens, grad_mixed)
    grad_tokens = grad_sum_one + times_transpose(grad_mixed, mix_full)
    norm_terms = jnp.stack([grad_gain_one, grad_bias_one, grad_gain_two, grad_bias_two])
    norm_grad = lax.psum(norm_terms, ("dp", "fsdp"))
    packed_all = jnp.concatenate(
        [
            by_owner_columns(grad_mix, owners),
            by_owner_rows(grad_out, owners),
            by_owner_columns(grad_up, owners),
            by_owner_rows(grad_down, owners),
        ],
        axis=1,
    )
    summed_all = lax.psum_scatter(packed_all, ("dp", "fsdp"), scatter_dimension=0, tiled=True)
    owned = tuple(
        unpack_owned(
            summed_all, (mix_weight.shape, out_weight.shape, up_weight.shape, down_weight.shape)
        )
    )
    local_sq = sum((jnp.sum(g * g) for g in owned))
    owned_sq = lax.psum(local_sq, ("dp", "fsdp"))
    global_norm = jnp.sqrt(owned_sq + jnp.sum(norm_grad * norm_grad))
    scale = 1.0 / jnp.maximum(global_norm, 1.0)
    params = (mix_weight, out_weight, up_weight, down_weight, norm_params)
    grads = (owned[0], owned[1], owned[2], owned[3], norm_grad)
    firsts = (mix_first, out_first, up_first, down_first, norm_first)
    seconds = (mix_second, out_second, up_second, down_second, norm_second)
    news = []
    for index in range(5):
        news.append(
            adamw(
                params[index],
                scale * grads[index],
                firsts[index],
                seconds[index],
                RATES[index],
                DECAYS[index],
            )
        )
    return (
        output,
        grad_tokens,
        global_norm,
        news[0][0],
        news[1][0],
        news[2][0],
        news[3][0],
        news[4][0],
        news[0][1],
        news[1][1],
        news[2][1],
        news[3][1],
        news[4][1],
        news[0][2],
        news[1][2],
        news[2][2],
        news[3][2],
        news[4][2],
    )


def solution(mesh):
    in_specs = (
        P(("dp", "fsdp"), None),
        P(("dp", "fsdp"), None),
        P(("dp", "fsdp"), None),
        P(None, ("dp", "fsdp")),
        P(("dp", "fsdp"), None),
        P(None, ("dp", "fsdp")),
        P(("dp", "fsdp"), None),
        P(),
        P(None, ("dp", "fsdp")),
        P(("dp", "fsdp"), None),
        P(None, ("dp", "fsdp")),
        P(("dp", "fsdp"), None),
        P(),
        P(None, ("dp", "fsdp")),
        P(("dp", "fsdp"), None),
        P(None, ("dp", "fsdp")),
        P(("dp", "fsdp"), None),
        P(),
    )
    out_specs = (
        P(("dp", "fsdp"), None),
        P(("dp", "fsdp"), None),
        P(),
        P(None, ("dp", "fsdp")),
        P(("dp", "fsdp"), None),
        P(None, ("dp", "fsdp")),
        P(("dp", "fsdp"), None),
        P(),
        P(None, ("dp", "fsdp")),
        P(("dp", "fsdp"), None),
        P(None, ("dp", "fsdp")),
        P(("dp", "fsdp"), None),
        P(),
        P(None, ("dp", "fsdp")),
        P(("dp", "fsdp"), None),
        P(None, ("dp", "fsdp")),
        P(("dp", "fsdp"), None),
        P(),
    )
    return jax.shard_map(
        on_device, mesh=mesh, in_specs=in_specs, out_specs=out_specs, check_vma=False
    )
```

profile of v0, /device:TPU:0, one launch (start us, length us, event | category | flops | bytes accessed | tf_op | source)
XLA Modules:
  0.0 753.8 jit_solution(2711216363849771369)
XLA Ops:
  18.8 55.5 %all-gather.5.cloned.1.call-done = bf16[768,2304]{0,1:T(8,128)(2,1)} async-done(((bf16[768,72]{0,1:T(8,128)(2,1)}), bf16[768,2304]{0,1:T(8,128)(2,1)}) %all-gather.5.cloned.1.call-update) | async-done | bytes 3538960 | tf_op jit(solution)/shard_map/all_gather | solution.py:128
  74.3 3.2 fusion.120
  83.4 12.0 %fusion.3 = f32[12,64,2,5,64]{4,1,3,2,0:T(8,128)S(1)} fusion(f32[256,12,64,1,1]{0,2,4,3,1:T(8,128)S(1)} %bitcast.176, f32[256,2,5]{0,1,2:T(2,128)S(1)} %multiply_bitcast_fusion.20, f32[256,12,64]{0,2,1:T(8,128)S(1)} %bitcast.170), kind=kOutput, calls=%fused_computation.5 | convolution fusion | flops 1511915520 | bytes 3549184 | tf_op jit(solution)/shard_map/jvp(psrhd,rhe->pshde)/dot_general | solution.py:40
  97.4 3.7 fusion.9
  101.9 28.7 %all-gather.7.cloned.1.call-done = bf16[768,768]{1,0:T(8,128)(2,1)} async-done(((bf16[24,768]{1,0:T(8,128)(2,1)}), bf16[768,768]{1,0:T(8,128)(2,1)}) %all-gather.7.cloned.1.call-update) | async-done | bytes 1179664 | tf_op jit(solution)/shard_map/all_gather | solution.py:129
  134.5 62.2 %all-gather.9.cloned.1.call-done = bf16[768,3072]{0,1:T(8,128)(2,1)} async-done(((bf16[768,96]{0,1:T(8,128)(2,1)}), bf16[768,3072]{0,1:T(8,128)(2,1)}) %all-gather.9.cloned.1.call-update) | async-done | bytes 4718608 | tf_op jit(solution)/shard_map/all_gather | solution.py:130
  196.7 5.5 fusion.108
  202.2 60.3 %all-gather.11.cloned.1.call-done = bf16[3072,768]{1,0:T(8,128)(2,1)} async-done(((bf16[96,768]{1,0:T(8,128)(2,1)}), bf16[3072,768]{1,0:T(8,128)(2,1)}) %all-gather.11.cloned.1.call-update) | async-done | bytes 4718608 | tf_op jit(solution)/shard_map/all_gather | solution.py:131
  262.6 5.5 fusion.119
  270.6 4.1 fusion.28
  274.8 2.2 multiply_reduce_fusion.1
  278.3 2.6 fusion.82
  280.8 2.6 fusion.50
  283.4 5.9 fusion.102
  289.3 5.1 fusion.106
  296.4 4.4 fusion.31
  300.8 6.2 fusion.44
  308.0 9.1 %fusion.36 = f32[256,12,64]{0,2,1:T(8,128)S(1)} fusion(f32[12,256,2,64]{1,3,2,0:T(8,128)} %fusion.82, f32[12,64,2,5,64]{4,1,3,2,0:T(8,128)} %copy-done, f32[256,5]{0,1:T(8,128)S(1)} %get-tuple-element.148, f32[256,12,64]{0,2,1:T(8,128)S(1)} %copy-done.6, f32[2,256]{1,0:T(2,128)S(1)} %copy-done.44), kind=kOutput, calls=%fused_computation.52 | convolution fusion | flops 1511915520 | bytes 5118976 | tf_op jit(solution)/shard_map/transpose(jvp(prhd,pshde->rshe))/dot_general | solution.py:43
  317.4 9.6 %fusion.2 = f32[256,12,64]{0,2,1:T(8,128)S(1)} fusion(f32[256,2,5]{0,2,1:T(8,128)} %copy.190, f32[12,64,2,5]{1,3,2,0:T(8,128)} %fusion.50, f32[256,12,64,1,1]{0,2,4,3,1:T(8,128)S(1)} %bitcast.177, f32[12,64,2,5,64]{4,1,2,3,0:T(8,128)} %copy-done.10), kind=kOutput, calls=%fused_computation.4 | convolution fusion | flops 1515651072 | bytes 3579904 | tf_op jit(solution)/shard_map/transpose(jvp(psrhd,rhe->pshde))/dot_general | solution.py:40
  328.2 10.8 %reshape.281 = f32[32,576,128]{2,1,0:T(8,128)} reshape(f32[3072,768]{1,0:T(8,128)} %fusion.102) | data formatting | bytes 18874368 | tf_op jit(solution)/shard_map/reshape | solution.py:73
  339.0 11.5 %copy.147 = f32[32,768,96]{2,1,0:T(8,128)} copy(f32[32,768,96]{1,2,0:T(8,128)} %bitcast.164) | data formatting | bytes 18874368 | tf_op jit(solution)/shard_map/transpose | solution.py:79
  350.5 14.2 %reshape.280 = f32[32,576,128]{2,1,0:T(8,128)} reshape(f32[32,768,96]{2,1,0:T(8,128)} %copy.147) | data formatting | bytes 18874368 | tf_op jit(solution)/shard_map/reshape | solution.py:79
  364.7 3.4 reshape.278
  368.1 2.4 fusion.66
  370.5 4.0 fusion.78
  374.5 10.0 %copy.145 = f32[768,32,72]{2,0,1:T(8,128)} copy(f32[768,32,72]{0,2,1:T(8,128)} %bitcast.163) | data formatting | bytes 14155776 | tf_op jit(solution)/shard_map/reshape | solution.py:78
  384.5 14.9 %reshape.277 = f32[32,432,128]{2,1,0:T(8,128)} reshape(f32[32,768,72]{2,1,0:T(8,128)} %bitcast.162) | data formatting | bytes 14155776 | tf_op jit(solution)/shard_map/reshape | solution.py:79
  399.5 19.0 %pad_maximum_fusion = f32[32,1728,128]{2,1,0:T(8,128)} fusion(f32[32,576,128]{2,1,0:T(8,128)} %reshape.281, f32[32,576,128]{2,1,0:T(8,128)} %reshape.280, f32[32,144,128]{2,1,0:T(8,128)S(1)} %copy-done.4, f32[32,432,128]{2,1,0:T(8,128)} %reshape.277), kind=kLoop, calls=%fused_computation | loop fusion | flops 21233664 | bytes 56623104 | tf_op jit(solution)/shard_map/concatenate | solution.py:179
  421.6 259.8 %reduce-scatter.2.cloned.1.call-done = f32[1,1728,128]{2,1,0:T(8,128)} async-done(((f32[32,1728,128]{2,1,0:T(8,128)}), f32[1,1728,128]{2,1,0:T(8,128)}) %reduce-scatter.2.cloned.1.call-update) | async-done | bytes 884752 | tf_op jit(solution)/shard_map/reduce_scatter | solution.py:188
  688.9 4.0 convolution_add_fusion.1
  693.0 40.5 %all-reduce = (f32[]{:T(128)}, f32[4,768]{1,0:T(4,128)S(1)}) all-reduce(f32[]{:T(128)S(6)} %add.200, f32[4,768]{1,0:T(4,128)S(1)} %pad_maximum_fusion.4), channel_id=1, replica_groups=mesh['dp'=16,'fsdp'=2] {'dp','fsdp'}, use_global_device_ids=true, to_apply=%region_20.22 | all-reduce | flops 3073 | bytes 24584 | tf_op jit(solution)/shard_map/psum | solution.py:195
  742.0 2.2 multiply_subtract_fusion.2
  (220 shorter events, 48.6 us)
Async XLA Ops:
  7.2 67.1 %all-gather.5.cloned.1.call-start = ((), (), s32[]{:S(2)}) async-start(), calls=%async_computation.1 | async-start | bytes 3649536 | tf_op jit(solution)/shard_map/all_gather | solution.py:128
  8.9 121.8 %all-gather.7.cloned.1.call-start = ((), (), s32[]{:S(2)}) async-start(), calls=%async_computation.2 | async-start | bytes 1216512 | tf_op jit(solution)/shard_map/all_gather | solution.py:129
  10.4 186.3 %all-gather.9.cloned.1.call-start = ((), (), s32[]{:S(2)}) async-start(), calls=%async_computation.3 | async-start | bytes 4866048 | tf_op jit(solution)/shard_map/all_gather | solution.py:130
  12.2 250.4 %all-gather.11.cloned.1.call-start = ((), (), s32[]{:S(2)}) async-start(), calls=%async_computation.4 | async-start | bytes 4866048 | tf_op jit(solution)/shard_map/all_gather | solution.py:131
  13.9 667.6 %reduce-scatter.2.cloned.1.call-start = ((), (), s32[]{:S(2)}) async-start(), calls=%async_computation.5 | async-start | bytes 29196288 | tf_op jit(solution)/shard_map/reduce_scatter | solution.py:188
  16.3 65.5 %copy-start.41 = (f32[2,256]{1,0:T(2,128)}, f32[2,256]{1,0:T(2,128)S(1)}, u32[]{:S(2)}) copy-start(f32[2,256]{1,0:T(2,128)S(1)} %pad_maximum_fusion.5) | copy-start | bytes 6148
  16.4 65.4 %copy-start.46 = (f32[256,5]{0,1:T(8,128)}, f32[256,5]{0,1:T(8,128)S(1)}, u32[]{:S(2)}) copy-start(f32[256,5]{0,1:T(8,128)S(1)} %get-tuple-element.150) | copy-start | bytes 15364
  16.7 66.7 %copy-start.35 = (f32[256,2,5]{0,1,2:T(2,128)}, f32[256,2,5]{0,1,2:T(2,128)S(1)}, u32[]{:S(2)}) copy-start(f32[256,2,5]{0,1,2:T(2,128)S(1)} %multiply_bitcast_fusion.20) | copy-start | bytes 30724
  80.0 15.4 %copy-start.14 = (f32[256,768]{0,1:T(8,128)}, f32[256,768]{0,1:T(8,128)S(1)}, u32[]{:S(2)}) copy-start(f32[256,768]{0,1:T(8,128)S(1)} %copy.131) | copy-start | bytes 2359300
  82.8 14.6 %copy-start.42 = (f32[2,256]{1,0:T(2,128)S(1)}, f32[2,256]{1,0:T(2,128)}, u32[]{:S(2)}) copy-start(f32[2,256]{1,0:T(2,128)} %copy-done.41) | copy-start | bytes 6148
  82.8 14.6 %copy-start.47 = (f32[256,5]{0,1:T(8,128)S(1)}, f32[256,5]{0,1:T(8,128)}, u32[]{:S(2)}) copy-start(f32[256,5]{0,1:T(8,128)} %copy-done.46) | copy-start | bytes 15364
  83.4 17.7 %copy-start.37 = (f32[256,12]{0,1:T(8,128)}, f32[256,12]{0,1:T(8,128)S(1)}, u32[]{:S(2)}) copy-start(f32[256,12]{0,1:T(8,128)S(1)} %get-tuple-element.131) | copy-start | bytes 36868
  97.4 33.3 %copy-start.11 = (bf16[256,768]{1,0:T(8,128)(2,1)S(1)}, bf16[256,768]{1,0:T(8,128)(2,1)}, u32[]{:S(2)}) copy-start(bf16[256,768]{1,0:T(8,128)(2,1)} %param.19) | copy-start | bytes 1179652
  262.5 8.0 %copy-start.65 = (bf16[3072,768]{1,0:T(8,128)(2,1)S(1)}, bf16[3072,768]{1,0:T(8,128)(2,1)}, u32[]{:S(2)}) copy-start(bf16[3072,768]{1,0:T(8,128)(2,1)} %all-gather.11.cloned.1.call-done) | copy-start | bytes 14155780
  277.3 17.1 %copy-start.7 = (f32[256,768]{1,0:T(8,128)}, f32[256,768]{1,0:T(8,128)S(1)}, u32[]{:S(2)}) copy-start(f32[256,768]{1,0:T(8,128)S(1)} %get-tuple-element.133) | copy-start | bytes 2359300
  277.4 17.1 %copy-start.61 = (f32[256]{0:T(256)}, f32[256]{0:T(256)S(1)}, u32[]{:S(2)}) copy-start(f32[256]{0:T(256)S(1)} %negate_multiply_fusion) | copy-start | bytes 3076
  278.2 18.2 %copy-start.5 = (f32[256,12,64]{0,2,1:T(8,128)}, f32[256,12,64]{0,2,1:T(8,128)S(1)}, u32[]{:S(2)}) copy-start(f32[256,12,64]{0,2,1:T(8,128)S(1)} %get-tuple-element.147) | copy-start | bytes 2359300
  300.8 7.2 copy-start.6
  300.8 7.2 copy-start.44
  308.0 9.4 %copy-start.15 = (f32[256,768]{0,1:T(8,128)S(1)}, f32[256,768]{0,1:T(8,128)}, u32[]{:S(2)}) copy-start(f32[256,768]{0,1:T(8,128)} %copy-done.14) | copy-start | bytes 2359300
  384.5 14.9 %copy-start.4 = (f32[32,144,128]{2,1,0:T(8,128)S(1)}, f32[32,144,128]{2,1,0:T(8,128)}, u32[]{:S(2)}) copy-start(f32[32,144,128]{2,1,0:T(8,128)} %reshape.278) | copy-start | bytes 7077892
  418.6 270.3 %copy-start.8 = (f32[256,768]{1,0:T(8,128)S(1)}, f32[256,768]{1,0:T(8,128)}, u32[]{:S(2)}) copy-start(f32[256,768]{1,0:T(8,128)} %copy-done.7) | copy-start | bytes 2359300
  418.6 270.3 %copy-start.17 = (bf16[256,768]{1,0:T(8,128)(2,1)S(1)}, bf16[256,768]{1,0:T(8,128)(2,1)}, u32[]{:S(2)}) copy-start(bf16[256,768]{1,0:T(8,128)(2,1)} %copy.144) | copy-start | bytes 1179652
  418.6 270.3 %copy-start.19 = (bf16[256,768]{1,0:T(8,128)(2,1)S(1)}, bf16[256,768]{1,0:T(8,128)(2,1)}, u32[]{:S(2)}) copy-start(bf16[256,768]{1,0:T(8,128)(2,1)} %copy-done.18) | copy-start | bytes 1179652
  418.6 270.3 %copy-start.21 = (bf16[256,768]{1,0:T(8,128)(2,1)S(1)}, bf16[256,768]{1,0:T(8,128)(2,1)}, u32[]{:S(2)}) copy-start(bf16[256,768]{1,0:T(8,128)(2,1)} %copy-done.20) | copy-start | bytes 1179652
  418.6 270.3 %copy-start.62 = (f32[256]{0:T(256)S(1)}, f32[256]{0:T(256)}, u32[]{:S(2)}) copy-start(f32[256]{0:T(256)} %copy-done.61) | copy-start | bytes 3076
  688.9 46.5 %copy-start.12 = (f32[1,1728,128]{2,1,0:T(8,128)S(1)}, f32[1,1728,128]{2,1,0:T(8,128)}, u32[]{:S(2)}) copy-start(f32[1,1728,128]{2,1,0:T(8,128)} %reduce-scatter.2.cloned.1.call-done) | copy-start | bytes 2654212
  693.0 44.6 %copy-start.23 = (f32[768,96]{1,0:T(8,128)S(1)}, f32[768,96]{1,0:T(8,128)}, u32[]{:S(2)}) copy-start(f32[768,96]{1,0:T(8,128)} %copy.151) | copy-start | bytes 884740
  693.0 44.6 %copy-start.24 = (f32[768,96]{1,0:T(8,128)S(1)}, f32[768,96]{1,0:T(8,128)}, u32[]{:S(2)}) copy-start(f32[768,96]{1,0:T(8,128)} %copy.152) | copy-start | bytes 884740
  737.5 7.4 copy-start.26
  737.9 7.0 copy-start.33
  737.9 7.0 copy-start.34
  (41 other events, 138.8 us)
Sparse Core Ops, SparseCore 0:
  11.5 62.7 all-gather.4
  77.8 52.8 all-gather.6
  134.1 62.5 all-gather.8
  200.0 62.4 all-gather.10
  418.8 262.6 reduce-scatter.1
where the time goes:
time: 765 us; the launch traced here: 754 us
  waiting for transfers between devices  467 us (61%)
  matrix products  95.3 us (12%)
  local copies, waits for them, and re-layouts  82.7 us (11%)
  other arithmetic  48.6 us (6%)
  blocking collectives  40.5 us (5%)
  between operations  20 us (3%)
    reduce_scatter x1, waiting for transfers between devices, on_device(): lax.psum_scatter(packed_all, ('dp', 'fsdp'), scatter_dimension=0, tiled=T...  260 us
    all_gather x1, waiting for transfers between devices, on_device(): lax.all_gather(rounded[2], ('dp', 'fsdp'), axis=1, tiled=True)  62.2 us
    all_gather x1, waiting for transfers between devices, on_device(): lax.all_gather(rounded[3], ('dp', 'fsdp'), axis=0, tiled=True)  60.3 us
    all_gather x1, waiting for transfers between devices, on_device(): lax.all_gather(rounded[0], ('dp', 'fsdp'), axis=1, tiled=True)  55.5 us
    psum x1, blocking collectives, on_device(): owned_sq = lax.psum(local_sq, ('dp', 'fsdp'))  40.5 us
    reshape x2, local copies, waits for them, and re-layouts, by_owner_columns(): return jnp.transpose(split, (1, 0, 2)).reshape(owners, -1, 128)  29.2 us
    all_gather x1, waiting for transfers between devices, on_device(): lax.all_gather(rounded[1], ('dp', 'fsdp'), axis=0, tiled=True)  28.7 us
    dot_general x3, matrix products, cos_attention(): state = jnp.einsum('psrhd,rhe->pshde', scaled, vals, precision=HIGH)  27.9 us
  transfers between devices with their start and end apart: 5, of which 5 were waited for; matrix products, arithmetic and copies ran while one was open for 6% of the time, Pallas kernels for 0%

commit v1 on v0

--- a/solution.py
+++ b/solution.py
@@ -3,6 +3,8 @@
 import jax
 import jax.numpy as jnp
 from jax import lax
+from jax.experimental import pallas as pl
+from jax.experimental.pallas import tpu as pltpu
 from jax.sharding import PartitionSpec as P
 
 DH = 64
@@ -233,6 +235,555 @@
     )
 
 
+BF = jnp.bfloat16
+F32 = jnp.float32
+AXES = ("dp", "fsdp")
+CHIPS = 16
+BLOCK = 96
+QKV = 72
+PLANE = 4 * BLOCK
+ZROWS = 3 * BLOCK
+HALF = CHIPS * BLOCK
+STEPS_Z = (4, 8, 12)
+
+
+def nt(left, right):
+    return lax.dot_general(
+        left, right, (((1,), (1,)), ((), ())), preferred_element_type=F32
+    )
+
+
+def tn(left, right):
+    return lax.dot_general(
+        left, right, (((0,), (0,)), ((), ())), preferred_element_type=F32
+    )
+
+
+def nn(left, right):
+    return jnp.dot(left, right, preferred_element_type=F32)
+
+
+def block_places():
+    places = [(BLOCK * p, p, 0) for p in range(4)]
+    for p in range(4):
+        for j, step in enumerate(STEPS_Z):
+            places.append((PLANE + ZROWS * p + BLOCK * j, p, step))
+    return places
+
+
+PLACES = block_places()
+PIECES = [(0, PLANE)] + [(PLANE + ZROWS * p, ZROWS) for p in range(4)]
+
+
+def shard_index(chip, core, plane, step, other):
+    owner = 1 - core if other else core
+    first = 1 + owner
+    mask = (0, first, 3 - first, 3)[plane]
+    return 2 * (chip ^ mask ^ step) + owner
+
+
+def call(body, outs, args, scratch=(), smem=0, flops=0, moved=0, mb=56):
+    in_specs = [
+        pl.BlockSpec(memory_space=pltpu.SMEM if i < smem else pltpu.VMEM)
+        for i in range(len(args))
+    ]
+    return pl.pallas_call(
+        body,
+        out_shape=[jax.ShapeDtypeStruct(s, t) for s, t in outs],
+        in_specs=in_specs,
+        out_specs=[pl.BlockSpec(memory_space=pltpu.VMEM) for _ in outs],
+        scratch_shapes=list(scratch),
+        compiler_params=pltpu.CompilerParams(vmem_limit_bytes=mb << 20),
+        cost_estimate=pl.CostEstimate(flops=flops, bytes_accessed=moved, transcendentals=0),
+        name=body.__name__,
+    )(*args)
+
+
+def pack_weights(mix, out, up, down, s_ref, g1, g2, g3):
+    def flip(ref):
+        held = ref[...].astype(BF)
+        n = held.shape[1]
+        eye = (
+            lax.broadcasted_iota(jnp.int32, (n, n), 0)
+            == lax.broadcasted_iota(jnp.int32, (n, n), 1)
+        )
+        return nt(eye.astype(F32).astype(BF), held)
+
+    first = jnp.concatenate([flip(mix), out[...]], axis=0).astype(BF)
+    second = flip(up).astype(BF)
+    third = down[...].astype(BF)
+    s_ref[0:BLOCK, :] = first
+    s_ref[BLOCK : 2 * BLOCK, :] = second
+    s_ref[2 * BLOCK : 3 * BLOCK, :] = third
+    g1[...] = first
+    g2[...] = second
+    g3[...] = third
+
+
+def segment_of(lengths, place):
+    start = jnp.int32(0)
+    seg = jnp.full(place.shape, -1, jnp.int32)
+    offset = jnp.zeros(place.shape, F32)
+    extent = jnp.ones(place.shape, F32)
+    for s in range(5):
+        size = lengths[0, s]
+        inside = (place >= start) & (place < start + size)
+        seg = jnp.where(inside, s, seg)
+        offset = jnp.where(inside, (place - start).astype(F32), offset)
+        extent = jnp.where(inside, size.astype(F32), extent)
+        start = start + size
+    angle = 0.5 * math.pi * offset / extent
+    return seg, jnp.cos(angle), jnp.sin(angle)
+
+
+def pair_mask(lengths, rows):
+    seg_i, cos_i, sin_i = segment_of(lengths, lax.broadcasted_iota(jnp.int32, (1, rows), 1))
+    seg_j, cos_j, sin_j = segment_of(lengths, lax.broadcasted_iota(jnp.int32, (rows, 1), 0))
+    same = (seg_i == seg_j) & (seg_i >= 0)
+    dead = jnp.where(seg_i >= 0, 0.0, 1.0)
+    return jnp.where(same, cos_j * cos_i + sin_j * sin_i, 0.0), dead
+
+
+def softplus(v):
+    return jnp.maximum(v, 0.0) + jnp.log1p(jnp.exp(-jnp.abs(v)))
+
+
+def attend_forward(
+    lengths, me, x_ref, so, z0, z1, z2, z3, sp, y0, y1, y2, y3, norms,
+    mix, att, den, rel_own, rel_par, first, first_low, xhat, rstd,
+):
+    rows = x_ref.shape[0]
+    width = x_ref.shape[1]
+    chip, core = me[0], me[1]
+    x = x_ref[...]
+    sides = ((False, (so, z0, z1, z2, z3), rel_own), (True, (sp, y0, y1, y2, y3), rel_par))
+    for other, refs, _ in sides:
+        for (base, size), ref in zip(PIECES, refs):
+            got = nt(ref[...], x)
+            for at, plane, step in PLACES:
+                if base <= at < base + size:
+                    d = shard_index(chip, core, plane, step, other)
+                    mix[pl.ds(pl.multiple_of(QKV * d, 8), QKV), :] = got[
+                        at - base : at - base + QKV
+                    ]
+    mask, dead = pair_mask(lengths, rows)
+    for h in range(width // DH):
+        here = slice(DH * h, DH * h + DH)
+        fq = softplus(mix[here, :]).astype(BF)
+        fk = softplus(mix[width + DH * h : width + DH * h + DH, :]).astype(BF)
+        v = mix[2 * width + DH * h : 2 * width + DH * h + DH, :].astype(BF)
+        pairs = tn(fk, fq) * mask
+        total = jnp.sum(pairs, axis=0, keepdims=True) + dead
+        den[h : h + 1, :] = total
+        att[here, :] = nn(v, pairs.astype(BF)) / total
+    side = QKV // 3
+    blank = jnp.zeros((QKV, rows), F32)
+    branch = x.astype(F32)
+    for other, refs, rel in sides:
+        for at, plane, step in PLACES:
+            d = shard_index(chip, core, plane, step, other)
+            part = att[pl.ds(pl.multiple_of(side * d, 8), side), :]
+            rel[at : at + BLOCK, :] = jnp.concatenate([blank, part], axis=0).astype(BF)
+        for (base, size), ref in zip(PIECES, refs):
+            branch = branch + tn(rel[base : base + size, :], ref[...])
+    centered = branch - jnp.mean(branch, axis=-1, keepdims=True)
+    spread = jnp.mean(centered * centered, axis=-1, keepdims=True)
+    scale = lax.rsqrt(spread + 1e-05)
+    hat = centered * scale
+    xhat[...] = hat
+    rstd[...] = scale
+    out = hat * norms[0:1, :] + norms[1:2, :]
+    first[...] = out
+    first_low[...] = out.astype(BF)
+
+
+GELU_A = math.sqrt(2.0 / math.pi)
+GELU_B = 0.044715
+
+
+def feed_up(ya, yb, s, z0, z1, z2, z3, hid, slope):
+    rows = ya.shape[0]
+    for half, y in ((0, ya), (1, yb)):
+        cols = slice(half * rows, half * rows + rows)
+        for (base, size), ref in zip(PIECES, (s, z0, z1, z2, z3)):
+            u = nt(ref[...], y[...])
+            sq = u * u
+            t = jnp.tanh(GELU_A * u * (1.0 + GELU_B * sq))
+            half_up = 0.5 * (1.0 + t)
+            hid[base : base + size, cols] = (u * half_up).astype(BF)
+            slope[base : base + size, cols] = half_up + 0.5 * u * (1.0 - t * t) * (
+                GELU_A * (1.0 + 3.0 * GELU_B * sq)
+            )
+
+
+def feed_down(hid, s, z0, z1, z2, z3, own, other, whole):
+    for (base, size), ref in zip(PIECES, (s, z0, z1, z2, z3)):
+        whole[base : base + size, :] = ref[...]
+    rows = own.shape[0]
+    w = whole[...]
+    own[...] = tn(hid[:, 0:rows], w)
+    other[...] = tn(hid[:, rows : 2 * rows], w)
+
+
+def norm_back(dy, gain, hat, scale):
+    dhat = dy * gain
+    return scale * (
+        dhat
+        - jnp.mean(dhat, axis=-1, keepdims=True)
+        - hat * jnp.mean(dhat * hat, axis=-1, keepdims=True)
+    )
+
+
+def finish_forward(lengths, first, own, got, cot, norms, out, ds2, dz, terms):
+    rows = first.shape[0]
+    used = jnp.int32(0)
+    for s in range(5):
+        used = used + lengths[0, s]
+    live = jnp.where(lax.broadcasted_iota(jnp.int32, (rows, 1), 0) < used, 1.0, 0.0)
+    h = first[...] + (own[...] + got[...])
+    centered = h - jnp.mean(h, axis=-1, keepdims=True)
+    spread = jnp.mean(centered * centered, axis=-1, keepdims=True)
+    scale = lax.rsqrt(spread + 1e-05)
+    hat = centered * scale
+    out[...] = ((hat * norms[2:3, :] + norms[3:4, :]) * live).astype(BF)
+    dy = cot[...].astype(F32) * live
+    back = norm_back(dy, norms[2:3, :], hat, scale)
+    ds2[...] = back
+    dz[...] = back.astype(BF)
+    terms[0:1, :] = jnp.sum(dy * hat, axis=0, keepdims=True)
+    terms[1:2, :] = jnp.sum(dy, axis=0, keepdims=True)
+
+
+def spread_rows(get, send, turn, own):
+    goals = ((own, 0), (turn, 0), (send, 0), (send, PLANE))
+    for base, size in PIECES:
+        g = get(base, size)
+        if base == 0:
+            for p, (ref, off) in enumerate(goals):
+                ref[off : off + BLOCK, :] = g[BLOCK * p : BLOCK * p + BLOCK].astype(ref.dtype)
+        else:
+            ref, off = goals[(base - PLANE) // ZROWS]
+            ref[off + BLOCK : off + PLANE, :] = g.astype(ref.dtype)
+
+
+def grad_down(hid, za, zb, send, turn, own):
+    rows = za.shape[0]
+
+    def get(base, size):
+        return nn(hid[base : base + size, 0:rows], za[...]) + nn(
+            hid[base : base + size, rows : 2 * rows], zb[...]
+        )
+
+    spread_rows(get, send, turn, own)
+
+
+def grad_up(
+    slope, za, zb, ya, yb, s, z0, z1, z2, z3, s2, v0, v1, v2, v3,
+    send, turn, own, mine, other, dup, whole,
+):
+    rows = za.shape[0]
+    for (base, size), ref, ref2 in zip(PIECES, (s, z0, z1, z2, z3), (s2, v0, v1, v2, v3)):
+        here = slice(base, base + size)
+        whole[here, :] = ref2[...]
+        dup[here, 0:rows] = (nt(ref[...], za[...]) * slope[here, 0:rows]).astype(BF)
+        dup[here, rows:] = (nt(ref[...], zb[...]) * slope[here, rows:]).astype(BF)
+
+    def get(base, size):
+        return nn(dup[base : base + size, 0:rows], ya[...]) + nn(
+            dup[base : base + size, rows : 2 * rows], yb[...]
+        )
+
+    spread_rows(get, send, turn, own)
+    w = whole[...]
+    mine[...] = tn(dup[:, 0:rows], w)
+    other[...] = tn(dup[:, rows : 2 * rows], w)
+
+
+def attend_backward(
+    lengths, me, ds2, mine, got, xhat, rstd, norms, mix, att, den,
+    so, z0, z1, z2, z3, sp, y0, y1, y2, y3,
+    dh_ref, do_ref, terms, rel_own, rel_par, datt, dmix,
+):
+    rows, width = ds2.shape
+    chip, core = me[0], me[1]
+    dy1 = ds2[...] + (mine[...] + got[...])
+    hat = xhat[...]
+    terms[0:1, :] = jnp.sum(dy1 * hat, axis=0, keepdims=True)
+    terms[1:2, :] = jnp.sum(dy1, axis=0, keepdims=True)
+    dh = norm_back(dy1, norms[0:1, :], hat, rstd[...])
+    dh_ref[...] = dh
+    do = dh.astype(BF)
+    do_ref[...] = do
+    side = QKV // 3
+    sides = ((False, (so, z0, z1, z2, z3), rel_own), (True, (sp, y0, y1, y2, y3), rel_par))
+    for other, refs, _ in sides:
+        for (base, size), ref in zip(PIECES, refs):
+            got_t = nt(ref[...], do)
+            for at, plane, step in PLACES:
+                if base <= at < base + size:
+                    d = shard_index(chip, core, plane, step, other)
+                    datt[pl.ds(pl.multiple_of(side * d, 8), side), :] = got_t[
+                        at - base + QKV : at - base + BLOCK
+                    ]
+    mask, _ = pair_mask(lengths, rows)
+    for h in range(width // DH):
+        here = slice(DH * h, DH * h + DH)
+        q = mix[here, :]
+        k = mix[width + DH * h : width + DH * h + DH, :]
+        v = mix[2 * width + DH * h : 2 * width + DH * h + DH, :].astype(BF)
+        fq = softplus(q).astype(BF)
+        fk = softplus(k).astype(BF)
+        pairs = (tn(fk, fq) * mask).astype(BF)
+        da = datt[here, :]
+        total = den[h : h + 1, :]
+        dnum = da / total
+        dden = -jnp.sum(dnum * att[here, :], axis=0, keepdims=True)
+        dnum = dnum.astype(BF)
+        dpairs = ((tn(v, dnum) + dden) * mask).astype(BF)
+        dmix[2 * width + DH * h : 2 * width + DH * h + DH, :] = nt(dnum, pairs)
+        dmix[width + DH * h : width + DH * h + DH, :] = nt(fq, dpairs) * jax.nn.sigmoid(k)
+        dmix[here, :] = nn(fk, dpairs) * jax.nn.sigmoid(q)
+    blank = jnp.zeros((BLOCK - QKV, rows), F32)
+    for other, _, rel in sides:
+        for at, plane, step in PLACES:
+            d = shard_index(chip, core, plane, step, other)
+            part = dmix[pl.ds(pl.multiple_of(QKV * d, 8), QKV), :]
+            rel[at : at + BLOCK, :] = jnp.concatenate([part, blank], axis=0).astype(BF)
+
+
+def grad_mix(dma, dmb, xa, xb, ata, atb, doa, dob, send, turn, own):
+    def get(base, size):
+        here = slice(base, base + size)
+        return (nn(dma[here, :], xa[...]) + nn(dmb[here, :], xb[...])) + (
+            nn(ata[here, :], doa[...]) + nn(atb[here, :], dob[...])
+        )
+
+    spread_rows(get, send, turn, own)
+
+
+def grad_input(dh, rel_own, rel_par, so, z0, z1, z2, z3, sp, y0, y1, y2, y3, out):
+    total = dh[...]
+    for refs, rel in (((so, z0, z1, z2, z3), rel_own), ((sp, y0, y1, y2, y3), rel_par)):
+        for (base, size), ref in zip(PIECES, refs):
+            total = total + tn(rel[base : base + size, :], ref[...])
+    out[...] = total
+
+
+def close_sums(k1, a1, b1, c1, g2, g3, t1, t2, g1, note):
+    s1 = (k1[...] + a1[...].astype(F32)) + (b1[...].astype(F32) + c1[...].astype(F32))
+    g1[...] = s1
+    sq = s1 * s1 + g2[...] * g2[...] + g3[...] * g3[...]
+    note[0:2, :] = t1[...]
+    note[2:4, :] = t2[...]
+    note[4:5, :] = jnp.sum(sq, axis=0, keepdims=True)
+    note[5:8, :] = jnp.zeros((3, note.shape[1]), F32)
+
+
+def update(
+    note, g1, g2, g3, mw, ow, uw, dw, nw, mm, om, um, dm, nm, mv, ov, uv, dv, nv,
+    norm_out, mw2, ow2, uw2, dw2, nw2, mm2, om2, um2, dm2, nm2, mv2, ov2, uv2, dv2, nv2,
+):
+    terms = note[0:4, :]
+    total = jnp.sum(note[4:5, :]) + jnp.sum(terms * terms)
+    norm = jnp.sqrt(jnp.full((1, 1), total, F32))
+    norm_out[...] = norm
+    scale = 1.0 / jnp.maximum(norm, 1.0)
+
+    def flip(v):
+        n, width = v.shape
+        padded = jnp.concatenate([v, jnp.zeros((128 - n, width), F32)], axis=0)
+        return padded.T[:, 0:n]
+
+    one = g1[...]
+    grads = (flip(one[0:QKV]), one[QKV:BLOCK], flip(g2[...]), g3[...], terms)
+    groups = (
+        (mw, mm, mv, mw2, mm2, mv2),
+        (ow, om, ov, ow2, om2, ov2),
+        (uw, um, uv, uw2, um2, uv2),
+        (dw, dm, dv, dw2, dm2, dv2),
+        (nw, nm, nv, nw2, nm2, nv2),
+    )
+    for g, (w, m, v, w2, m2, v2), rate, decay in zip(grads, groups, RATES, DECAYS):
+        new_w, new_m, new_v = adamw(w[...], scale * g, m[...], v[...], rate, decay)
+        w2[...] = new_w
+        m2[...] = new_m
+        v2[...] = new_v
+
+
+def tie(value, *others):
+    return lax.optimization_barrier((value,) + others)[0]
+
+
+def swap(value):
+    return lax.ppermute(value, "fsdp", [(0, 1), (1, 0)])
+
+
+def hop_first(value):
+    return lax.ppermute(value, AXES, [(i, i ^ (4 if i % 2 else 2)) for i in range(2 * CHIPS)])
+
+
+def hop_second(value):
+    return lax.ppermute(value, AXES, [(i, i ^ (2 if i % 2 else 4)) for i in range(2 * CHIPS)])
+
+
+def hop_z(value, step):
+    return lax.ppermute(value, "dp", [(i, i ^ step) for i in range(CHIPS)])
+
+
+def spread_plane(value):
+    turned = hop_first(value)
+    across = hop_second(value)
+    return value, turned, across, hop_second(turned)
+
+
+def reduce_group(send, turn, own):
+    got = hop_second(send)
+    turned = (turn + got[PLANE:].astype(F32)).astype(BF)
+    back = hop_first(turned)
+    total = own + got[:PLANE].astype(F32) + back.astype(F32)
+    low = total.astype(BF)
+    parts = [
+        hop_z(low[BLOCK * (j + 1) : BLOCK * (j + 2)], step) for j, step in enumerate(STEPS_Z)
+    ]
+    return total[:BLOCK], parts
+
+
+def tuned_device(
+    tokens, cotangent, lengths,
+    mix_weight, out_weight, up_weight, down_weight, norm_params,
+    mix_first, out_first, up_first, down_first, norm_first,
+    mix_second, out_second, up_second, down_second, norm_second,
+):
+    rows, width = tokens.shape
+    chip, core = lax.axis_index("dp"), lax.axis_index("fsdp")
+    me = jnp.stack([chip, core]).astype(jnp.int32)
+    wide = 3 * width
+
+    s_all, *blocks = call(
+        pack_weights,
+        [((3 * BLOCK, width), BF)] + [((BLOCK, width), BF)] * 3,
+        (mix_weight, out_weight, up_weight, down_weight),
+        flops=1 << 20, moved=3 << 20,
+    )
+    s_parts = spread_plane(s_all)
+    z_parts = []
+    gate = ()
+    link = ()
+    for group in range(3):
+        block = tie(blocks[group], *gate) if gate else blocks[group]
+        arrived = [hop_z(block, step) for step in STEPS_Z]
+        gate = (arrived[2],)
+        joined = jnp.concatenate(arrived, axis=0)
+        if link:
+            joined = tie(joined, *link)
+        z_parts.append(spread_plane(joined))
+        link = (z_parts[-1][2],)
+    s_groups = [
+        jnp.concatenate([p[BLOCK * g : BLOCK * g + BLOCK] for p in s_parts], axis=0)
+        for g in range(3)
+    ]
+    weights = [(s_groups[g],) + tuple(z_parts[g]) for g in range(3)]
+    attn_own = weights[0]
+    attn_par = tuple(swap(p) for p in attn_own)
+    x_par = swap(tokens)
+
+    mix, att, den, at_own, at_par, first, first_low, xhat, rstd = call(
+        attend_forward,
+        [
+            ((wide, rows), F32), ((width, rows), F32), ((16, rows), F32),
+            ((HALF, rows), BF), ((HALF, rows), BF),
+            ((rows, width), F32), ((rows, width), BF), ((rows, width), F32), ((rows, 1), F32),
+        ],
+        (lengths, me, tokens) + attn_own + attn_par + (norm_params,),
+        smem=2, flops=12 << 30, moved=16 << 20,
+    )
+    at_got = swap(at_par)
+    first_par = swap(first_low)
+    hid, slope = call(
+        feed_up,
+        [((HALF, 2 * rows), BF), ((HALF, 2 * rows), F32)],
+        (first_low, first_par) + weights[1],
+        flops=4 << 30, moved=8 << 20,
+    )
+    down_own, down_par = call(
+        feed_down,
+        [((rows, width), F32)] * 2,
+        (hid,) + weights[2],
+        scratch=[pltpu.VMEM((HALF, width), BF)],
+        flops=2 << 30, moved=6 << 20,
+    )
+    output, ds2, dz, terms_two = call(
+        finish_forward,
+        [((rows, width), BF), ((rows, width), F32), ((rows, width), BF), ((2, width), F32)],
+        (lengths, first, down_own, swap(down_par), cotangent, norm_params),
+        smem=1, flops=1 << 28, moved=6 << 20,
+    )
+    dz_par = swap(dz)
+    spread_shapes = [((2 * PLANE, width), BF), ((PLANE, width), F32), ((PLANE, width), F32)]
+    send3, turn3, own3 = call(
+        grad_down, spread_shapes, (hid, dz, dz_par), flops=2 << 30, moved=6 << 20
+    )
+    keep3, parts3 = reduce_group(send3, turn3, own3)
+    send2, turn2, own2, dy_own, dy_par = call(
+        grad_up,
+        spread_shapes + [((rows, width), F32)] * 2,
+        (slope, dz, dz_par, first_low, first_par) + weights[2] + weights[1],
+        scratch=[pltpu.VMEM((HALF, 2 * rows), BF), pltpu.VMEM((HALF, width), BF)],
+        flops=5 << 30, moved=16 << 20,
+    )
+    keep2, parts2 = reduce_group(send2, turn2, own2)
+    dh, do, terms_one, dm_own, dm_par = call(
+        attend_backward,
+        [
+            ((rows, width), F32), ((rows, width), BF), ((2, width), F32),
+            ((HALF, rows), BF), ((HALF, rows), BF),
+        ],
+        (lengths, me, ds2, dy_own, swap(dy_par), xhat, rstd, norm_params, mix, att, den)
+        + attn_own + attn_par,
+        scratch=[pltpu.VMEM((width, rows), F32), pltpu.VMEM((wide, rows), F32)],
+        smem=2, flops=16 << 30, moved=20 << 20,
+    )
+    send1, turn1, own1 = call(
+        grad_mix,
+        spread_shapes,
+        (dm_own, swap(dm_par), tokens, x_par, at_own, at_got, do, swap(do)),
+        flops=3 << 30, moved=8 << 20,
+    )
+    keep1, parts1 = reduce_group(send1, turn1, own1)
+    (grad_tokens,) = call(
+        grad_input,
+        [((rows, width), F32)],
+        (dh, dm_own, dm_par) + attn_own + attn_par,
+        flops=3 << 30, moved=9 << 20,
+    )
+    g3 = (keep3 + parts3[0]) + (parts3[1].astype(F32) + parts3[2].astype(F32))
+    g2 = (keep2 + parts2[0]) + (parts2[1].astype(F32) + parts2[2].astype(F32))
+    g1, note = call(
+        close_sums,
+        [((BLOCK, width), F32), ((8, width), F32)],
+        (keep1,) + tuple(parts1) + (g2, g3, terms_one, terms_two),
+        flops=1 << 22, moved=1 << 21,
+    )
+    note = note + swap(note)
+    for step in (1, 2, 4, 8):
+        note = note + hop_z(note, step)
+    shapes = [
+        (mix_weight.shape, F32), (out_weight.shape, F32), (up_weight.shape, F32),
+        (down_weight.shape, F32), (norm_params.shape, F32),
+    ]
+    norm, *news = call(
+        update,
+        [((1, 1), F32)] + shapes * 3,
+        (
+            note, g1, g2, g3, mix_weight, out_weight, up_weight, down_weight, norm_params,
+            mix_first, out_first, up_first, down_first, norm_first,
+            mix_second, out_second, up_second, down_second, norm_second,
+        ),
+        flops=1 << 23, moved=8 << 20,
+    )
+    return (output, grad_tokens, norm.reshape(())) + tuple(news)
+
+
 def solution(mesh):
     in_specs = (
         P(("dp", "fsdp"), None),
@@ -274,6 +825,8 @@
         P(("dp", "fsdp"), None),
         P(),
     )
+    sizes = dict(mesh.shape)
+    tuned = sizes["dp"] == CHIPS and sizes["fsdp"] == 2
     return jax.shard_map(
-        on_device, mesh=mesh, in_specs=in_specs, out_specs=out_specs, check_vma=False
-    )
+        tuned_device if tuned else on_device, mesh=mesh, in_specs=in_specs, out_specs=out_specs, check_vma=False
+    )

time: 765 us -> 250 us (0.33); the launches traced: 754 us -> 250 us
  waiting for transfers between devices: 467 us -> 85.2 us
  matrix products: 95.3 us -> 0 us
  Pallas kernels: 0 us -> 72.5 us
  starting transfers between devices: 0.21 us -> 59.9 us
  local copies, waits for them, and re-layouts: 82.7 us -> 24.7 us
  other arithmetic: 48.6 us -> 6.25 us
  blocking collectives: 40.5 us -> 0 us
  between operations: 20 us -> 1.15 us
    reduce_scatter x1 -> x0, waiting for transfers between devices: 260 us -> none  [on_device(): lax.psum_scatter(packed_all, ('dp', 'fsdp'), scatter_dimension=0, tiled=T...]
    all_gather x4 -> x0, waiting for transfers between devices: 207 us -> none  [the longest x1 62.2 us: on_device(): lax.all_gather(rounded[2], ('dp', 'fsdp'), axis=1, tiled=True)]
    dot_general x21 -> x0, matrix products: 95.3 us -> none  [the longest x3 27.9 us: cos_attention(): state = jnp.einsum('psrhd,rhe->pshde', scaled, vals, precision=HIGH)]
    ppermute x0 -> x54, waiting for transfers between devices: none -> 85.2 us  [the longest x22 38 us: hop_z(): return lax.ppermute(value, 'dp', [(i, i ^ step) for i in range(CHIPS)])]
    pallas_call x0 -> x12, Pallas kernels: none -> 72.5 us  [call(): pl.pallas_call(body, out_shape=[jax.ShapeDtypeStruct(s, t) for s, t in ou...]
    ppermute x0 -> x54, starting transfers between devices: none -> 59.9 us  [the longest x22 38.5 us: hop_z(): return lax.ppermute(value, 'dp', [(i, i ^ step) for i in range(CHIPS)])]
    reshape x12 -> x0, local copies, waits for them, and re-layouts: 55.7 us -> none  [the longest x2 29.2 us: by_owner_columns(): return jnp.transpose(split, (1, 0, 2)).reshape(owners, -1, 128)]
    psum x1 -> x0, blocking collectives: 40.5 us -> none  [on_device(): owned_sq = lax.psum(local_sq, ('dp', 'fsdp'))]
  transfers between devices with their start and end apart: 5 -> 54, of which waited for: 5 -> 22; matrix products, arithmetic and copies ran while one was open for 6% -> 4% of each run, Pallas kernels for 0% -> 19%
where the time goes in v1:
time: 250 us
  waiting for transfers between devices  85.2 us (34%)
  Pallas kernels  72.5 us (29%)
  starting transfers between devices  59.9 us (24%)
  local copies, waits for them, and re-layouts  24.7 us (10%)
  other arithmetic  6.25 us (2%)
    pallas_call x12, Pallas kernels, call(): pl.pallas_call(body, out_shape=[jax.ShapeDtypeStruct(s, t) for s, t in ou...  72.5 us
    ppermute x22, starting transfers between devices, hop_z(): return lax.ppermute(value, 'dp', [(i, i ^ step) for i in range(CHIPS)])  38.5 us
    ppermute x22, waiting for transfers between devices, hop_z(): return lax.ppermute(value, 'dp', [(i, i ^ step) for i in range(CHIPS)])  38 us
    ppermute x11, waiting for transfers between devices, hop_second(): lax.ppermute(value, AXES, [(i, i ^ (2 if i % 2 else 4)) for i in range(2...  30.1 us
    unnamed x98, local copies, waits for them, and re-layouts  22.6 us
    ppermute x7, starting transfers between devices, hop_first(): lax.ppermute(value, AXES, [(i, i ^ (4 if i % 2 else 2)) for i in range(2...  9.87 us
    ppermute x11, starting transfers between devices, hop_second(): lax.ppermute(value, AXES, [(i, i ^ (2 if i % 2 else 4)) for i in range(2...  9.69 us
    ppermute x7, waiting for transfers between devices, hop_first(): lax.ppermute(value, AXES, [(i, i ^ (4 if i % 2 else 2)) for i in range(2...  8.79 us
  transfers between devices with their start and end apart: 54, of which 22 were waited for; matrix products, arithmetic and copies ran while one was open for 4% of the time, Pallas kernels for 19%

profile of v1, /device:TPU:0, one launch (start us, length us, event | category | flops | bytes accessed | tf_op | source)
XLA Modules:
  0.0 249.6 jit_solution(3945186690741939509)
XLA Ops:
  4.4 2.3 pack_weights.1
  6.8 2.9 %collective-permute-start = (bf16[288,768]{1,0:T(8,128)(2,1)}, bf16[288,768]{1,0:T(8,128)(2,1)S(1)}, u32[]{:S(2)}, u32[]{:S(2)}) collective-permute-start(bf16[288,768]{1,0:T(8,128)(2,1)} %get-tuple-element.77), channel_id=1, source_target_pairs={{0,2},{1,5},{2,0},{3,7},{4,6},{5,1},{6,4},{7,3},{8,10},{9,13},{10,... | collective-permute-start | bytes 1327112 | tf_op jit(solution)/shard_map/ppermute | solution.py:622
  12.8 2.6 %collective-permute-start.4 = (bf16[96,768]{1,0:T(8,128)(2,1)}, bf16[96,768]{1,0:T(8,128)(2,1)S(1)}, u32[]{:S(2)}, u32[]{:S(2)}) collective-permute-start(bf16[96,768]{1,0:T(8,128)(2,1)} %get-tuple-element.78), channel_id=1, source_target_pairs={{0,16},{2,18},{4,20},{6,22},{8,24},{10,26},{12,28},{14,30},{16,0},... | collective-permute-start | bytes 442376 | tf_op jit(solution)/shard_map/ppermute | solution.py:630
  16.7 8.1 %collective-permute-done.5 = bf16[96,768]{1,0:T(8,128)(2,1)S(1)} collective-permute-done((bf16[96,768]{1,0:T(8,128)(2,1)}, bf16[96,768]{1,0:T(8,128)(2,1)S(1)}, u32[]{:S(2)}, u32[]{:S(2)}) %collective-permute-start.5) | collective-permute-done | bytes 147488 | tf_op jit(solution)/shard_map/ppermute | solution.py:630
  26.3 7.5 %collective-permute-start.15 = (bf16[96,768]{1,0:T(8,128)(2,1)}, bf16[96,768]{1,0:T(8,128)(2,1)S(1)}, u32[]{:S(2)}, u32[]{:S(2)}) collective-permute-start(bf16[96,768]{1,0:T(8,128)(2,1)} %get-tuple-element.82), channel_id=1, source_target_pairs={{0,8},{2,10},{4,12},{6,14},{8,0},{10,2},{12,4},{14,6},{16,24},{18,... | collective-permute-start | bytes 442376 | tf_op jit(solution)/shard_map/ppermute | solution.py:630
  34.6 3.3 %collective-permute-done.15 = bf16[96,768]{1,0:T(8,128)(2,1)S(1)} collective-permute-done((bf16[96,768]{1,0:T(8,128)(2,1)}, bf16[96,768]{1,0:T(8,128)(2,1)S(1)}, u32[]{:S(2)}, u32[]{:S(2)}) %collective-permute-start.15) | collective-permute-done | bytes 147488 | tf_op jit(solution)/shard_map/ppermute | solution.py:630
  38.4 2.8 %collective-permute-done.16 = bf16[96,768]{1,0:T(8,128)(2,1)S(1)} collective-permute-done((bf16[96,768]{1,0:T(8,128)(2,1)S(1)}, bf16[96,768]{1,0:T(8,128)(2,1)S(1)}, u32[]{:S(2)}, u32[]{:S(2)}) %collective-permute-start.16) | collective-permute-done | bytes 147488 | tf_op jit(solution)/shard_map/ppermute | solution.py:630
  42.0 4.3 %collective-permute-done.7.z2 = bf16[288,768]{1,0:T(8,128)(2,1)} collective-permute-done((bf16[288,768]{1,0:T(8,128)(2,1)S(1)}, bf16[288,768]{1,0:T(8,128)(2,1)}, u32[]{:S(2)}, u32[]{:S(2)}) %collective-permute-start.7) | collective-permute-done | bytes 442400 | tf_op jit(solution)/shard_map/ppermute | solution.py:626
  53.9 4.7 %collective-permute-done.23 = bf16[96,768]{1,0:T(8,128)(2,1)S(1)} collective-permute-done((bf16[96,768]{1,0:T(8,128)(2,1)S(1)}, bf16[96,768]{1,0:T(8,128)(2,1)S(1)}, u32[]{:S(2)}, u32[]{:S(2)}) %collective-permute-start.23) | collective-permute-done | bytes 147488 | tf_op jit(solution)/shard_map/ppermute | solution.py:630
  64.8 2.3 collective-permute-done.18.z1.v1
  69.4 12.5 %attend_forward.1 = (f32[2304,256]{1,0:T(8,128)}, f32[768,256]{1,0:T(8,128)}, f32[16,256]{1,0:T(8,128)}, bf16[1536,256]{1,0:T(8,128)(2,1)}, bf16[1536,256]{1,0:T...) custom-call(s32[1,6]{1,0:T(1,128)} %lengths.5, ...), custom_call_target="tpu_custom_call" | custom-call | flops 12884901888 | bytes 16777216 | tf_op jit(solution)/shard_map/attend_forward/pallas_call | solution.py:290
  87.3 6.6 %feed_up.1 = (bf16[1536,512]{1,0:T(8,128)(2,1)}, f32[1536,512]{1,0:T(8,128)}) custom-call(bf16[256,768]{1,0:T(8,128)(2,1)} %get-tuple-element.80.ya, bf16[256,768]{1,0:T(8,128)(2,1)} %copy-done.36, bf16[384,768]{1,0:T(8,128)(2,1)} %pad_maximum_fusion.1.s.s2, bf16[288,768]{1,0:T(8,128)(2,1)} %copy-done.8, bf16[288,768]{1,0:T(8,128)(2,1)} %collective-permute-done.18.z1.v1, ...), custom_call_target="tpu_custom_call" | custom-call | flops 4294967296 | bytes 8388608 | tf_op jit(solution)/shard_map/feed_up/pallas_call | solution.py:290
  96.6 4.6 %feed_down.1 = (f32[256,768]{1,0:T(8,128)}, f32[256,768]{1,0:T(8,128)}) custom-call(bf16[1536,512]{1,0:T(8,128)(2,1)} %get-tuple-element.84.hid, bf16[384,768]{1,0:T(8,128)(2,1)} %pad_maximum_fusion.2.s, bf16[288,768]{1,0:T(8,128)(2,1)} %copy-done.9, bf16[288,768]{1,0:T(8,128)(2,1)} %copy-done.31, bf16[288,768]{1,0:T(8,128)(2,1)} %copy-done.33, ...), custom_call_target="tpu_custom_call" | custom-call | flops 2147483648 | bytes 6291456 | tf_op jit(solution)/shard_map/feed_down/pallas_call | solution.py:290
  101.2 2.5 collective-permute-done.27.got
  104.6 3.5 %finish_forward.1 = (bf16[256,768]{1,0:T(8,128)(2,1)}, f32[256,768]{1,0:T(8,128)}, bf16[256,768]{1,0:T(8,128)(2,1)}, f32[2,768]{1,0:T(2,128)}) custom-call(s32[1,6]{1,0:T(1,128)} %lengths.5, f32[256,768]{1,0:T(8,128)} %get-tuple-element.79.first, f32[256,768]{1,0:T(8,128)} %get-tuple-element.88.own, f32[256,768]{1,0:T(8,128)} %copy-done.6, ...), custom_call_target="tpu_custom_call" | custom-call | flops 268435456 | bytes 6291456 | tf_op jit(solution)/shard_map/finish_forward/pallas_call | solution.py:290
  110.7 8.5 %grad_up.1 = (bf16[768,768]{1,0:T(8,128)(2,1)}, f32[384,768]{1,0:T(8,128)}, f32[384,768]{1,0:T(8,128)}, f32[256,768]{1,0:T(8,128)}, f32[256,768]{1,0:T(8,128)}) custom-call(f32[1536,512]{1,0:T(8,128)} %get-tuple-element.92.slope, bf16[256,768]{1,0:T(8,128)(2,1)} %get-tuple-element.93.za, bf16[256,768]{1,0:T(8,128)(2,1)} %copy-done.37, ...), custom_call_target="tpu_custom_call" | custom-call | flops 5368709120 | bytes 16777216 | tf_op jit(solution)/shard_map/grad_up/pallas_call | solution.py:290
  119.7 4.3 %grad_down.1 = (bf16[768,768]{1,0:T(8,128)(2,1)}, f32[384,768]{1,0:T(8,128)}, f32[384,768]{1,0:T(8,128)}) custom-call(bf16[1536,512]{1,0:T(8,128)(2,1)} %get-tuple-element.84.hid, bf16[256,768]{1,0:T(8,128)(2,1)} %get-tuple-element.93.za, bf16[256,768]{1,0:T(8,128)(2,1)} %copy-done.37), custom_call_target="tpu_custom_call" | custom-call | flops 2147483648 | bytes 6291456 | tf_op jit(solution)/shard_map/grad_down/pallas_call | solution.py:290
  125.4 11.1 %attend_backward.1 = (f32[256,768]{1,0:T(8,128)}, bf16[256,768]{1,0:T(8,128)(2,1)}, f32[2,768]{1,0:T(2,128)}, bf16[1536,256]{1,0:T(8,128)(2,1)}, bf16[1536,256]{1,0:T(8,128)(2,1)}) custom-call(s32[1,6]{1,0:T(1,128)} %lengths.5, s32[2]{0:T(128)} %pad_add_fusion.me, f32[256,768]{1,0:T(8,128)} %get-tuple-element.91.ds2, f32[256,768]{1,0:T(8,128)} %get-tuple-element.94.mine, ...), custom_call_target="tpu_custom_call" | custom-call | flops 17179869184 | bytes 20971520 | tf_op jit(solution)/shard_map/attend_backward/pallas_call | solution.py:290
  137.1 2.5 %collective-permute-done.31.xb = bf16[256,768]{1,0:T(8,128)(2,1)S(1)} collective-permute-done((bf16[256,768]{1,0:T(8,128)(2,1)S(1)}, bf16[256,768]{1,0:T(8,128)(2,1)S(1)}, u32[]{:S(2)}, u32[]{:S(2)}) %collective-permute-start.31) | collective-permute-done | bytes 393248 | tf_op jit(solution)/shard_map/ppermute | solution.py:618
  142.5 6.3 %grad_mix.1 = (bf16[768,768]{1,0:T(8,128)(2,1)}, f32[384,768]{1,0:T(8,128)}, f32[384,768]{1,0:T(8,128)}) custom-call(bf16[1536,256]{1,0:T(8,128)(2,1)} %get-tuple-element.102.rel_own.dma, bf16[1536,256]{1,0:T(8,128)(2,1)} %copy-done.26, bf16[256,768]{1,0:T(8,128)(2,1)} %xa.1, bf16[256,768]{1,0:T(8,128)(2,1)} %copy-done.38, ...), custom_call_target="tpu_custom_call" | custom-call | flops 3221225472 | bytes 8388608 | tf_op jit(solution)/shard_map/grad_mix/pallas_call | solution.py:290
  150.6 9.4 %collective-permute-done.39 = bf16[768,768]{1,0:T(8,128)(2,1)S(1)} collective-permute-done((bf16[768,768]{1,0:T(8,128)(2,1)S(1)}, bf16[768,768]{1,0:T(8,128)(2,1)S(1)}, u32[]{:S(2)}, u32[]{:S(2)}) %collective-permute-start.39) | collective-permute-done | bytes 1179680 | tf_op jit(solution)/shard_map/ppermute | solution.py:626
  161.4 4.3 %collective-permute-done.45 = bf16[384,768]{1,0:T(8,128)(2,1)S(1)} collective-permute-done((bf16[384,768]{1,0:T(8,128)(2,1)S(1)}, bf16[384,768]{1,0:T(8,128)(2,1)S(1)}, u32[]{:S(2)}, u32[]{:S(2)}) %collective-permute-start.45) | collective-permute-done | bytes 589856 | tf_op jit(solution)/shard_map/ppermute | solution.py:622
  165.9 2.7 %collective-permute-start.46 = (bf16[96,768]{1,0:T(8,128)(2,1)S(1)}, bf16[96,768]{1,0:T(8,128)(2,1)S(1)}, u32[]{:S(2)}, u32[]{:S(2)}) collective-permute-start(bf16[96,768]{1,0:T(8,128)(2,1)S(1)} %get-tuple-element.160), channel_id=1, source_target_pairs={{0,8},{2,10},{4,12},{6,14},{8,0},{10,2},{12,4},{14,6},{16,24},{18,... | collective-permute-start | bytes 442376 | tf_op jit(solution)/shard_map/ppermute | solution.py:630
  171.0 10.1 %collective-permute-done.34 = bf16[768,768]{1,0:T(8,128)(2,1)S(1)} collective-permute-done((bf16[768,768]{1,0:T(8,128)(2,1)}, bf16[768,768]{1,0:T(8,128)(2,1)S(1)}, u32[]{:S(2)}, u32[]{:S(2)}) %collective-permute-start.34) | collective-permute-done | bytes 1179680 | tf_op jit(solution)/shard_map/ppermute | solution.py:626
  182.8 3.0 %collective-permute-start.41 = (bf16[96,768]{1,0:T(8,128)(2,1)S(1)}, bf16[96,768]{1,0:T(8,128)(2,1)S(1)}, u32[]{:S(2)}, u32[]{:S(2)}) collective-permute-start(bf16[96,768]{1,0:T(8,128)(2,1)S(1)} %get-tuple-element.163), channel_id=1, source_target_pairs={{0,8},{2,10},{4,12},{6,14},{8,0},{10,2},{12,4},{14,6},{16,24},{18,... | collective-permute-start | bytes 442376 | tf_op jit(solution)/shard_map/ppermute | solution.py:630
  191.5 2.7 %collective-permute-start.36 = (bf16[96,768]{1,0:T(8,128)(2,1)S(1)}, bf16[96,768]{1,0:T(8,128)(2,1)S(1)}, u32[]{:S(2)}, u32[]{:S(2)}) collective-permute-start(bf16[96,768]{1,0:T(8,128)(2,1)S(1)} %get-tuple-element.168), channel_id=1, source_target_pairs={{0,8},{2,10},{4,12},{6,14},{8,0},{10,2},{12,4},{14,6},{16,24},{18,... | collective-permute-start | bytes 442376 | tf_op jit(solution)/shard_map/ppermute | solution.py:630
  196.6 2.7 %collective-permute-done.42 = bf16[96,768]{1,0:T(8,128)(2,1)S(1)} collective-permute-done((bf16[96,768]{1,0:T(8,128)(2,1)S(1)}, bf16[96,768]{1,0:T(8,128)(2,1)S(1)}, u32[]{:S(2)}, u32[]{:S(2)}) %collective-permute-start.42) | collective-permute-done | bytes 147488 | tf_op jit(solution)/shard_map/ppermute | solution.py:630
  200.8 10.8 %collective-permute-done.37.b1 = bf16[96,768]{1,0:T(8,128)(2,1)S(1)} collective-permute-done((bf16[96,768]{1,0:T(8,128)(2,1)S(1)}, bf16[96,768]{1,0:T(8,128)(2,1)S(1)}, u32[]{:S(2)}, u32[]{:S(2)}) %collective-permute-start.37) | collective-permute-done | bytes 147488 | tf_op jit(solution)/shard_map/ppermute | solution.py:630
  218.2 2.3 collective-permute-done.50
  221.6 2.8 %collective-permute-done.51 = f32[8,768]{1,0:T(8,128)S(1)} collective-permute-done((f32[8,768]{1,0:T(8,128)S(1)}, f32[8,768]{1,0:T(8,128)S(1)}, u32[]{:S(2)}, u32[]{:S(2)}) %collective-permute-start.51) | collective-permute-done | bytes 24608 | tf_op jit(solution)/shard_map/ppermute | solution.py:630
  231.0 6.1 %grad_input.1 = f32[256,768]{1,0:T(8,128)} custom-call(f32[256,768]{1,0:T(8,128)} %get-tuple-element.101.dh, bf16[1536,256]{1,0:T(8,128)(2,1)} %get-tuple-element.102.rel_own.dma, bf16[1536,256]{1,0:T(8,128)(2,1)} %get-tuple-element.103.rel_par, bf16[384,768]{1,0:T(8,128)(2,1)} %copy-done.7, bf16[288,768]{1,0:T(8,128)(2,1)} %copy-done.21, ...), custom_call_target="tpu_custom_call" | custom-call | flops 3221225472 | bytes 9437184 | tf_op jit(solution)/shard_map/grad_input/pallas_call | solution.py:290
  237.7 4.6 %update.1 = (f32[1,1]{1,0:T(1,128)}, f32[768,72]{1,0:T(8,128)}, f32[24,768]{1,0:T(8,128)}, f32[768,96]{1,0:T(8,128)}, f32[96,768]{1,0:T(8,128)}, /*index=5*/f32[...) custom-call(f32[8,768]{1,0:T(8,128)} %add.79.note, ...), custom_call_target="tpu_custom_call" | custom-call | flops 8388608 | bytes 8388608 | tf_op jit(solution)/shard_map/update/pallas_call | solution.py:290
  (214 shorter events, 84.0 us)
Async XLA Ops:
  6.8 34.5 %collective-permute-start = (bf16[288,768]{1,0:T(8,128)(2,1)}, bf16[288,768]{1,0:T(8,128)(2,1)S(1)}, u32[]{:S(2)}, u32[]{:S(2)}) collective-permute-start(bf16[288,768]{1,0:T(8,128)(2,1)} %get-tuple-element.77), channel_id=1, source_target_pairs={{0,2},{1,5},{2,0},{3,7},{4,6},{5,1},{6,4},{7,3},{8,10},{9,13},{10,... | collective-permute-start | bytes 1327112 | tf_op jit(solution)/shard_map/ppermute | solution.py:622
  9.7 32.1 %collective-permute-start.1 = (bf16[288,768]{1,0:T(8,128)(2,1)}, bf16[288,768]{1,0:T(8,128)(2,1)S(1)}, u32[]{:S(2)}, u32[]{:S(2)}) collective-permute-start(bf16[288,768]{1,0:T(8,128)(2,1)} %get-tuple-element.77), channel_id=1, source_target_pairs={{0,4},{1,3},{2,6},{3,1},{4,0},{5,7},{6,2},{7,5},{8,12},{9,11},{10,... | collective-permute-start | bytes 1327112 | tf_op jit(solution)/shard_map/ppermute | solution.py:626
  11.2 15.1 %collective-permute-start.3 = (bf16[96,768]{1,0:T(8,128)(2,1)}, bf16[96,768]{1,0:T(8,128)(2,1)S(1)}, u32[]{:S(2)}, u32[]{:S(2)}) collective-permute-start(bf16[96,768]{1,0:T(8,128)(2,1)} %get-tuple-element.78), channel_id=1, source_target_pairs={{0,8},{2,10},{4,12},{6,14},{8,0},{10,2},{12,4},{14,6},{16,24},{18,... | collective-permute-start | bytes 442376 | tf_op jit(solution)/shard_map/ppermute | solution.py:630
  12.8 21.0 %collective-permute-start.4 = (bf16[96,768]{1,0:T(8,128)(2,1)}, bf16[96,768]{1,0:T(8,128)(2,1)S(1)}, u32[]{:S(2)}, u32[]{:S(2)}) collective-permute-start(bf16[96,768]{1,0:T(8,128)(2,1)} %get-tuple-element.78), channel_id=1, source_target_pairs={{0,16},{2,18},{4,20},{6,22},{8,24},{10,26},{12,28},{14,30},{16,0},... | collective-permute-start | bytes 442376 | tf_op jit(solution)/shard_map/ppermute | solution.py:630
  15.4 9.4 %collective-permute-start.5 = (bf16[96,768]{1,0:T(8,128)(2,1)}, bf16[96,768]{1,0:T(8,128)(2,1)S(1)}, u32[]{:S(2)}, u32[]{:S(2)}) collective-permute-start(bf16[96,768]{1,0:T(8,128)(2,1)} %get-tuple-element.78), channel_id=1, source_target_pairs={{0,24},{2,26},{4,28},{6,30},{8,16},{10,18},{12,20},{14,22},{16,8},... | collective-permute-start | bytes 442376 | tf_op jit(solution)/shard_map/ppermute | solution.py:630
  26.3 11.6 %collective-permute-start.15 = (bf16[96,768]{1,0:T(8,128)(2,1)}, bf16[96,768]{1,0:T(8,128)(2,1)S(1)}, u32[]{:S(2)}, u32[]{:S(2)}) collective-permute-start(bf16[96,768]{1,0:T(8,128)(2,1)} %get-tuple-element.82), channel_id=1, source_target_pairs={{0,8},{2,10},{4,12},{6,14},{8,0},{10,2},{12,4},{14,6},{16,24},{18,... | collective-permute-start | bytes 442376 | tf_op jit(solution)/shard_map/ppermute | solution.py:630
  34.0 14.3 %collective-permute-start.6 = (bf16[288,768]{1,0:T(8,128)(2,1)S(1)}, bf16[288,768]{1,0:T(8,128)(2,1)S(1)}, u32[]{:S(2)}, u32[]{:S(2)}) collective-permute-start(bf16[288,768]{1,0:T(8,128)(2,1)S(1)} %constant_dynamic-update-slice_fusion.z0), channel_id=1, source_target_pairs={{0,2},{1,5},{2,0},{3,7},{4,6},{5,1},{6,4},{7,3},{8,10},{9,13},{10,... | collective-permute-start | bytes 1327112 | tf_op jit(solution)/shard_map/ppermute | solution.py:622
  41.2 17.4 %collective-permute-start.10 = (bf16[288,768]{1,0:T(8,128)(2,1)S(1)}, bf16[288,768]{1,0:T(8,128)(2,1)S(1)}, u32[]{:S(2)}, u32[]{:S(2)}) collective-permute-start(bf16[288,768]{1,0:T(8,128)(2,1)S(1)} %constant_dynamic-update-slice_fusion.z0), channel_id=1, source_target_pairs={{0,1},{1,0},{2,3},{3,2},{4,5},{5,4},{6,7},{7,6},{8,9},{9,8},{10,11... | collective-permute-start | bytes 1327112 | tf_op jit(solution)/shard_map/ppermute | solution.py:618
  41.2 9.7 %collective-permute-start.2 = (bf16[288,768]{1,0:T(8,128)(2,1)S(1)}, bf16[288,768]{1,0:T(8,128)(2,1)S(1)}, u32[]{:S(2)}, u32[]{:S(2)}) collective-permute-start(bf16[288,768]{1,0:T(8,128)(2,1)S(1)} %collective-permute-done), channel_id=1, source_target_pairs={{0,4},{1,3},{2,6},{3,1},{4,0},{5,7},{6,2},{7,5},{8,12},{9,11},{10,... | collective-permute-start | bytes 1327112 | tf_op jit(solution)/shard_map/ppermute | solution.py:626
  41.9 9.6 %collective-permute-start.21 = (bf16[96,768]{1,0:T(8,128)(2,1)S(1)}, bf16[96,768]{1,0:T(8,128)(2,1)S(1)}, u32[]{:S(2)}, u32[]{:S(2)}) collective-permute-start(bf16[96,768]{1,0:T(8,128)(2,1)S(1)} %copy-done.40), channel_id=1, source_target_pairs={{0,8},{2,10},{4,12},{6,14},{8,0},{10,2},{12,4},{14,6},{16,24},{18,... | collective-permute-start | bytes 442376 | tf_op jit(solution)/shard_map/ppermute | solution.py:630
  48.2 13.2 %collective-permute-start.19 = (bf16[288,768]{1,0:T(8,128)(2,1)S(1)}, bf16[288,768]{1,0:T(8,128)(2,1)S(1)}, u32[]{:S(2)}, u32[]{:S(2)}) collective-permute-start(bf16[288,768]{1,0:T(8,128)(2,1)S(1)} %pad_maximum_fusion.3.z0.v0), channel_id=1, source_target_pairs={{0,4},{1,3},{2,6},{3,1},{4,0},{5,7},{6,2},{7,5},{8,12},{9,11},{10,... | collective-permute-start | bytes 1327112 | tf_op jit(solution)/shard_map/ppermute | solution.py:626
  50.9 10.5 %collective-permute-start.8 = (bf16[288,768]{1,0:T(8,128)(2,1)S(1)}, bf16[288,768]{1,0:T(8,128)(2,1)}, u32[]{:S(2)}, u32[]{:S(2)}) collective-permute-start(bf16[288,768]{1,0:T(8,128)(2,1)S(1)} %collective-permute-done.6.z1), channel_id=1, source_target_pairs={{0,4},{1,3},{2,6},{3,1},{4,0},{5,7},{6,2},{7,5},{8,12},{9,11},{10,... | collective-permute-start | bytes 1327112 | tf_op jit(solution)/shard_map/ppermute | solution.py:626
  53.9 14.7 %collective-permute-start.9 = (bf16[384,768]{1,0:T(8,128)(2,1)S(1)}, bf16[384,768]{1,0:T(8,128)(2,1)}, u32[]{:S(2)}, u32[]{:S(2)}) collective-permute-start(bf16[384,768]{1,0:T(8,128)(2,1)S(1)} %pad_maximum_fusion.so), channel_id=1, source_target_pairs={{0,1},{1,0},{2,3},{3,2},{4,5},{5,4},{6,7},{7,6},{8,9},{9,8},{10,11... | collective-permute-start | bytes 1769480 | tf_op jit(solution)/shard_map/ppermute | solution.py:618
  62.8 20.5 %collective-permute-start.24 = (bf16[288,768]{1,0:T(8,128)(2,1)S(1)}, bf16[288,768]{1,0:T(8,128)(2,1)S(1)}, u32[]{:S(2)}, u32[]{:S(2)}) collective-permute-start(bf16[288,768]{1,0:T(8,128)(2,1)S(1)} %pad_maximum_fusion.4.z0), channel_id=1, source_target_pairs={{0,2},{1,5},{2,0},{3,7},{4,6},{5,1},{6,4},{7,3},{8,10},{9,13},{10,... | collective-permute-start | bytes 1327112 | tf_op jit(solution)/shard_map/ppermute | solution.py:622
  67.1 18.6 %collective-permute-start.20 = (bf16[288,768]{1,0:T(8,128)(2,1)}, bf16[288,768]{1,0:T(8,128)(2,1)S(1)}, u32[]{:S(2)}, u32[]{:S(2)}) collective-permute-start(bf16[288,768]{1,0:T(8,128)(2,1)} %collective-permute-done.18.z1.v1), channel_id=1, source_target_pairs={{0,4},{1,3},{2,6},{3,1},{4,0},{5,7},{6,2},{7,5},{8,12},{9,11},{10,... | collective-permute-start | bytes 1327112 | tf_op jit(solution)/shard_map/ppermute | solution.py:626
  82.8 11.1 %collective-permute-start.25 = (bf16[288,768]{1,0:T(8,128)(2,1)S(1)}, bf16[288,768]{1,0:T(8,128)(2,1)S(1)}, u32[]{:S(2)}, u32[]{:S(2)}) collective-permute-start(bf16[288,768]{1,0:T(8,128)(2,1)S(1)} %pad_maximum_fusion.4.z0), channel_id=1, source_target_pairs={{0,4},{1,3},{2,6},{3,1},{4,0},{5,7},{6,2},{7,5},{8,12},{9,11},{10,... | collective-permute-start | bytes 1327112 | tf_op jit(solution)/shard_map/ppermute | solution.py:626
  83.3 12.5 %collective-permute-start.26 = (bf16[288,768]{1,0:T(8,128)(2,1)S(1)}, bf16[288,768]{1,0:T(8,128)(2,1)S(1)}, u32[]{:S(2)}, u32[]{:S(2)}) collective-permute-start(bf16[288,768]{1,0:T(8,128)(2,1)S(1)} %collective-permute-done.24.z1), channel_id=1, source_target_pairs={{0,4},{1,3},{2,6},{3,1},{4,0},{5,7},{6,2},{7,5},{8,12},{9,11},{10,... | collective-permute-start | bytes 1327112 | tf_op jit(solution)/shard_map/ppermute | solution.py:626
  119.4 21.8 %collective-permute-start.32 = (bf16[1536,256]{1,0:T(8,128)(2,1)S(1)}, bf16[1536,256]{1,0:T(8,128)(2,1)S(1)}, u32[]{:S(2)}, u32[]{:S(2)}) collective-permute-start(bf16[1536,256]{1,0:T(8,128)(2,1)S(1)} %copy-done.23), channel_id=1, source_target_pairs={{0,1},{1,0},{2,3},{3,2},{4,5},{5,4},{6,7},{7,6},{8,9},{9,8},{10,11... | collective-permute-start | bytes 2359304 | tf_op jit(solution)/shard_map/ppermute | solution.py:618
  124.0 25.2 %collective-permute-start.44 = (bf16[768,768]{1,0:T(8,128)(2,1)}, bf16[768,768]{1,0:T(8,128)(2,1)S(1)}, u32[]{:S(2)}, u32[]{:S(2)}) collective-permute-start(bf16[768,768]{1,0:T(8,128)(2,1)} %get-tuple-element.114), channel_id=1, source_target_pairs={{0,4},{1,3},{2,6},{3,1},{4,0},{5,7},{6,2},{7,5},{8,12},{9,11},{10,... | collective-permute-start | bytes 3538952 | tf_op jit(solution)/shard_map/ppermute | solution.py:626
  139.7 20.3 %collective-permute-start.39 = (bf16[768,768]{1,0:T(8,128)(2,1)S(1)}, bf16[768,768]{1,0:T(8,128)(2,1)S(1)}, u32[]{:S(2)}, u32[]{:S(2)}) collective-permute-start(bf16[768,768]{1,0:T(8,128)(2,1)S(1)} %copy-done.22), channel_id=1, source_target_pairs={{0,4},{1,3},{2,6},{3,1},{4,0},{5,7},{6,2},{7,5},{8,12},{9,11},{10,... | collective-permute-start | bytes 3538952 | tf_op jit(solution)/shard_map/ppermute | solution.py:626
  148.7 32.4 %collective-permute-start.34 = (bf16[768,768]{1,0:T(8,128)(2,1)}, bf16[768,768]{1,0:T(8,128)(2,1)S(1)}, u32[]{:S(2)}, u32[]{:S(2)}) collective-permute-start(bf16[768,768]{1,0:T(8,128)(2,1)} %get-tuple-element.108), channel_id=1, source_target_pairs={{0,4},{1,3},{2,6},{3,1},{4,0},{5,7},{6,2},{7,5},{8,12},{9,11},{10,... | collective-permute-start | bytes 3538952 | tf_op jit(solution)/shard_map/ppermute | solution.py:626
  149.3 16.3 %collective-permute-start.45 = (bf16[384,768]{1,0:T(8,128)(2,1)S(1)}, bf16[384,768]{1,0:T(8,128)(2,1)S(1)}, u32[]{:S(2)}, u32[]{:S(2)}) collective-permute-start(bf16[384,768]{1,0:T(8,128)(2,1)S(1)} %add_convert_fusion), channel_id=1, source_target_pairs={{0,2},{1,5},{2,0},{3,7},{4,6},{5,1},{6,4},{7,3},{8,10},{9,13},{10,... | collective-permute-start | bytes 1769480 | tf_op jit(solution)/shard_map/ppermute | solution.py:622
  160.1 22.5 %collective-permute-start.40 = (bf16[384,768]{1,0:T(8,128)(2,1)S(1)}, bf16[384,768]{1,0:T(8,128)(2,1)S(1)}, u32[]{:S(2)}, u32[]{:S(2)}) collective-permute-start(bf16[384,768]{1,0:T(8,128)(2,1)S(1)} %add_convert_fusion.1), channel_id=1, source_target_pairs={{0,2},{1,5},{2,0},{3,7},{4,6},{5,1},{6,4},{7,3},{8,10},{9,13},{10,... | collective-permute-start | bytes 1769480 | tf_op jit(solution)/shard_map/ppermute | solution.py:622
  165.9 19.9 %collective-permute-start.46 = (bf16[96,768]{1,0:T(8,128)(2,1)S(1)}, bf16[96,768]{1,0:T(8,128)(2,1)S(1)}, u32[]{:S(2)}, u32[]{:S(2)}) collective-permute-start(bf16[96,768]{1,0:T(8,128)(2,1)S(1)} %get-tuple-element.160), channel_id=1, source_target_pairs={{0,8},{2,10},{4,12},{6,14},{8,0},{10,2},{12,4},{14,6},{16,24},{18,... | collective-permute-start | bytes 442376 | tf_op jit(solution)/shard_map/ppermute | solution.py:630
  168.6 17.9 %collective-permute-start.47 = (bf16[96,768]{1,0:T(8,128)(2,1)S(1)}, bf16[96,768]{1,0:T(8,128)(2,1)S(1)}, u32[]{:S(2)}, u32[]{:S(2)}) collective-permute-start(bf16[96,768]{1,0:T(8,128)(2,1)S(1)} %get-tuple-element.162), channel_id=1, source_target_pairs={{0,16},{2,18},{4,20},{6,22},{8,24},{10,26},{12,28},{14,30},{16,0},... | collective-permute-start | bytes 442376 | tf_op jit(solution)/shard_map/ppermute | solution.py:630
  169.3 18.9 %collective-permute-start.48 = (bf16[96,768]{1,0:T(8,128)(2,1)S(1)}, bf16[96,768]{1,0:T(8,128)(2,1)S(1)}, u32[]{:S(2)}, u32[]{:S(2)}) collective-permute-start(bf16[96,768]{1,0:T(8,128)(2,1)S(1)} %get-tuple-element.161), channel_id=1, source_target_pairs={{0,24},{2,26},{4,28},{6,30},{8,16},{10,18},{12,20},{14,22},{16,8},... | collective-permute-start | bytes 442376 | tf_op jit(solution)/shard_map/ppermute | solution.py:630
  181.3 9.9 %collective-permute-start.35 = (bf16[384,768]{1,0:T(8,128)(2,1)S(1)}, bf16[384,768]{1,0:T(8,128)(2,1)S(1)}, u32[]{:S(2)}, u32[]{:S(2)}) collective-permute-start(bf16[384,768]{1,0:T(8,128)(2,1)S(1)} %add_convert_fusion.2), channel_id=1, source_target_pairs={{0,2},{1,5},{2,0},{3,7},{4,6},{5,1},{6,4},{7,3},{8,10},{9,13},{10,... | collective-permute-start | bytes 1769480 | tf_op jit(solution)/shard_map/ppermute | solution.py:622
  182.8 12.1 %collective-permute-start.41 = (bf16[96,768]{1,0:T(8,128)(2,1)S(1)}, bf16[96,768]{1,0:T(8,128)(2,1)S(1)}, u32[]{:S(2)}, u32[]{:S(2)}) collective-permute-start(bf16[96,768]{1,0:T(8,128)(2,1)S(1)} %get-tuple-element.163), channel_id=1, source_target_pairs={{0,8},{2,10},{4,12},{6,14},{8,0},{10,2},{12,4},{14,6},{16,24},{18,... | collective-permute-start | bytes 442376 | tf_op jit(solution)/shard_map/ppermute | solution.py:630
  185.8 13.5 %collective-permute-start.42 = (bf16[96,768]{1,0:T(8,128)(2,1)S(1)}, bf16[96,768]{1,0:T(8,128)(2,1)S(1)}, u32[]{:S(2)}, u32[]{:S(2)}) collective-permute-start(bf16[96,768]{1,0:T(8,128)(2,1)S(1)} %get-tuple-element.165), channel_id=1, source_target_pairs={{0,16},{2,18},{4,20},{6,22},{8,24},{10,26},{12,28},{14,30},{16,0},... | collective-permute-start | bytes 442376 | tf_op jit(solution)/shard_map/ppermute | solution.py:630
  186.5 12.8 %collective-permute-start.43 = (bf16[96,768]{1,0:T(8,128)(2,1)S(1)}, bf16[96,768]{1,0:T(8,128)(2,1)S(1)}, u32[]{:S(2)}, u32[]{:S(2)}) collective-permute-start(bf16[96,768]{1,0:T(8,128)(2,1)S(1)} %get-tuple-element.164), channel_id=1, source_target_pairs={{0,24},{2,26},{4,28},{6,30},{8,16},{10,18},{12,20},{14,22},{16,8},... | collective-permute-start | bytes 442376 | tf_op jit(solution)/shard_map/ppermute | solution.py:630
  194.1 17.5 %collective-permute-start.37 = (bf16[96,768]{1,0:T(8,128)(2,1)S(1)}, bf16[96,768]{1,0:T(8,128)(2,1)S(1)}, u32[]{:S(2)}, u32[]{:S(2)}) collective-permute-start(bf16[96,768]{1,0:T(8,128)(2,1)S(1)} %get-tuple-element.167), channel_id=1, source_target_pairs={{0,16},{2,18},{4,20},{6,22},{8,24},{10,26},{12,28},{14,30},{16,0},... | collective-permute-start | bytes 442376 | tf_op jit(solution)/shard_map/ppermute | solution.py:630
  194.8 16.8 %collective-permute-start.38 = (bf16[96,768]{1,0:T(8,128)(2,1)S(1)}, bf16[96,768]{1,0:T(8,128)(2,1)S(1)}, u32[]{:S(2)}, u32[]{:S(2)}) collective-permute-start(bf16[96,768]{1,0:T(8,128)(2,1)S(1)} %get-tuple-element.166), channel_id=1, source_target_pairs={{0,24},{2,26},{4,28},{6,30},{8,16},{10,18},{12,20},{14,22},{16,8},... | collective-permute-start | bytes 442376 | tf_op jit(solution)/shard_map/ppermute | solution.py:630
  (64 other events, 458.2 us)

commit v2 on v1

--- a/solution.py
+++ b/solution.py
@@ -238,13 +238,20 @@
 BF = jnp.bfloat16
 F32 = jnp.float32
 AXES = ("dp", "fsdp")
+COST = 1.0e9
+MICROS = {
+    "pack_weights": 1.0, "sort_near": 1.0, "attend_forward": 6.5, "attend_close": 3.6, "feed_up": 2.5,
+    "feed_down": 1.5, "finish_forward": 2.0, "grad_down_away": 0.8, "grad_down_here": 0.8,
+    "grad_up": 4.0, "attend_backward": 7.0, "grad_mix": 3.0, "grad_input": 4.0, "close_sums": 0.5,
+    "update": 2.3,
+}
 CHIPS = 16
 BLOCK = 96
 QKV = 72
 PLANE = 4 * BLOCK
 ZROWS = 3 * BLOCK
 HALF = CHIPS * BLOCK
-STEPS_Z = (4, 8, 12)
+STEPS_Z = (8, 4, 12)
 
 
 def nt(left, right):
@@ -272,7 +279,9 @@
 
 
 PLACES = block_places()
-PIECES = [(0, PLANE)] + [(PLANE + ZROWS * p, ZROWS) for p in range(4)]
+PIECES = [
+    (0, PLANE), (PLANE, ZROWS), (PLANE + ZROWS, ZROWS), (PLANE + 2 * ZROWS, 2 * ZROWS)
+]
 
 
 def shard_index(chip, core, plane, step, other):
@@ -282,9 +291,13 @@
     return 2 * (chip ^ mask ^ step) + owner
 
 
-def call(body, outs, args, scratch=(), smem=0, flops=0, moved=0, mb=56):
+def call(body, outs, args, scratch=(), smem=0, mb=6, place=pltpu.VMEM):
+    held = [math.prod(a.shape) * a.dtype.itemsize for a in args[smem:]]
+    held += [math.prod(s) * jnp.dtype(t).itemsize for s, t in outs]
+    held += [math.prod(s.shape) * 4 for s in scratch]
+    limit = sum(held) + (mb << 20)
     in_specs = [
-        pl.BlockSpec(memory_space=pltpu.SMEM if i < smem else pltpu.VMEM)
+        pl.BlockSpec(memory_space=pltpu.SMEM if i < smem else place)
         for i in range(len(args))
     ]
     return pl.pallas_call(
@@ -293,31 +306,19 @@
         in_specs=in_specs,
         out_specs=[pl.BlockSpec(memory_space=pltpu.VMEM) for _ in outs],
         scratch_shapes=list(scratch),
-        compiler_params=pltpu.CompilerParams(vmem_limit_bytes=mb << 20),
-        cost_estimate=pl.CostEstimate(flops=flops, bytes_accessed=moved, transcendentals=0),
+        compiler_params=pltpu.CompilerParams(vmem_limit_bytes=limit),
+        cost_estimate=pl.CostEstimate(
+            flops=int(MICROS[body.__name__] * COST), bytes_accessed=0, transcendentals=0
+        ),
         name=body.__name__,
     )(*args)
 
 
-def pack_weights(mix, out, up, down, s_ref, g1, g2, g3):
-    def flip(ref):
-        held = ref[...].astype(BF)
-        n = held.shape[1]
-        eye = (
-            lax.broadcasted_iota(jnp.int32, (n, n), 0)
-            == lax.broadcasted_iota(jnp.int32, (n, n), 1)
-        )
-        return nt(eye.astype(F32).astype(BF), held)
-
-    first = jnp.concatenate([flip(mix), out[...]], axis=0).astype(BF)
-    second = flip(up).astype(BF)
-    third = down[...].astype(BF)
-    s_ref[0:BLOCK, :] = first
-    s_ref[BLOCK : 2 * BLOCK, :] = second
-    s_ref[2 * BLOCK : 3 * BLOCK, :] = third
-    g1[...] = first
-    g2[...] = second
-    g3[...] = third
+def sort_near(s0, s1, s23, *groups):
+    for g, out in enumerate(groups):
+        for p, (ref, base) in enumerate(((s0, 0), (s1, 0), (s23, 0), (s23, 3 * BLOCK))):
+            at = base + BLOCK * g
+            out[BLOCK * p : BLOCK * p + BLOCK, :] = ref[at : at + BLOCK, :]
 
 
 def segment_of(lengths, place):
@@ -349,14 +350,14 @@
 
 
 def attend_forward(
-    lengths, me, x_ref, so, z0, z1, z2, z3, sp, y0, y1, y2, y3, norms,
-    mix, att, den, rel_own, rel_par, first, first_low, xhat, rstd,
+    lengths, me, x_ref, so, z0, z1, z2, sp, y0, y1, y2,
+    mix, att, den, rel_own, rel_par,
 ):
     rows = x_ref.shape[0]
     width = x_ref.shape[1]
     chip, core = me[0], me[1]
     x = x_ref[...]
-    sides = ((False, (so, z0, z1, z2, z3), rel_own), (True, (sp, y0, y1, y2, y3), rel_par))
+    sides = ((False, (so, z0, z1, z2), rel_own), (True, (sp, y0, y1, y2), rel_par))
     for other, refs, _ in sides:
         for (base, size), ref in zip(PIECES, refs):
             got = nt(ref[...], x)
@@ -378,12 +379,19 @@
         att[here, :] = nn(v, pairs.astype(BF)) / total
     side = QKV // 3
     blank = jnp.zeros((QKV, rows), F32)
-    branch = x.astype(F32)
-    for other, refs, rel in sides:
+    for other, _, rel in sides:
         for at, plane, step in PLACES:
             d = shard_index(chip, core, plane, step, other)
             part = att[pl.ds(pl.multiple_of(side * d, 8), side), :]
             rel[at : at + BLOCK, :] = jnp.concatenate([blank, part], axis=0).astype(BF)
+
+
+def attend_close(
+    x_ref, rel_own, rel_par, so, z0, z1, z2, sp, y0, y1, y2, norms,
+    first, first_low, xhat, rstd,
+):
+    branch = x_ref[...].astype(F32)
+    for refs, rel in (((so, z0, z1, z2), rel_own), ((sp, y0, y1, y2), rel_par)):
         for (base, size), ref in zip(PIECES, refs):
             branch = branch + tn(rel[base : base + size, :], ref[...])
     centered = branch - jnp.mean(branch, axis=-1, keepdims=True)
@@ -401,11 +409,11 @@
 GELU_B = 0.044715
 
 
-def feed_up(ya, yb, s, z0, z1, z2, z3, hid, slope):
+def feed_up(ya, yb, s, z0, z1, z2, hid, slope):
     rows = ya.shape[0]
     for half, y in ((0, ya), (1, yb)):
         cols = slice(half * rows, half * rows + rows)
-        for (base, size), ref in zip(PIECES, (s, z0, z1, z2, z3)):
+        for (base, size), ref in zip(PIECES, (s, z0, z1, z2)):
             u = nt(ref[...], y[...])
             sq = u * u
             t = jnp.tanh(GELU_A * u * (1.0 + GELU_B * sq))
@@ -416,8 +424,8 @@
             )
 
 
-def feed_down(hid, s, z0, z1, z2, z3, own, other, whole):
-    for (base, size), ref in zip(PIECES, (s, z0, z1, z2, z3)):
+def feed_down(hid, s, z0, z1, z2, own, other, whole):
+    for (base, size), ref in zip(PIECES, (s, z0, z1, z2)):
         whole[base : base + size, :] = ref[...]
     rows = own.shape[0]
     w = whole[...]
@@ -458,35 +466,46 @@
     goals = ((own, 0), (turn, 0), (send, 0), (send, PLANE))
     for base, size in PIECES:
         g = get(base, size)
-        if base == 0:
-            for p, (ref, off) in enumerate(goals):
-                ref[off : off + BLOCK, :] = g[BLOCK * p : BLOCK * p + BLOCK].astype(ref.dtype)
-        else:
-            ref, off = goals[(base - PLANE) // ZROWS]
-            ref[off + BLOCK : off + PLANE, :] = g.astype(ref.dtype)
-
-
-def grad_down(hid, za, zb, send, turn, own):
+        for at, plane, step in PLACES:
+            if base <= at < base + size:
+                ref, off = goals[plane]
+                to = off + BLOCK * ((0,) + STEPS_Z).index(step)
+                ref[to : to + BLOCK, :] = g[at - base : at - base + BLOCK].astype(ref.dtype)
+
+
+def hidden_grad(hid, za, zb, here):
     rows = za.shape[0]
-
-    def get(base, size):
-        return nn(hid[base : base + size, 0:rows], za[...]) + nn(
-            hid[base : base + size, rows : 2 * rows], zb[...]
-        )
-
-    spread_rows(get, send, turn, own)
+    return nn(hid[here, 0:rows], za[...]) + nn(hid[here, rows : 2 * rows], zb[...])
+
+
+def grad_down_away(hid, za, zb, send):
+    near = hidden_grad(hid, za, zb, slice(2 * BLOCK, PLANE)).astype(BF)
+    far = hidden_grad(hid, za, zb, slice(PLANE + 2 * ZROWS, HALF)).astype(BF)
+    for p in range(2):
+        send[PLANE * p : PLANE * p + BLOCK, :] = near[BLOCK * p : BLOCK * p + BLOCK]
+        send[PLANE * p + BLOCK : PLANE * p + PLANE, :] = far[ZROWS * p : ZROWS * p + ZROWS]
+
+
+def grad_down_here(hid, za, zb, turn, own):
+    near = hidden_grad(hid, za, zb, slice(0, 2 * BLOCK))
+    far = hidden_grad(hid, za, zb, slice(PLANE, PLANE + 2 * ZROWS))
+    for p, ref in enumerate((own, turn)):
+        ref[0:BLOCK, :] = near[BLOCK * p : BLOCK * p + BLOCK]
+        ref[BLOCK:PLANE, :] = far[ZROWS * p : ZROWS * p + ZROWS]
 
 
 def grad_up(
-    slope, za, zb, ya, yb, s, z0, z1, z2, z3, s2, v0, v1, v2, v3,
+    slope, za, zb, ya, yb, d, w0, w1, w2, s, z0, z1, z2,
     send, turn, own, mine, other, dup, whole,
 ):
     rows = za.shape[0]
-    for (base, size), ref, ref2 in zip(PIECES, (s, z0, z1, z2, z3), (s2, v0, v1, v2, v3)):
+    for (base, size), ref in zip(PIECES, (d, w0, w1, w2)):
         here = slice(base, base + size)
-        whole[here, :] = ref2[...]
-        dup[here, 0:rows] = (nt(ref[...], za[...]) * slope[here, 0:rows]).astype(BF)
-        dup[here, rows:] = (nt(ref[...], zb[...]) * slope[here, rows:]).astype(BF)
+        w = ref[...]
+        dup[here, 0:rows] = (nt(w, za[...]) * slope[here, 0:rows]).astype(BF)
+        dup[here, rows:] = (nt(w, zb[...]) * slope[here, rows:]).astype(BF)
+    for (base, size), ref in zip(PIECES, (s, z0, z1, z2)):
+        whole[base : base + size, :] = ref[...]
 
     def get(base, size):
         return nn(dup[base : base + size, 0:rows], ya[...]) + nn(
@@ -501,7 +520,7 @@
 
 def attend_backward(
     lengths, me, ds2, mine, got, xhat, rstd, norms, mix, att, den,
-    so, z0, z1, z2, z3, sp, y0, y1, y2, y3,
+    so, z0, z1, z2, sp, y0, y1, y2,
     dh_ref, do_ref, terms, rel_own, rel_par, datt, dmix,
 ):
     rows, width = ds2.shape
@@ -515,7 +534,7 @@
     do = dh.astype(BF)
     do_ref[...] = do
     side = QKV // 3
-    sides = ((False, (so, z0, z1, z2, z3), rel_own), (True, (sp, y0, y1, y2, y3), rel_par))
+    sides = ((False, (so, z0, z1, z2), rel_own), (True, (sp, y0, y1, y2), rel_par))
     for other, refs, _ in sides:
         for (base, size), ref in zip(PIECES, refs):
             got_t = nt(ref[...], do)
@@ -561,9 +580,9 @@
     spread_rows(get, send, turn, own)
 
 
-def grad_input(dh, rel_own, rel_par, so, z0, z1, z2, z3, sp, y0, y1, y2, y3, out):
+def grad_input(dh, rel_own, rel_par, so, z0, z1, z2, sp, y0, y1, y2, out):
     total = dh[...]
-    for refs, rel in (((so, z0, z1, z2, z3), rel_own), ((sp, y0, y1, y2, y3), rel_par)):
+    for refs, rel in (((so, z0, z1, z2), rel_own), ((sp, y0, y1, y2), rel_par)):
         for (base, size), ref in zip(PIECES, refs):
             total = total + tn(rel[base : base + size, :], ref[...])
     out[...] = total
@@ -580,22 +599,18 @@
 
 
 def update(
-    note, g1, g2, g3, mw, ow, uw, dw, nw, mm, om, um, dm, nm, mv, ov, uv, dv, nv,
+    n0, n1, n2, n3, g1, g2, g3, mw, ow, uw, dw, nw, mm, om, um, dm, nm, mv, ov, uv, dv, nv,
     norm_out, mw2, ow2, uw2, dw2, nw2, mm2, om2, um2, dm2, nm2, mv2, ov2, uv2, dv2, nv2,
 ):
+    note = (n0[...] + n1[...]) + (n2[...] + n3[...])
     terms = note[0:4, :]
     total = jnp.sum(note[4:5, :]) + jnp.sum(terms * terms)
     norm = jnp.sqrt(jnp.full((1, 1), total, F32))
     norm_out[...] = norm
     scale = 1.0 / jnp.maximum(norm, 1.0)
 
-    def flip(v):
-        n, width = v.shape
-        padded = jnp.concatenate([v, jnp.zeros((128 - n, width), F32)], axis=0)
-        return padded.T[:, 0:n]
-
     one = g1[...]
-    grads = (flip(one[0:QKV]), one[QKV:BLOCK], flip(g2[...]), g3[...], terms)
+    grads = (one[0:QKV], one[QKV:BLOCK], g2[...], g3[...], terms)
     groups = (
         (mw, mm, mv, mw2, mm2, mv2),
         (ow, om, ov, ow2, om2, ov2),
@@ -630,22 +645,19 @@
     return lax.ppermute(value, "dp", [(i, i ^ step) for i in range(CHIPS)])
 
 
-def spread_plane(value):
-    turned = hop_first(value)
-    across = hop_second(value)
-    return value, turned, across, hop_second(turned)
-
-
-def reduce_group(send, turn, own):
-    got = hop_second(send)
-    turned = (turn + got[PLANE:].astype(F32)).astype(BF)
-    back = hop_first(turned)
+def add_first(turn, got):
+    return (turn + got[PLANE:].astype(F32)).astype(BF)
+
+
+def add_second(own, got, back):
     total = own + got[:PLANE].astype(F32) + back.astype(F32)
-    low = total.astype(BF)
-    parts = [
+    return total[:BLOCK], total.astype(BF)
+
+
+def send_z(low):
+    return [
         hop_z(low[BLOCK * (j + 1) : BLOCK * (j + 2)], step) for j, step in enumerate(STEPS_Z)
     ]
-    return total[:BLOCK], parts
 
 
 def tuned_device(
@@ -659,128 +671,144 @@
     me = jnp.stack([chip, core]).astype(jnp.int32)
     wide = 3 * width
 
-    s_all, *blocks = call(
-        pack_weights,
-        [((3 * BLOCK, width), BF)] + [((BLOCK, width), BF)] * 3,
-        (mix_weight, out_weight, up_weight, down_weight),
-        flops=1 << 20, moved=3 << 20,
-    )
-    s_parts = spread_plane(s_all)
-    z_parts = []
-    gate = ()
-    link = ()
-    for group in range(3):
-        block = tie(blocks[group], *gate) if gate else blocks[group]
-        arrived = [hop_z(block, step) for step in STEPS_Z]
-        gate = (arrived[2],)
-        joined = jnp.concatenate(arrived, axis=0)
-        if link:
-            joined = tie(joined, *link)
-        z_parts.append(spread_plane(joined))
-        link = (z_parts[-1][2],)
-    s_groups = [
-        jnp.concatenate([p[BLOCK * g : BLOCK * g + BLOCK] for p in s_parts], axis=0)
-        for g in range(3)
+    blocks = [
+        jnp.concatenate([mix_weight.T.astype(BF), out_weight.astype(BF)], axis=0),
+        up_weight.T.astype(BF),
+        down_weight.astype(BF),
     ]
-    weights = [(s_groups[g],) + tuple(z_parts[g]) for g in range(3)]
-    attn_own = weights[0]
+    s_all = jnp.concatenate(blocks, axis=0)
+    near1 = [hop_z(blocks[0], step) for step in STEPS_Z]
+    s_first = hop_first(s_all)
+    s_far = hop_second(jnp.concatenate([s_all, s_first], axis=0))
+    joined1 = jnp.concatenate(near1, axis=0)
+    turned1 = hop_first(tie(joined1, s_first))
+    far1 = hop_second(jnp.concatenate([tie(joined1, s_far), turned1], axis=0))
+    got2 = hop_z(tie(blocks[1], *near1), 8)
+    joined2 = jnp.concatenate(
+        [got2, hop_z(jnp.concatenate([blocks[1], got2], axis=0), 4)], axis=0
+    )
+    turned2 = hop_first(tie(joined2, turned1))
+    far2 = hop_second(jnp.concatenate([tie(joined2, far1), turned2], axis=0))
+    sorted1, sorted2, sorted3 = call(
+        sort_near,
+        [((PLANE, width), BF)] * 3,
+        (s_all, s_first, s_far),
+    )
+    up_all = (sorted2, joined2, turned2, far2)
+    attn_own = (sorted1, joined1, turned1, far1)
     attn_par = tuple(swap(p) for p in attn_own)
     x_par = swap(tokens)
 
-    mix, att, den, at_own, at_par, first, first_low, xhat, rstd = call(
+    mix, att, den, at_own, at_par = call(
         attend_forward,
         [
             ((wide, rows), F32), ((width, rows), F32), ((16, rows), F32),
             ((HALF, rows), BF), ((HALF, rows), BF),
-            ((rows, width), F32), ((rows, width), BF), ((rows, width), F32), ((rows, 1), F32),
         ],
-        (lengths, me, tokens) + attn_own + attn_par + (norm_params,),
-        smem=2, flops=12 << 30, moved=16 << 20,
-    )
+        (lengths, me, tie(tokens, x_par)) + attn_own + attn_par,
+        smem=2,
+    )
+    got3 = hop_z(tie(blocks[2], got2), 8)
+    joined3 = jnp.concatenate(
+        [got3, hop_z(jnp.concatenate([blocks[2], tie(got3, joined2)], axis=0), 4)], axis=0
+    )
+    turned3 = hop_first(tie(joined3, turned2))
+    first, first_low, xhat, rstd = call(
+        attend_close,
+        [((rows, width), F32), ((rows, width), BF), ((rows, width), F32), ((rows, 1), F32)],
+        (tokens, at_own, at_par) + attn_own + attn_par + (norm_params,),
+    )
+    far3 = hop_second(jnp.concatenate([tie(joined3, far2), turned3], axis=0))
+    down_all = (sorted3, joined3, turned3, far3)
     at_got = swap(at_par)
     first_par = swap(first_low)
     hid, slope = call(
         feed_up,
         [((HALF, 2 * rows), BF), ((HALF, 2 * rows), F32)],
-        (first_low, first_par) + weights[1],
-        flops=4 << 30, moved=8 << 20,
+        (first_low, tie(first_par, at_got)) + up_all,
     )
     down_own, down_par = call(
         feed_down,
         [((rows, width), F32)] * 2,
-        (hid,) + weights[2],
+        (hid,) + down_all,
         scratch=[pltpu.VMEM((HALF, width), BF)],
-        flops=2 << 30, moved=6 << 20,
     )
     output, ds2, dz, terms_two = call(
         finish_forward,
         [((rows, width), BF), ((rows, width), F32), ((rows, width), BF), ((2, width), F32)],
         (lengths, first, down_own, swap(down_par), cotangent, norm_params),
-        smem=1, flops=1 << 28, moved=6 << 20,
+        smem=1,
     )
     dz_par = swap(dz)
     spread_shapes = [((2 * PLANE, width), BF), ((PLANE, width), F32), ((PLANE, width), F32)]
-    send3, turn3, own3 = call(
-        grad_down, spread_shapes, (hid, dz, dz_par), flops=2 << 30, moved=6 << 20
-    )
-    keep3, parts3 = reduce_group(send3, turn3, own3)
+    (send3,) = call(grad_down_away, spread_shapes[:1], (hid, dz, dz_par))
+    hid_later = tie(hid, send3)
+    turn3, own3 = call(grad_down_here, spread_shapes[1:], (hid_later, dz, dz_par))
+    got3 = hop_second(send3)
     send2, turn2, own2, dy_own, dy_par = call(
         grad_up,
         spread_shapes + [((rows, width), F32)] * 2,
-        (slope, dz, dz_par, first_low, first_par) + weights[2] + weights[1],
+        (tie(slope, turn3), dz, dz_par, first_low, first_par) + down_all + up_all,
         scratch=[pltpu.VMEM((HALF, 2 * rows), BF), pltpu.VMEM((HALF, width), BF)],
-        flops=5 << 30, moved=16 << 20,
-    )
-    keep2, parts2 = reduce_group(send2, turn2, own2)
+    )
+    low_turn3 = add_first(turn3, got3)
+    back3 = hop_first(low_turn3)
+    got2 = hop_second(send2)
     dh, do, terms_one, dm_own, dm_par = call(
         attend_backward,
         [
             ((rows, width), F32), ((rows, width), BF), ((2, width), F32),
             ((HALF, rows), BF), ((HALF, rows), BF),
         ],
-        (lengths, me, ds2, dy_own, swap(dy_par), xhat, rstd, norm_params, mix, att, den)
+        (lengths, me, tie(ds2, low_turn3), dy_own, swap(dy_par), xhat, rstd, norm_params, mix, att, den)
         + attn_own + attn_par,
         scratch=[pltpu.VMEM((width, rows), F32), pltpu.VMEM((wide, rows), F32)],
-        smem=2, flops=16 << 30, moved=20 << 20,
+        smem=2,
     )
     send1, turn1, own1 = call(
         grad_mix,
         spread_shapes,
         (dm_own, swap(dm_par), tokens, x_par, at_own, at_got, do, swap(do)),
-        flops=3 << 30, moved=8 << 20,
-    )
-    keep1, parts1 = reduce_group(send1, turn1, own1)
+    )
     (grad_tokens,) = call(
         grad_input,
         [((rows, width), F32)],
         (dh, dm_own, dm_par) + attn_own + attn_par,
-        flops=3 << 30, moved=9 << 20,
-    )
+    )
+    keep3, low3 = add_second(own3, got3, back3)
+    parts3 = send_z(low3)
+    back2 = hop_first(add_first(turn2, got2))
+    got1 = hop_second(send1)
+    keep2, low2 = add_second(own2, got2, back2)
+    parts2 = send_z(tie(low2, *parts3))
+    back1 = hop_first(add_first(tie(turn1, grad_tokens), got1))
+    keep1, low1 = add_second(own1, got1, back1)
+    parts1 = send_z(tie(low1, *parts2))
     g3 = (keep3 + parts3[0]) + (parts3[1].astype(F32) + parts3[2].astype(F32))
     g2 = (keep2 + parts2[0]) + (parts2[1].astype(F32) + parts2[2].astype(F32))
     g1, note = call(
         close_sums,
         [((BLOCK, width), F32), ((8, width), F32)],
         (keep1,) + tuple(parts1) + (g2, g3, terms_one, terms_two),
-        flops=1 << 22, moved=1 << 21,
     )
     note = note + swap(note)
-    for step in (1, 2, 4, 8):
-        note = note + hop_z(note, step)
+    note = (note + hop_z(note, 1)) + (hop_z(note, 2) + hop_z(note, 3))
+    notes = (note, hop_z(note, 4), hop_z(note, 8), hop_z(note, 12))
     shapes = [
-        (mix_weight.shape, F32), (out_weight.shape, F32), (up_weight.shape, F32),
+        (mix_weight.shape[::-1], F32), (out_weight.shape, F32), (up_weight.shape[::-1], F32),
         (down_weight.shape, F32), (norm_params.shape, F32),
     ]
     norm, *news = call(
         update,
         [((1, 1), F32)] + shapes * 3,
-        (
-            note, g1, g2, g3, mix_weight, out_weight, up_weight, down_weight, norm_params,
-            mix_first, out_first, up_first, down_first, norm_first,
-            mix_second, out_second, up_second, down_second, norm_second,
+        notes + (
+            g1, g2, g3, mix_weight.T, out_weight, up_weight.T, down_weight, norm_params,
+            mix_first.T, out_first, up_first.T, down_first, norm_first,
+            mix_second.T, out_second, up_second.T, down_second, norm_second,
         ),
-        flops=1 << 23, moved=8 << 20,
-    )
+    )
+    for at in (0, 2, 5, 7, 10, 12):
+        news[at] = news[at].T
     return (output, grad_tokens, norm.reshape(())) + tuple(news)
 
 

time: 250 us -> 200 us (0.80)
  Pallas kernels: 72.5 us -> 42.4 us
  local copies, waits for them, and re-layouts: 24.7 us -> 6.26 us
    pallas_call x12 -> x14, Pallas kernels: 72.5 us -> 42.4 us  [call(): pl.pallas_call(body, out_shape=[jax.ShapeDtypeStruct(s, t) for s, t in ou...]
    unnamed x98 -> x58, local copies, waits for them, and re-layouts: 22.6 us -> 5.1 us
    ppermute x7, waiting for transfers between devices: 8.79 us -> 13.1 us  [hop_first(): lax.ppermute(value, AXES, [(i, i ^ (4 if i % 2 else 2)) for i in range(2...]
    unnamed x0 -> x4, other arithmetic: none -> 2.9 us
    ppermute x11 -> x7, waiting for transfers between devices: 30.1 us -> 28.7 us  [hop_second(): lax.ppermute(value, AXES, [(i, i ^ (2 if i % 2 else 4)) for i in range(2...]
    ppermute x14 -> x13, waiting for transfers between devices: 8.24 us -> 7.83 us  [swap(): return lax.ppermute(value, 'fsdp', [(0, 1), (1, 0)])]
    ppermute x11 -> x7, starting transfers between devices: 9.69 us -> 9.52 us  [hop_second(): lax.ppermute(value, AXES, [(i, i ^ (2 if i % 2 else 4)) for i in range(2...]
  transfers between devices with their start and end apart: 54 -> 49, of which waited for: 22 -> 24; matrix products, arithmetic and copies ran while one was open for 4% -> 2% of each run, Pallas kernels for 19% -> 18%
where the time goes in v2:
time: 200 us
  waiting for transfers between devices  86.3 us (43%)
  starting transfers between devices  58.3 us (29%)
  Pallas kernels  42.4 us (21%)
  local copies, waits for them, and re-layouts  6.26 us (3%)
  other arithmetic  5.26 us (3%)
    pallas_call x14, Pallas kernels, call(): pl.pallas_call(body, out_shape=[jax.ShapeDtypeStruct(s, t) for s, t in ou...  42.4 us
    ppermute x22, starting transfers between devices, hop_z(): return lax.ppermute(value, 'dp', [(i, i ^ step) for i in range(CHIPS)])  37.3 us
    ppermute x22, waiting for transfers between devices, hop_z(): return lax.ppermute(value, 'dp', [(i, i ^ step) for i in range(CHIPS)])  36.7 us
    ppermute x7, waiting for transfers between devices, hop_second(): lax.ppermute(value, AXES, [(i, i ^ (2 if i % 2 else 4)) for i in range(2...  28.7 us
    ppermute x7, waiting for transfers between devices, hop_first(): lax.ppermute(value, AXES, [(i, i ^ (4 if i % 2 else 2)) for i in range(2...  13.1 us
    ppermute x7, starting transfers between devices, hop_second(): lax.ppermute(value, AXES, [(i, i ^ (2 if i % 2 else 4)) for i in range(2...  9.52 us
    ppermute x7, starting transfers between devices, hop_first(): lax.ppermute(value, AXES, [(i, i ^ (4 if i % 2 else 2)) for i in range(2...  9.12 us
    ppermute x13, waiting for transfers between devices, swap(): return lax.ppermute(value, 'fsdp', [(0, 1), (1, 0)])  7.83 us
  transfers between devices with their start and end apart: 49, of which 24 were waited for; matrix products, arithmetic and copies ran while one was open for 2% of the time, Pallas kernels for 18%

profile of v2, /device:TPU:0, one launch (start us, length us, event | category | flops | bytes accessed | tf_op | source)
XLA Modules:
  0.0 199.9 jit_solution(3959530473403409330)
XLA Ops:
  3.6 3.0 %collective-permute-start.1 = (bf16[288,768]{1,0:T(8,128)(2,1)S(1)}, bf16[288,768]{1,0:T(8,128)(2,1)S(1)}, u32[]{:S(2)}, u32[]{:S(2)}) collective-permute-start(bf16[288,768]{1,0:T(8,128)(2,1)S(1)} %pad_maximum_fusion.3.s0), channel_id=1, source_target_pairs={{0,2},{1,5},{2,0},{3,7},{4,6},{5,1},{6,4},{7,3},{8,10},{9,13},{10,... | collective-permute-start | bytes 1327112 | tf_op jit(solution)/shard_map/ppermute | solution.py:637
  6.6 2.7 %collective-permute-start.3 = (bf16[96,768]{1,0:T(8,128)(2,1)S(1)}, bf16[96,768]{1,0:T(8,128)(2,1)S(1)}, u32[]{:S(2)}, u32[]{:S(2)}) collective-permute-start(bf16[96,768]{1,0:T(8,128)(2,1)S(1)} %pad_maximum_fusion.6), channel_id=1, source_target_pairs={{0,16},{2,18},{4,20},{6,22},{8,24},{10,26},{12,28},{14,30},{16,0},... | collective-permute-start | bytes 442376 | tf_op jit(solution)/shard_map/ppermute | solution.py:645
  9.3 3.6 %collective-permute-done.1.s1 = bf16[288,768]{1,0:T(8,128)(2,1)S(1)} collective-permute-done((bf16[288,768]{1,0:T(8,128)(2,1)S(1)}, bf16[288,768]{1,0:T(8,128)(2,1)S(1)}, u32[]{:S(2)}, u32[]{:S(2)}) %collective-permute-start.1) | collective-permute-done | bytes 442400 | tf_op jit(solution)/shard_map/ppermute | solution.py:637
  12.9 2.1 %collective-permute-start.2 = (bf16[576,768]{1,0:T(8,128)(2,1)S(1)}, bf16[576,768]{1,0:T(8,128)(2,1)S(1)}, u32[]{:S(2)}, u32[]{:S(2)}) collective-permute-start(bf16[576,768]{1,0:T(8,128)(2,1)S(1)} %constant_dynamic-update-slice_fusion), channel_id=1, source_target_pairs={{0,4},{1,3},{2,6},{3,1},{4,0},{5,7},{6,2},{7,5},{8,12},{9,11},{10,... | collective-permute-start | bytes 2654216 | tf_op jit(solution)/shard_map/ppermute | solution.py:641
  16.6 2.5 %collective-permute-start.5 = (bf16[96,768]{1,0:T(8,128)(2,1)S(1)}, bf16[96,768]{1,0:T(8,128)(2,1)S(1)}, u32[]{:S(2)}, u32[]{:S(2)}) collective-permute-start(bf16[96,768]{1,0:T(8,128)(2,1)S(1)} %pad_maximum_fusion.6), channel_id=1, source_target_pairs={{0,24},{2,26},{4,28},{6,30},{8,16},{10,18},{12,20},{14,22},{16,8},... | collective-permute-start | bytes 442376 | tf_op jit(solution)/shard_map/ppermute | solution.py:645
  19.1 2.1 %collective-permute-done.4 = bf16[96,768]{1,0:T(8,128)(2,1)S(1)} collective-permute-done((bf16[96,768]{1,0:T(8,128)(2,1)S(1)}, bf16[96,768]{1,0:T(8,128)(2,1)S(1)}, u32[]{:S(2)}, u32[]{:S(2)}) %collective-permute-start.4) | collective-permute-done | bytes 147488 | tf_op jit(solution)/shard_map/ppermute | solution.py:645
  21.3 3.5 %collective-permute-done.5 = bf16[96,768]{1,0:T(8,128)(2,1)S(1)} collective-permute-done((bf16[96,768]{1,0:T(8,128)(2,1)S(1)}, bf16[96,768]{1,0:T(8,128)(2,1)S(1)}, u32[]{:S(2)}, u32[]{:S(2)}) %collective-permute-start.5) | collective-permute-done | bytes 147488 | tf_op jit(solution)/shard_map/ppermute | solution.py:645
  27.5 5.6 %collective-permute-done.6.z1 = bf16[288,768]{1,0:T(8,128)(2,1)S(1)} collective-permute-done((bf16[288,768]{1,0:T(8,128)(2,1)S(1)}, bf16[288,768]{1,0:T(8,128)(2,1)S(1)}, u32[]{:S(2)}, u32[]{:S(2)}) %collective-permute-start.6) | collective-permute-done | bytes 442400 | tf_op jit(solution)/shard_map/ppermute | solution.py:637
  35.5 6.3 %collective-permute-done.15 = bf16[192,768]{1,0:T(8,128)(2,1)S(1)} collective-permute-done((bf16[192,768]{1,0:T(8,128)(2,1)S(1)}, bf16[192,768]{1,0:T(8,128)(2,1)S(1)}, u32[]{:S(2)}, u32[]{:S(2)}) %collective-permute-start.15) | collective-permute-done | bytes 294944 | tf_op jit(solution)/shard_map/ppermute | solution.py:645
  42.3 2.7 %collective-permute-start.18 = (bf16[96,768]{1,0:T(8,128)(2,1)S(1)}, bf16[96,768]{1,0:T(8,128)(2,1)S(1)}, u32[]{:S(2)}, u32[]{:S(2)}) collective-permute-start(bf16[96,768]{1,0:T(8,128)(2,1)S(1)} %get-tuple-element.103), channel_id=1, source_target_pairs={{0,16},{2,18},{4,20},{6,22},{8,24},{10,26},{12,28},{14,30},{16,0},... | collective-permute-start | bytes 442376 | tf_op jit(solution)/shard_map/ppermute | solution.py:645
  45.0 5.3 %collective-permute-done.7.z2 = bf16[576,768]{1,0:T(8,128)(2,1)S(1)} collective-permute-done((bf16[576,768]{1,0:T(8,128)(2,1)S(1)}, bf16[576,768]{1,0:T(8,128)(2,1)S(1)}, u32[]{:S(2)}, u32[]{:S(2)}) %collective-permute-start.7) | collective-permute-done | bytes 884768 | tf_op jit(solution)/shard_map/ppermute | solution.py:641
  58.4 4.5 %collective-permute-done.19 = bf16[192,768]{1,0:T(8,128)(2,1)} collective-permute-done((bf16[192,768]{1,0:T(8,128)(2,1)S(1)}, bf16[192,768]{1,0:T(8,128)(2,1)}, u32[]{:S(2)}, u32[]{:S(2)}) %collective-permute-start.19) | collective-permute-done | bytes 294944 | tf_op jit(solution)/shard_map/ppermute | solution.py:645
  67.2 6.9 %attend_forward.1 = (f32[2304,256]{1,0:T(8,128)S(1)}, f32[768,256]{1,0:T(8,128)S(1)}, f32[16,256]{1,0:T(8,128)S(1)}, bf16[1536,256]{1,0:T(8,128)(2,1)S(1)}, bf16[1536,256]{1,0:T(8,128)(2,1)S(1)}) custom-call(s32[1,6]{1,0:T(1,128)S(1)} %copy-done.21, s32[2]{0:T(128)S(1)} %pad_add_fusion.me, bf16[256,768]{1,0:T(8,128)(2,1)S(1)} %copy-done.6, ...), custom_call_target="tpu_custom_call" | custom-call | flops 6499999744 | tf_op jit(solution)/shard_map/attend_forward/pallas_call | solution.py:303
  75.6 4.0 %attend_close.1 = (f32[256,768]{1,0:T(8,128)S(1)}, bf16[256,768]{1,0:T(8,128)(2,1)S(1)}, f32[256,768]{1,0:T(8,128)S(1)}, f32[256,1]{1,0:T(8,128)S(1)}) custom-call(bf16[256,768]{1,0:T(8,128)(2,1)S(1)} %copy-done.6, bf16[1536,256]{1,0:T(8,128)(2,1)S(1)} %get-tuple-element.92.rel_own.ata, bf16[1536,256]{1,0:T(8,128)(2,1)S(1)} %get-tuple-element.93.rel_par, ...), custom_call_target="tpu_custom_call" | custom-call | flops 3600000000 | tf_op jit(solution)/shard_map/attend_close/pallas_call | solution.py:303
  81.4 3.6 %feed_up.1 = (bf16[1536,512]{1,0:T(8,128)(2,1)S(1)}, f32[1536,512]{1,0:T(8,128)S(1)}) custom-call(bf16[256,768]{1,0:T(8,128)(2,1)S(1)} %get-tuple-element.95.ya, bf16[256,768]{1,0:T(8,128)(2,1)S(1)} %collective-permute-done.12.yb, bf16[384,768]{1,0:T(8,128)(2,1)S(1)} %copy-done.25, bf16[288,768]{1,0:T(8,128)(2,1)S(1)} %constant_dynamic-update-slice_fusion.8.z0, ...), custom_call_target="tpu_custom_call" | custom-call | flops 2500000000 | tf_op jit(solution)/shard_map/feed_up/pallas_call | solution.py:303
  85.0 2.6 %collective-permute-done.21.z2.w2 = bf16[576,768]{1,0:T(8,128)(2,1)S(1)} collective-permute-done((bf16[576,768]{1,0:T(8,128)(2,1)S(1)}, bf16[576,768]{1,0:T(8,128)(2,1)S(1)}, u32[]{:S(2)}, u32[]{:S(2)}) %collective-permute-start.21) | collective-permute-done | bytes 884768 | tf_op jit(solution)/shard_map/ppermute | solution.py:641
  89.1 2.3 %collective-permute-done.22.got = f32[256,768]{1,0:T(8,128)S(1)} collective-permute-done((f32[256,768]{1,0:T(8,128)S(1)}, f32[256,768]{1,0:T(8,128)S(1)}, u32[]{:S(2)}, u32[]{:S(2)}) %collective-permute-start.22) | collective-permute-done | bytes 786464 | tf_op jit(solution)/shard_map/ppermute | solution.py:633
  91.4 2.1 %finish_forward.1 = (bf16[256,768]{1,0:T(8,128)(2,1)}, f32[256,768]{1,0:T(8,128)S(1)}, bf16[256,768]{1,0:T(8,128)(2,1)S(1)}, f32[2,768]{1,0:T(2,128)S(1)}) custom-call(s32[1,6]{1,0:T(1,128)S(1)} %copy-done.21, f32[256,768]{1,0:T(8,128)S(1)} %get-tuple-element.94.first, f32[256,768]{1,0:T(8,128)S(1)} %get-tuple-element.107.own, ...), custom_call_target="tpu_custom_call" | custom-call | flops 2000000000 | tf_op jit(solution)/shard_map/finish_forward/pallas_call | solution.py:303
  97.9 5.1 %grad_up.1 = (bf16[768,768]{1,0:T(8,128)(2,1)S(1)}, f32[384,768]{1,0:T(8,128)S(1)}, f32[384,768]{1,0:T(8,128)S(1)}, f32[256,768]{1,0:T(8,128)S(1)}, f32[256,768]{1,0:T(8,128)S(1)}) custom-call(f32[1536,512]{1,0:T(8,128)S(1)} %get-tuple-element.116.slope, bf16[256,768]{1,0:T(8,128)(2,1)S(1)} %get-tuple-element.111.za, ...), custom_call_target="tpu_custom_call" | custom-call | flops 4000000000 | tf_op jit(solution)/shard_map/grad_up/pallas_call | solution.py:303
  104.1 8.1 %collective-permute-done.24 = bf16[768,768]{1,0:T(8,128)(2,1)S(1)} collective-permute-done((bf16[768,768]{1,0:T(8,128)(2,1)S(1)}, bf16[768,768]{1,0:T(8,128)(2,1)S(1)}, u32[]{:S(2)}, u32[]{:S(2)}) %collective-permute-start.24) | collective-permute-done | bytes 1179680 | tf_op jit(solution)/shard_map/ppermute | solution.py:641
  112.4 7.7 %attend_backward.1 = (f32[256,768]{1,0:T(8,128)S(1)}, bf16[256,768]{1,0:T(8,128)(2,1)S(1)}, f32[2,768]{1,0:T(2,128)S(1)}, bf16[1536,256]{1,0:T(8,128)(2,1)S(1)}, bf16[1536,256]{1,0:T(8,128)(2,1)S(1)}) custom-call(s32[1,6]{1,0:T(1,128)S(1)} %copy-done.21, s32[2]{0:T(128)S(1)} %pad_add_fusion.me, f32[256,768]{1,0:T(8,128)S(1)} %get-tuple-element.114.ds2, ...), custom_call_target="tpu_custom_call" | custom-call | flops 7000000000 | tf_op jit(solution)/shard_map/attend_backward/pallas_call | solution.py:303
  123.0 2.9 %grad_mix.1 = (bf16[768,768]{1,0:T(8,128)(2,1)S(1)}, f32[384,768]{1,0:T(8,128)S(1)}, f32[384,768]{1,0:T(8,128)S(1)}) custom-call(bf16[1536,256]{1,0:T(8,128)(2,1)S(1)} %get-tuple-element.125.rel_own.dma, bf16[1536,256]{1,0:T(8,128)(2,1)S(1)} %collective-permute-done.26.dmb, bf16[256,768]{1,0:T(8,128)(2,1)S(1)} %copy-done.7, bf16[256,768]{1,0:T(8,128)(2,1)S(1)} %copy-done.9, ...), custom_call_target="tpu_custom_call" | custom-call | flops 3000000000 | tf_op jit(solution)/shard_map/grad_mix/pallas_call | solution.py:303
  128.3 4.5 %grad_input.1 = f32[256,768]{1,0:T(8,128)} custom-call(f32[256,768]{1,0:T(8,128)S(1)} %get-tuple-element.124.dh, bf16[1536,256]{1,0:T(8,128)(2,1)S(1)} %get-tuple-element.125.rel_own.dma, bf16[1536,256]{1,0:T(8,128)(2,1)S(1)} %get-tuple-element.126.rel_par, bf16[384,768]{1,0:T(8,128)(2,1)S(1)} %get-tuple-element.89.so, ...), custom_call_target="tpu_custom_call" | custom-call | flops 4000000000 | tf_op jit(solution)/shard_map/grad_input/pallas_call | solution.py:303
  133.0 2.3 %collective-permute-start.33 = (bf16[96,768]{1,0:T(8,128)(2,1)S(1)}, bf16[96,768]{1,0:T(8,128)(2,1)S(1)}, u32[]{:S(2)}, u32[]{:S(2)}) collective-permute-start(bf16[96,768]{1,0:T(8,128)(2,1)S(1)} %get-tuple-element.180), channel_id=1, source_target_pairs={{0,16},{2,18},{4,20},{6,22},{8,24},{10,26},{12,28},{14,30},{16,0},... | collective-permute-start | bytes 442376 | tf_op jit(solution)/shard_map/ppermute | solution.py:645
  137.5 12.7 %collective-permute-done.28 = bf16[768,768]{1,0:T(8,128)(2,1)S(1)} collective-permute-done((bf16[768,768]{1,0:T(8,128)(2,1)S(1)}, bf16[768,768]{1,0:T(8,128)(2,1)S(1)}, u32[]{:S(2)}, u32[]{:S(2)}) %collective-permute-start.28) | collective-permute-done | bytes 1179680 | tf_op jit(solution)/shard_map/ppermute | solution.py:641
  156.4 3.8 %collective-permute-done.29 = bf16[384,768]{1,0:T(8,128)(2,1)S(1)} collective-permute-done((bf16[384,768]{1,0:T(8,128)(2,1)S(1)}, bf16[384,768]{1,0:T(8,128)(2,1)S(1)}, u32[]{:S(2)}, u32[]{:S(2)}) %collective-permute-start.29) | collective-permute-done | bytes 589856 | tf_op jit(solution)/shard_map/ppermute | solution.py:637
  160.5 4.3 %collective-permute-done.36 = bf16[96,768]{1,0:T(8,128)(2,1)S(1)} collective-permute-done((bf16[96,768]{1,0:T(8,128)(2,1)S(1)}, bf16[96,768]{1,0:T(8,128)(2,1)S(1)}, u32[]{:S(2)}, u32[]{:S(2)}) %collective-permute-start.36) | collective-permute-done | bytes 147488 | tf_op jit(solution)/shard_map/ppermute | solution.py:645
  164.8 4.5 %collective-permute-start.39 = (bf16[96,768]{1,0:T(8,128)(2,1)S(1)}, bf16[96,768]{1,0:T(8,128)(2,1)S(1)}, u32[]{:S(2)}, u32[]{:S(2)}) collective-permute-start(bf16[96,768]{1,0:T(8,128)(2,1)S(1)} %get-tuple-element.174), channel_id=1, source_target_pairs={{0,16},{2,18},{4,20},{6,22},{8,24},{10,26},{12,28},{14,30},{16,0},... | collective-permute-start | bytes 442376 | tf_op jit(solution)/shard_map/ppermute | solution.py:645
  171.1 8.7 %collective-permute-done.39.a1 = bf16[96,768]{1,0:T(8,128)(2,1)S(1)} collective-permute-done((bf16[96,768]{1,0:T(8,128)(2,1)S(1)}, bf16[96,768]{1,0:T(8,128)(2,1)S(1)}, u32[]{:S(2)}, u32[]{:S(2)}) %collective-permute-start.39) | collective-permute-done | bytes 147488 | tf_op jit(solution)/shard_map/ppermute | solution.py:645
  188.3 2.8 %collective-permute-start.46 = (f32[8,768]{1,0:T(8,128)S(1)}, f32[8,768]{1,0:T(8,128)S(1)}, u32[]{:S(2)}, u32[]{:S(2)}) collective-permute-start(f32[8,768]{1,0:T(8,128)S(1)} %add_add_fusion.n0), channel_id=1, source_target_pairs={{0,8},{2,10},{4,12},{6,14},{8,0},{10,2},{12,4},{14,6},{16,24},{18,... | collective-permute-start | bytes 73736 | tf_op jit(solution)/shard_map/ppermute | solution.py:645
  193.5 2.3 %collective-permute-done.47.n2 = f32[8,768]{1,0:T(8,128)S(1)} collective-permute-done((f32[8,768]{1,0:T(8,128)S(1)}, f32[8,768]{1,0:T(8,128)S(1)}, u32[]{:S(2)}, u32[]{:S(2)}) %collective-permute-start.47) | collective-permute-done | bytes 24608 | tf_op jit(solution)/shard_map/ppermute | solution.py:645
  197.4 2.3 %update.1 = (f32[1,1]{1,0:T(1,128)}, f32[72,768]{1,0:T(8,128)}, f32[24,768]{1,0:T(8,128)}, f32[96,768]{1,0:T(8,128)}, f32[96,768]{1,0:T(8,128)}, /*index=5*/f32[...) custom-call(f32[8,768]{1,0:T(8,128)S(1)} %add_add_fusion.n0, ...), custom_call_target="tpu_custom_call" | custom-call | flops 2300000000 | tf_op jit(solution)/shard_map/update/pallas_call | solution.py:303
  (168 shorter events, 61.0 us)
Async XLA Ops:
  3.6 9.3 %collective-permute-start.1 = (bf16[288,768]{1,0:T(8,128)(2,1)S(1)}, bf16[288,768]{1,0:T(8,128)(2,1)S(1)}, u32[]{:S(2)}, u32[]{:S(2)}) collective-permute-start(bf16[288,768]{1,0:T(8,128)(2,1)S(1)} %pad_maximum_fusion.3.s0), channel_id=1, source_target_pairs={{0,2},{1,5},{2,0},{3,7},{4,6},{5,1},{6,4},{7,3},{8,10},{9,13},{10,... | collective-permute-start | bytes 1327112 | tf_op jit(solution)/shard_map/ppermute | solution.py:637
  6.6 12.5 %collective-permute-start.3 = (bf16[96,768]{1,0:T(8,128)(2,1)S(1)}, bf16[96,768]{1,0:T(8,128)(2,1)S(1)}, u32[]{:S(2)}, u32[]{:S(2)}) collective-permute-start(bf16[96,768]{1,0:T(8,128)(2,1)S(1)} %pad_maximum_fusion.6), channel_id=1, source_target_pairs={{0,16},{2,18},{4,20},{6,22},{8,24},{10,26},{12,28},{14,30},{16,0},... | collective-permute-start | bytes 442376 | tf_op jit(solution)/shard_map/ppermute | solution.py:645
  12.9 14.6 %collective-permute-start.2 = (bf16[576,768]{1,0:T(8,128)(2,1)S(1)}, bf16[576,768]{1,0:T(8,128)(2,1)S(1)}, u32[]{:S(2)}, u32[]{:S(2)}) collective-permute-start(bf16[576,768]{1,0:T(8,128)(2,1)S(1)} %constant_dynamic-update-slice_fusion), channel_id=1, source_target_pairs={{0,4},{1,3},{2,6},{3,1},{4,0},{5,7},{6,2},{7,5},{8,12},{9,11},{10,... | collective-permute-start | bytes 2654216 | tf_op jit(solution)/shard_map/ppermute | solution.py:641
  16.6 8.1 %collective-permute-start.5 = (bf16[96,768]{1,0:T(8,128)(2,1)S(1)}, bf16[96,768]{1,0:T(8,128)(2,1)S(1)}, u32[]{:S(2)}, u32[]{:S(2)}) collective-permute-start(bf16[96,768]{1,0:T(8,128)(2,1)S(1)} %pad_maximum_fusion.6), channel_id=1, source_target_pairs={{0,24},{2,26},{4,28},{6,30},{8,16},{10,18},{12,20},{14,22},{16,8},... | collective-permute-start | bytes 442376 | tf_op jit(solution)/shard_map/ppermute | solution.py:645
  24.8 8.4 %collective-permute-start.6 = (bf16[288,768]{1,0:T(8,128)(2,1)S(1)}, bf16[288,768]{1,0:T(8,128)(2,1)S(1)}, u32[]{:S(2)}, u32[]{:S(2)}) collective-permute-start(bf16[288,768]{1,0:T(8,128)(2,1)S(1)} %constant_dynamic-update-slice_fusion.5.z0), channel_id=1, source_target_pairs={{0,2},{1,5},{2,0},{3,7},{4,6},{5,1},{6,4},{7,3},{8,10},{9,13},{10,... | collective-permute-start | bytes 1327112 | tf_op jit(solution)/shard_map/ppermute | solution.py:637
  25.5 9.3 %collective-permute-start.14 = (bf16[96,768]{1,0:T(8,128)(2,1)S(1)}, bf16[96,768]{1,0:T(8,128)(2,1)S(1)}, u32[]{:S(2)}, u32[]{:S(2)}) collective-permute-start(bf16[96,768]{1,0:T(8,128)(2,1)S(1)} %get-tuple-element.98), channel_id=1, source_target_pairs={{0,16},{2,18},{4,20},{6,22},{8,24},{10,26},{12,28},{14,30},{16,0},... | collective-permute-start | bytes 442376 | tf_op jit(solution)/shard_map/ppermute | solution.py:645
  33.2 17.0 %collective-permute-start.7 = (bf16[576,768]{1,0:T(8,128)(2,1)S(1)}, bf16[576,768]{1,0:T(8,128)(2,1)S(1)}, u32[]{:S(2)}, u32[]{:S(2)}) collective-permute-start(bf16[576,768]{1,0:T(8,128)(2,1)S(1)} %pad_maximum_fusion), channel_id=1, source_target_pairs={{0,4},{1,3},{2,6},{3,1},{4,0},{5,7},{6,2},{7,5},{8,12},{9,11},{10,... | collective-permute-start | bytes 2654216 | tf_op jit(solution)/shard_map/ppermute | solution.py:641
  41.8 8.5 %collective-permute-start.16 = (bf16[288,768]{1,0:T(8,128)(2,1)S(1)}, bf16[288,768]{1,0:T(8,128)(2,1)S(1)}, u32[]{:S(2)}, u32[]{:S(2)}) collective-permute-start(bf16[288,768]{1,0:T(8,128)(2,1)S(1)} %constant_dynamic-update-slice_fusion.8.z0), channel_id=1, source_target_pairs={{0,2},{1,5},{2,0},{3,7},{4,6},{5,1},{6,4},{7,3},{8,10},{9,13},{10,... | collective-permute-start | bytes 1327112 | tf_op jit(solution)/shard_map/ppermute | solution.py:637
  42.3 11.0 %collective-permute-start.18 = (bf16[96,768]{1,0:T(8,128)(2,1)S(1)}, bf16[96,768]{1,0:T(8,128)(2,1)S(1)}, u32[]{:S(2)}, u32[]{:S(2)}) collective-permute-start(bf16[96,768]{1,0:T(8,128)(2,1)S(1)} %get-tuple-element.103), channel_id=1, source_target_pairs={{0,16},{2,18},{4,20},{6,22},{8,24},{10,26},{12,28},{14,30},{16,0},... | collective-permute-start | bytes 442376 | tf_op jit(solution)/shard_map/ppermute | solution.py:645
  51.3 13.6 %collective-permute-start.17 = (bf16[576,768]{1,0:T(8,128)(2,1)}, bf16[576,768]{1,0:T(8,128)(2,1)}, u32[]{:S(2)}, u32[]{:S(2)}) collective-permute-start(bf16[576,768]{1,0:T(8,128)(2,1)} %pad_maximum_fusion.1), channel_id=1, source_target_pairs={{0,4},{1,3},{2,6},{3,1},{4,0},{5,7},{6,2},{7,5},{8,12},{9,11},{10,... | collective-permute-start | bytes 2654216 | tf_op jit(solution)/shard_map/ppermute | solution.py:641
  52.7 13.5 %collective-permute-start.11 = (bf16[576,768]{1,0:T(8,128)(2,1)S(1)}, bf16[576,768]{1,0:T(8,128)(2,1)}, u32[]{:S(2)}, u32[]{:S(2)}) collective-permute-start(bf16[576,768]{1,0:T(8,128)(2,1)S(1)} %collective-permute-done.7.z2), channel_id=1, source_target_pairs={{0,1},{1,0},{2,3},{3,2},{4,5},{5,4},{6,7},{7,6},{8,9},{9,8},{10,11... | collective-permute-start | bytes 2654216 | tf_op jit(solution)/shard_map/ppermute | solution.py:633
  53.9 9.0 %collective-permute-start.19 = (bf16[192,768]{1,0:T(8,128)(2,1)S(1)}, bf16[192,768]{1,0:T(8,128)(2,1)}, u32[]{:S(2)}, u32[]{:S(2)}) collective-permute-start(bf16[192,768]{1,0:T(8,128)(2,1)S(1)} %pad_maximum_fusion.5), channel_id=1, source_target_pairs={{0,8},{2,10},{4,12},{6,14},{8,0},{10,2},{12,4},{14,6},{16,24},{18,... | collective-permute-start | bytes 884744 | tf_op jit(solution)/shard_map/ppermute | solution.py:645
  57.2 9.1 %collective-permute-start.8 = (bf16[384,768]{1,0:T(8,128)(2,1)S(1)}, bf16[384,768]{1,0:T(8,128)(2,1)}, u32[]{:S(2)}, u32[]{:S(2)}) collective-permute-start(bf16[384,768]{1,0:T(8,128)(2,1)S(1)} %get-tuple-element.89.so), channel_id=1, source_target_pairs={{0,1},{1,0},{2,3},{3,2},{4,5},{5,4},{6,7},{7,6},{8,9},{9,8},{10,11... | collective-permute-start | bytes 1769480 | tf_op jit(solution)/shard_map/ppermute | solution.py:633
  57.9 8.3 %collective-permute-start.9 = (bf16[288,768]{1,0:T(8,128)(2,1)S(1)}, bf16[288,768]{1,0:T(8,128)(2,1)}, u32[]{:S(2)}, u32[]{:S(2)}) collective-permute-start(bf16[288,768]{1,0:T(8,128)(2,1)S(1)} %constant_dynamic-update-slice_fusion.5.z0), channel_id=1, source_target_pairs={{0,1},{1,0},{2,3},{3,2},{4,5},{5,4},{6,7},{7,6},{8,9},{9,8},{10,11... | collective-permute-start | bytes 1327112 | tf_op jit(solution)/shard_map/ppermute | solution.py:633
  64.9 9.5 %collective-permute-start.20 = (bf16[288,768]{1,0:T(8,128)(2,1)S(1)}, bf16[288,768]{1,0:T(8,128)(2,1)S(1)}, u32[]{:S(2)}, u32[]{:S(2)}) collective-permute-start(bf16[288,768]{1,0:T(8,128)(2,1)S(1)} %constant_dynamic-update-slice_fusion.10.z0.w0), channel_id=1, source_target_pairs={{0,2},{1,5},{2,0},{3,7},{4,6},{5,1},{6,4},{7,3},{8,10},{9,13},{10,... | collective-permute-start | bytes 1327112 | tf_op jit(solution)/shard_map/ppermute | solution.py:637
  74.5 13.1 %collective-permute-start.21 = (bf16[576,768]{1,0:T(8,128)(2,1)S(1)}, bf16[576,768]{1,0:T(8,128)(2,1)S(1)}, u32[]{:S(2)}, u32[]{:S(2)}) collective-permute-start(bf16[576,768]{1,0:T(8,128)(2,1)S(1)} %pad_maximum_fusion.2), channel_id=1, source_target_pairs={{0,4},{1,3},{2,6},{3,1},{4,0},{5,7},{6,2},{7,5},{8,12},{9,11},{10,... | collective-permute-start | bytes 2654216 | tf_op jit(solution)/shard_map/ppermute | solution.py:641
  96.0 16.3 %collective-permute-start.24 = (bf16[768,768]{1,0:T(8,128)(2,1)S(1)}, bf16[768,768]{1,0:T(8,128)(2,1)S(1)}, u32[]{:S(2)}, u32[]{:S(2)}) collective-permute-start(bf16[768,768]{1,0:T(8,128)(2,1)S(1)} %grad_down_away.1), channel_id=1, source_target_pairs={{0,4},{1,3},{2,6},{3,1},{4,0},{5,7},{6,2},{7,5},{8,12},{9,11},{10,... | collective-permute-start | bytes 3538952 | tf_op jit(solution)/shard_map/ppermute | solution.py:641
  103.0 9.4 %collective-permute-start.25 = (f32[256,768]{1,0:T(8,128)S(1)}, f32[256,768]{1,0:T(8,128)S(1)}, u32[]{:S(2)}, u32[]{:S(2)}) collective-permute-start(f32[256,768]{1,0:T(8,128)S(1)} %get-tuple-element.118), channel_id=1, source_target_pairs={{0,1},{1,0},{2,3},{3,2},{4,5},{5,4},{6,7},{7,6},{8,9},{9,8},{10,11... | collective-permute-start | bytes 2359304 | tf_op jit(solution)/shard_map/ppermute | solution.py:633
  103.1 23.9 %collective-permute-start.30 = (bf16[768,768]{1,0:T(8,128)(2,1)S(1)}, bf16[768,768]{1,0:T(8,128)(2,1)S(1)}, u32[]{:S(2)}, u32[]{:S(2)}) collective-permute-start(bf16[768,768]{1,0:T(8,128)(2,1)S(1)} %get-tuple-element.133), channel_id=1, source_target_pairs={{0,4},{1,3},{2,6},{3,1},{4,0},{5,7},{6,2},{7,5},{8,12},{9,11},{10,... | collective-permute-start | bytes 3538952 | tf_op jit(solution)/shard_map/ppermute | solution.py:641
  120.6 12.2 %collective-permute-start.32 = (bf16[384,768]{1,0:T(8,128)(2,1)S(1)}, bf16[384,768]{1,0:T(8,128)(2,1)S(1)}, u32[]{:S(2)}, u32[]{:S(2)}) collective-permute-start(bf16[384,768]{1,0:T(8,128)(2,1)S(1)} %add_convert_fusion.2), channel_id=1, source_target_pairs={{0,2},{1,5},{2,0},{3,7},{4,6},{5,1},{6,4},{7,3},{8,10},{9,13},{10,... | collective-permute-start | bytes 1769480 | tf_op jit(solution)/shard_map/ppermute | solution.py:637
  125.9 24.2 %collective-permute-start.28 = (bf16[768,768]{1,0:T(8,128)(2,1)S(1)}, bf16[768,768]{1,0:T(8,128)(2,1)S(1)}, u32[]{:S(2)}, u32[]{:S(2)}) collective-permute-start(bf16[768,768]{1,0:T(8,128)(2,1)S(1)} %get-tuple-element.129), channel_id=1, source_target_pairs={{0,4},{1,3},{2,6},{3,1},{4,0},{5,7},{6,2},{7,5},{8,12},{9,11},{10,... | collective-permute-start | bytes 3538952 | tf_op jit(solution)/shard_map/ppermute | solution.py:641
  127.2 24.5 %collective-permute-start.31 = (bf16[384,768]{1,0:T(8,128)(2,1)S(1)}, bf16[384,768]{1,0:T(8,128)(2,1)S(1)}, u32[]{:S(2)}, u32[]{:S(2)}) collective-permute-start(bf16[384,768]{1,0:T(8,128)(2,1)S(1)} %add_convert_fusion), channel_id=1, source_target_pairs={{0,2},{1,5},{2,0},{3,7},{4,6},{5,1},{6,4},{7,3},{8,10},{9,13},{10,... | collective-permute-start | bytes 1769480 | tf_op jit(solution)/shard_map/ppermute | solution.py:637
  133.0 18.8 %collective-permute-start.33 = (bf16[96,768]{1,0:T(8,128)(2,1)S(1)}, bf16[96,768]{1,0:T(8,128)(2,1)S(1)}, u32[]{:S(2)}, u32[]{:S(2)}) collective-permute-start(bf16[96,768]{1,0:T(8,128)(2,1)S(1)} %get-tuple-element.180), channel_id=1, source_target_pairs={{0,16},{2,18},{4,20},{6,22},{8,24},{10,26},{12,28},{14,30},{16,0},... | collective-permute-start | bytes 442376 | tf_op jit(solution)/shard_map/ppermute | solution.py:645
  135.3 16.5 %collective-permute-start.34 = (bf16[96,768]{1,0:T(8,128)(2,1)S(1)}, bf16[96,768]{1,0:T(8,128)(2,1)S(1)}, u32[]{:S(2)}, u32[]{:S(2)}) collective-permute-start(bf16[96,768]{1,0:T(8,128)(2,1)S(1)} %get-tuple-element.179), channel_id=1, source_target_pairs={{0,8},{2,10},{4,12},{6,14},{8,0},{10,2},{12,4},{14,6},{16,24},{18,... | collective-permute-start | bytes 442376 | tf_op jit(solution)/shard_map/ppermute | solution.py:645
  136.6 15.2 %collective-permute-start.35 = (bf16[96,768]{1,0:T(8,128)(2,1)S(1)}, bf16[96,768]{1,0:T(8,128)(2,1)S(1)}, u32[]{:S(2)}, u32[]{:S(2)}) collective-permute-start(bf16[96,768]{1,0:T(8,128)(2,1)S(1)} %get-tuple-element.178), channel_id=1, source_target_pairs={{0,24},{2,26},{4,28},{6,30},{8,16},{10,18},{12,20},{14,22},{16,8},... | collective-permute-start | bytes 442376 | tf_op jit(solution)/shard_map/ppermute | solution.py:645
  150.3 9.9 %collective-permute-start.29 = (bf16[384,768]{1,0:T(8,128)(2,1)S(1)}, bf16[384,768]{1,0:T(8,128)(2,1)S(1)}, u32[]{:S(2)}, u32[]{:S(2)}) collective-permute-start(bf16[384,768]{1,0:T(8,128)(2,1)S(1)} %add_convert_fusion.1), channel_id=1, source_target_pairs={{0,2},{1,5},{2,0},{3,7},{4,6},{5,1},{6,4},{7,3},{8,10},{9,13},{10,... | collective-permute-start | bytes 1769480 | tf_op jit(solution)/shard_map/ppermute | solution.py:637
  151.9 12.9 %collective-permute-start.36 = (bf16[96,768]{1,0:T(8,128)(2,1)S(1)}, bf16[96,768]{1,0:T(8,128)(2,1)S(1)}, u32[]{:S(2)}, u32[]{:S(2)}) collective-permute-start(bf16[96,768]{1,0:T(8,128)(2,1)S(1)} %get-tuple-element.177), channel_id=1, source_target_pairs={{0,16},{2,18},{4,20},{6,22},{8,24},{10,26},{12,28},{14,30},{16,0},... | collective-permute-start | bytes 442376 | tf_op jit(solution)/shard_map/ppermute | solution.py:645
  154.0 10.8 %collective-permute-start.37 = (bf16[96,768]{1,0:T(8,128)(2,1)S(1)}, bf16[96,768]{1,0:T(8,128)(2,1)S(1)}, u32[]{:S(2)}, u32[]{:S(2)}) collective-permute-start(bf16[96,768]{1,0:T(8,128)(2,1)S(1)} %get-tuple-element.176), channel_id=1, source_target_pairs={{0,8},{2,10},{4,12},{6,14},{8,0},{10,2},{12,4},{14,6},{16,24},{18,... | collective-permute-start | bytes 442376 | tf_op jit(solution)/shard_map/ppermute | solution.py:645
  155.2 9.6 %collective-permute-start.38 = (bf16[96,768]{1,0:T(8,128)(2,1)S(1)}, bf16[96,768]{1,0:T(8,128)(2,1)S(1)}, u32[]{:S(2)}, u32[]{:S(2)}) collective-permute-start(bf16[96,768]{1,0:T(8,128)(2,1)S(1)} %get-tuple-element.175), channel_id=1, source_target_pairs={{0,24},{2,26},{4,28},{6,30},{8,16},{10,18},{12,20},{14,22},{16,8},... | collective-permute-start | bytes 442376 | tf_op jit(solution)/shard_map/ppermute | solution.py:645
  164.8 15.0 %collective-permute-start.39 = (bf16[96,768]{1,0:T(8,128)(2,1)S(1)}, bf16[96,768]{1,0:T(8,128)(2,1)S(1)}, u32[]{:S(2)}, u32[]{:S(2)}) collective-permute-start(bf16[96,768]{1,0:T(8,128)(2,1)S(1)} %get-tuple-element.174), channel_id=1, source_target_pairs={{0,16},{2,18},{4,20},{6,22},{8,24},{10,26},{12,28},{14,30},{16,0},... | collective-permute-start | bytes 442376 | tf_op jit(solution)/shard_map/ppermute | solution.py:645
  169.3 11.4 %collective-permute-start.40 = (bf16[96,768]{1,0:T(8,128)(2,1)S(1)}, bf16[96,768]{1,0:T(8,128)(2,1)S(1)}, u32[]{:S(2)}, u32[]{:S(2)}) collective-permute-start(bf16[96,768]{1,0:T(8,128)(2,1)S(1)} %get-tuple-element.173), channel_id=1, source_target_pairs={{0,8},{2,10},{4,12},{6,14},{8,0},{10,2},{12,4},{14,6},{16,24},{18,... | collective-permute-start | bytes 442376 | tf_op jit(solution)/shard_map/ppermute | solution.py:645
  169.3 11.4 %collective-permute-start.41 = (bf16[96,768]{1,0:T(8,128)(2,1)S(1)}, bf16[96,768]{1,0:T(8,128)(2,1)S(1)}, u32[]{:S(2)}, u32[]{:S(2)}) collective-permute-start(bf16[96,768]{1,0:T(8,128)(2,1)S(1)} %get-tuple-element.172), channel_id=1, source_target_pairs={{0,24},{2,26},{4,28},{6,30},{8,16},{10,18},{12,20},{14,22},{16,8},... | collective-permute-start | bytes 442376 | tf_op jit(solution)/shard_map/ppermute | solution.py:645
  (44 other events, 485.4 us)

commit v3 on v2

--- a/solution.py
+++ b/solution.py
@@ -238,13 +238,28 @@
 BF = jnp.bfloat16
 F32 = jnp.float32
 AXES = ("dp", "fsdp")
-COST = 1.0e9
+COST = 1000000000.0
 MICROS = {
-    "pack_weights": 1.0, "sort_near": 1.0, "attend_forward": 6.5, "attend_close": 3.6, "feed_up": 2.5,
-    "feed_down": 1.5, "finish_forward": 2.0, "grad_down_away": 0.8, "grad_down_here": 0.8,
-    "grad_up": 4.0, "attend_backward": 7.0, "grad_mix": 3.0, "grad_input": 4.0, "close_sums": 0.5,
-    "update": 2.3,
+    "sort_near": 0.1,
+    "attend_forward": 0.65,
+    "attend_close": 0.36,
+    "feed_up": 0.25,
+    "feed_down": 0.15,
+    "finish_forward": 0.0,
+    "grad_down_away": 0.0,
+    "grad_down_here": 0.0,
+    "grad_up": 0.0,
+    "attend_backward": 0.0,
+    "grad_input": 0.0,
+    "close_sums": 0.0,
+    "update": 0.0,
+    "grad_up_away": 0.0,
+    "grad_up_here": 1.0,
+    "feed_back": 0.0,
+    "mix_away": 0.0,
+    "mix_here": 2.0,
 }
+MB = 16
 CHIPS = 16
 BLOCK = 96
 QKV = 72
@@ -279,9 +294,7 @@
 
 
 PLACES = block_places()
-PIECES = [
-    (0, PLANE), (PLANE, ZROWS), (PLANE + ZROWS, ZROWS), (PLANE + 2 * ZROWS, 2 * ZROWS)
-]
+PIECES = [(0, PLANE)] + [(PLANE + ZROWS * p, ZROWS) for p in range(4)]
 
 
 def shard_index(chip, core, plane, step, other):
@@ -291,11 +304,10 @@
     return 2 * (chip ^ mask ^ step) + owner
 
 
-def call(body, outs, args, scratch=(), smem=0, mb=6, place=pltpu.VMEM):
-    held = [math.prod(a.shape) * a.dtype.itemsize for a in args[smem:]]
-    held += [math.prod(s) * jnp.dtype(t).itemsize for s, t in outs]
-    held += [math.prod(s.shape) * 4 for s in scratch]
-    limit = sum(held) + (mb << 20)
+def call(body, outs, args, scratch=(), smem=0, place=pltpu.VMEM, name=None):
+    name = name or body.__name__
+    held = [math.prod(s.shape) * 4 for s in scratch]
+    limit = int(sum(held) + (MB << 20))
     in_specs = [
         pl.BlockSpec(memory_space=pltpu.SMEM if i < smem else place)
         for i in range(len(args))
@@ -308,15 +320,15 @@
         scratch_shapes=list(scratch),
         compiler_params=pltpu.CompilerParams(vmem_limit_bytes=limit),
         cost_estimate=pl.CostEstimate(
-            flops=int(MICROS[body.__name__] * COST), bytes_accessed=0, transcendentals=0
+            flops=int(MICROS[name] * COST), bytes_accessed=0, transcendentals=0
         ),
-        name=body.__name__,
+        name=name,
     )(*args)
 
 
-def sort_near(s0, s1, s23, *groups):
+def sort_near(s0, s1, s2, s3, *groups):
     for g, out in enumerate(groups):
-        for p, (ref, base) in enumerate(((s0, 0), (s1, 0), (s23, 0), (s23, 3 * BLOCK))):
+        for p, (ref, base) in enumerate(((s0, 0), (s1, 0), (s2, 0), (s3, 0))):
             at = base + BLOCK * g
             out[BLOCK * p : BLOCK * p + BLOCK, :] = ref[at : at + BLOCK, :]
 
@@ -350,14 +362,14 @@
 
 
 def attend_forward(
-    lengths, me, x_ref, so, z0, z1, z2, sp, y0, y1, y2,
+    lengths, me, x_ref, so, z0, z1, z2, z3, sp, y0, y1, y2, y3,
     mix, att, den, rel_own, rel_par,
 ):
     rows = x_ref.shape[0]
     width = x_ref.shape[1]
     chip, core = me[0], me[1]
     x = x_ref[...]
-    sides = ((False, (so, z0, z1, z2), rel_own), (True, (sp, y0, y1, y2), rel_par))
+    sides = ((False, (so, z0, z1, z2, z3), rel_own), (True, (sp, y0, y1, y2, y3), rel_par))
     for other, refs, _ in sides:
         for (base, size), ref in zip(PIECES, refs):
             got = nt(ref[...], x)
@@ -387,11 +399,11 @@
 
 
 def attend_close(
-    x_ref, rel_own, rel_par, so, z0, z1, z2, sp, y0, y1, y2, norms,
+    x_ref, rel_own, rel_par, so, z0, z1, z2, z3, sp, y0, y1, y2, y3, norms,
     first, first_low, xhat, rstd,
 ):
     branch = x_ref[...].astype(F32)
-    for refs, rel in (((so, z0, z1, z2), rel_own), ((sp, y0, y1, y2), rel_par)):
+    for refs, rel in (((so, z0, z1, z2, z3), rel_own), ((sp, y0, y1, y2, y3), rel_par)):
         for (base, size), ref in zip(PIECES, refs):
             branch = branch + tn(rel[base : base + size, :], ref[...])
     centered = branch - jnp.mean(branch, axis=-1, keepdims=True)
@@ -409,11 +421,11 @@
 GELU_B = 0.044715
 
 
-def feed_up(ya, yb, s, z0, z1, z2, hid, slope):
+def feed_up(ya, yb, s, z0, z1, z2, z3, hid, slope):
     rows = ya.shape[0]
     for half, y in ((0, ya), (1, yb)):
         cols = slice(half * rows, half * rows + rows)
-        for (base, size), ref in zip(PIECES, (s, z0, z1, z2)):
+        for (base, size), ref in zip(PIECES, (s, z0, z1, z2, z3)):
             u = nt(ref[...], y[...])
             sq = u * u
             t = jnp.tanh(GELU_A * u * (1.0 + GELU_B * sq))
@@ -424,8 +436,8 @@
             )
 
 
-def feed_down(hid, s, z0, z1, z2, own, other, whole):
-    for (base, size), ref in zip(PIECES, (s, z0, z1, z2)):
+def feed_down(hid, s, z0, z1, z2, z3, own, other, whole):
+    for (base, size), ref in zip(PIECES, (s, z0, z1, z2, z3)):
         whole[base : base + size, :] = ref[...]
     rows = own.shape[0]
     w = whole[...]
@@ -462,65 +474,56 @@
     terms[1:2, :] = jnp.sum(dy, axis=0, keepdims=True)
 
 
-def spread_rows(get, send, turn, own):
-    goals = ((own, 0), (turn, 0), (send, 0), (send, PLANE))
-    for base, size in PIECES:
-        g = get(base, size)
-        for at, plane, step in PLACES:
-            if base <= at < base + size:
-                ref, off = goals[plane]
-                to = off + BLOCK * ((0,) + STEPS_Z).index(step)
-                ref[to : to + BLOCK, :] = g[at - base : at - base + BLOCK].astype(ref.dtype)
-
-
-def hidden_grad(hid, za, zb, here):
-    rows = za.shape[0]
-    return nn(hid[here, 0:rows], za[...]) + nn(hid[here, rows : 2 * rows], zb[...])
-
-
-def grad_down_away(hid, za, zb, send):
-    near = hidden_grad(hid, za, zb, slice(2 * BLOCK, PLANE)).astype(BF)
-    far = hidden_grad(hid, za, zb, slice(PLANE + 2 * ZROWS, HALF)).astype(BF)
+def rows_away(get, send):
+    near = get(slice(2 * BLOCK, PLANE)).astype(BF)
+    far = get(slice(PLANE + 2 * ZROWS, HALF)).astype(BF)
     for p in range(2):
         send[PLANE * p : PLANE * p + BLOCK, :] = near[BLOCK * p : BLOCK * p + BLOCK]
         send[PLANE * p + BLOCK : PLANE * p + PLANE, :] = far[ZROWS * p : ZROWS * p + ZROWS]
 
 
-def grad_down_here(hid, za, zb, turn, own):
-    near = hidden_grad(hid, za, zb, slice(0, 2 * BLOCK))
-    far = hidden_grad(hid, za, zb, slice(PLANE, PLANE + 2 * ZROWS))
+def rows_here(get, turn, own):
+    near = get(slice(0, 2 * BLOCK))
+    far = get(slice(PLANE, PLANE + 2 * ZROWS))
     for p, ref in enumerate((own, turn)):
         ref[0:BLOCK, :] = near[BLOCK * p : BLOCK * p + BLOCK]
         ref[BLOCK:PLANE, :] = far[ZROWS * p : ZROWS * p + ZROWS]
 
 
-def grad_up(
-    slope, za, zb, ya, yb, d, w0, w1, w2, s, z0, z1, z2,
-    send, turn, own, mine, other, dup, whole,
+def two_cores(hid, za, zb):
+    rows = za.shape[0]
+    return lambda here: nn(hid[here, 0:rows], za[...]) + nn(
+        hid[here, rows : 2 * rows], zb[...]
+    )
+
+
+def grad_away(hid, za, zb, send):
+    rows_away(two_cores(hid, za, zb), send)
+
+
+def grad_here(hid, za, zb, turn, own):
+    rows_here(two_cores(hid, za, zb), turn, own)
+
+
+def feed_back(
+    slope, za, zb, d, w0, w1, w2, w3, s, z0, z1, z2, z3, dup, mine, other, whole,
 ):
     rows = za.shape[0]
-    for (base, size), ref in zip(PIECES, (d, w0, w1, w2)):
+    for (base, size), ref in zip(PIECES, (d, w0, w1, w2, w3)):
         here = slice(base, base + size)
         w = ref[...]
         dup[here, 0:rows] = (nt(w, za[...]) * slope[here, 0:rows]).astype(BF)
         dup[here, rows:] = (nt(w, zb[...]) * slope[here, rows:]).astype(BF)
-    for (base, size), ref in zip(PIECES, (s, z0, z1, z2)):
+    for (base, size), ref in zip(PIECES, (s, z0, z1, z2, z3)):
         whole[base : base + size, :] = ref[...]
-
-    def get(base, size):
-        return nn(dup[base : base + size, 0:rows], ya[...]) + nn(
-            dup[base : base + size, rows : 2 * rows], yb[...]
-        )
-
-    spread_rows(get, send, turn, own)
     w = whole[...]
+    other[...] = tn(dup[:, rows : 2 * rows], w)
     mine[...] = tn(dup[:, 0:rows], w)
-    other[...] = tn(dup[:, rows : 2 * rows], w)
 
 
 def attend_backward(
     lengths, me, ds2, mine, got, xhat, rstd, norms, mix, att, den,
-    so, z0, z1, z2, sp, y0, y1, y2,
+    so, z0, z1, z2, z3, sp, y0, y1, y2, y3,
     dh_ref, do_ref, terms, rel_own, rel_par, datt, dmix,
 ):
     rows, width = ds2.shape
@@ -534,7 +537,7 @@
     do = dh.astype(BF)
     do_ref[...] = do
     side = QKV // 3
-    sides = ((False, (so, z0, z1, z2), rel_own), (True, (sp, y0, y1, y2), rel_par))
+    sides = ((False, (so, z0, z1, z2, z3), rel_own), (True, (sp, y0, y1, y2, y3), rel_par))
     for other, refs, _ in sides:
         for (base, size), ref in zip(PIECES, refs):
             got_t = nt(ref[...], do)
@@ -570,19 +573,23 @@
             rel[at : at + BLOCK, :] = jnp.concatenate([part, blank], axis=0).astype(BF)
 
 
-def grad_mix(dma, dmb, xa, xb, ata, atb, doa, dob, send, turn, own):
-    def get(base, size):
-        here = slice(base, base + size)
-        return (nn(dma[here, :], xa[...]) + nn(dmb[here, :], xb[...])) + (
-            nn(ata[here, :], doa[...]) + nn(atb[here, :], dob[...])
-        )
-
-    spread_rows(get, send, turn, own)
-
-
-def grad_input(dh, rel_own, rel_par, so, z0, z1, z2, sp, y0, y1, y2, out):
+def four_terms(dma, dmb, xa, xb, ata, atb, doa, dob):
+    return lambda here: (nn(dma[here, :], xa[...]) + nn(dmb[here, :], xb[...])) + (
+        nn(ata[here, :], doa[...]) + nn(atb[here, :], dob[...])
+    )
+
+
+def mix_away(dma, dmb, xa, xb, ata, atb, doa, dob, send):
+    rows_away(four_terms(dma, dmb, xa, xb, ata, atb, doa, dob), send)
+
+
+def mix_here(dma, dmb, xa, xb, ata, atb, doa, dob, turn, own):
+    rows_here(four_terms(dma, dmb, xa, xb, ata, atb, doa, dob), turn, own)
+
+
+def grad_input(dh, rel_own, rel_par, so, z0, z1, z2, z3, sp, y0, y1, y2, y3, out):
     total = dh[...]
-    for refs, rel in (((so, z0, z1, z2), rel_own), ((sp, y0, y1, y2), rel_par)):
+    for refs, rel in (((so, z0, z1, z2, z3), rel_own), ((sp, y0, y1, y2, y3), rel_par)):
         for (base, size), ref in zip(PIECES, refs):
             total = total + tn(rel[base : base + size, :], ref[...])
     out[...] = total
@@ -677,25 +684,37 @@
         down_weight.astype(BF),
     ]
     s_all = jnp.concatenate(blocks, axis=0)
-    near1 = [hop_z(blocks[0], step) for step in STEPS_Z]
+    def wide_join(*parts):
+        return jnp.concatenate(parts, axis=0)
+
+    def z_round(block, direct, before):
+        if direct:
+            got = [hop_z(tie(block, *before), step) for step in STEPS_Z]
+            return got, wide_join(*got)
+        far = hop_z(tie(block, *before), 8)
+        near = hop_z(wide_join(block, far), 4)
+        return [far, near], wide_join(far, near)
+
     s_first = hop_first(s_all)
-    s_far = hop_second(jnp.concatenate([s_all, s_first], axis=0))
-    joined1 = jnp.concatenate(near1, axis=0)
+    s_second = hop_second(s_all)
+    near1, joined1 = z_round(blocks[0], True, ())
+    near2, joined2 = z_round(blocks[1], False, (near1[0],))
+    near3, joined3 = z_round(blocks[2], False, (near2[0],))
+    s_third = hop_second(s_first)
+    s_parts = (s_all, s_first, s_second, s_third)
     turned1 = hop_first(tie(joined1, s_first))
-    far1 = hop_second(jnp.concatenate([tie(joined1, s_far), turned1], axis=0))
-    got2 = hop_z(tie(blocks[1], *near1), 8)
-    joined2 = jnp.concatenate(
-        [got2, hop_z(jnp.concatenate([blocks[1], got2], axis=0), 4)], axis=0
-    )
+    across1 = hop_second(tie(joined1, s_second))
+    corner1 = hop_second(tie(turned1, s_third))
     turned2 = hop_first(tie(joined2, turned1))
-    far2 = hop_second(jnp.concatenate([tie(joined2, far1), turned2], axis=0))
+    across2 = hop_second(tie(joined2, across1))
+    corner2 = hop_second(tie(turned2, corner1))
     sorted1, sorted2, sorted3 = call(
         sort_near,
         [((PLANE, width), BF)] * 3,
-        (s_all, s_first, s_far),
-    )
-    up_all = (sorted2, joined2, turned2, far2)
-    attn_own = (sorted1, joined1, turned1, far1)
+        s_parts,
+    )
+    up_all = (sorted2, joined2, turned2, across2, corner2)
+    attn_own = (sorted1, joined1, turned1, across1, corner1)
     attn_par = tuple(swap(p) for p in attn_own)
     x_par = swap(tokens)
 
@@ -708,18 +727,15 @@
         (lengths, me, tie(tokens, x_par)) + attn_own + attn_par,
         smem=2,
     )
-    got3 = hop_z(tie(blocks[2], got2), 8)
-    joined3 = jnp.concatenate(
-        [got3, hop_z(jnp.concatenate([blocks[2], tie(got3, joined2)], axis=0), 4)], axis=0
-    )
     turned3 = hop_first(tie(joined3, turned2))
+    across3 = hop_second(tie(joined3, across2))
     first, first_low, xhat, rstd = call(
         attend_close,
         [((rows, width), F32), ((rows, width), BF), ((rows, width), F32), ((rows, 1), F32)],
         (tokens, at_own, at_par) + attn_own + attn_par + (norm_params,),
     )
-    far3 = hop_second(jnp.concatenate([tie(joined3, far2), turned3], axis=0))
-    down_all = (sorted3, joined3, turned3, far3)
+    corner3 = hop_second(tie(turned3, corner2))
+    down_all = (sorted3, joined3, turned3, across3, corner3)
     at_got = swap(at_par)
     first_par = swap(first_low)
     hid, slope = call(
@@ -740,19 +756,17 @@
         smem=1,
     )
     dz_par = swap(dz)
-    spread_shapes = [((2 * PLANE, width), BF), ((PLANE, width), F32), ((PLANE, width), F32)]
-    (send3,) = call(grad_down_away, spread_shapes[:1], (hid, dz, dz_par))
-    hid_later = tie(hid, send3)
-    turn3, own3 = call(grad_down_here, spread_shapes[1:], (hid_later, dz, dz_par))
+    away = [((2 * PLANE, width), BF)]
+    stay = [((PLANE, width), F32)] * 2
+    (send3,) = call(grad_away, away, (hid, dz, dz_par), name="grad_down_away")
     got3 = hop_second(send3)
-    send2, turn2, own2, dy_own, dy_par = call(
-        grad_up,
-        spread_shapes + [((rows, width), F32)] * 2,
-        (tie(slope, turn3), dz, dz_par, first_low, first_par) + down_all + up_all,
-        scratch=[pltpu.VMEM((HALF, 2 * rows), BF), pltpu.VMEM((HALF, width), BF)],
-    )
-    low_turn3 = add_first(turn3, got3)
-    back3 = hop_first(low_turn3)
+    dup, dy_own, dy_par = call(
+        feed_back,
+        [((HALF, 2 * rows), BF)] + [((rows, width), F32)] * 2,
+        (slope, tie(dz, send3), dz_par) + down_all + up_all,
+        scratch=[pltpu.VMEM((HALF, width), BF)],
+    )
+    (send2,) = call(grad_away, away, (dup, first_low, first_par), name="grad_up_away")
     got2 = hop_second(send2)
     dh, do, terms_one, dm_own, dm_par = call(
         attend_backward,
@@ -760,30 +774,42 @@
             ((rows, width), F32), ((rows, width), BF), ((2, width), F32),
             ((HALF, rows), BF), ((HALF, rows), BF),
         ],
-        (lengths, me, tie(ds2, low_turn3), dy_own, swap(dy_par), xhat, rstd, norm_params, mix, att, den)
-        + attn_own + attn_par,
+        (
+            lengths, me, ds2, dy_own, swap(dy_par), xhat, rstd,
+            norm_params, mix, att, den,
+        ) + attn_own + attn_par,
         scratch=[pltpu.VMEM((width, rows), F32), pltpu.VMEM((wide, rows), F32)],
         smem=2,
     )
-    send1, turn1, own1 = call(
-        grad_mix,
-        spread_shapes,
-        (dm_own, swap(dm_par), tokens, x_par, at_own, at_got, do, swap(do)),
-    )
+    turn3, own3 = call(
+        grad_here, stay, (hid, dz, dz_par), name="grad_down_here"
+    )
+    turn2, own2 = call(
+        grad_here, stay, (dup, first_low, first_par),
+        name="grad_up_here",
+    )
+    low_turn3 = add_first(turn3, got3)
+    back3 = hop_first(low_turn3)
+    back2 = hop_first(add_first(turn2, got2))
+    factors = (
+        dm_own, swap(dm_par), tokens, x_par, at_own, at_got,
+        do, swap(do),
+    )
+    (send1,) = call(mix_away, away, factors)
+    got1 = hop_second(tie(send1, back3))
+    turn1, own1 = call(mix_here, stay, (tie(dm_own, send1),) + factors[1:])
     (grad_tokens,) = call(
         grad_input,
         [((rows, width), F32)],
-        (dh, dm_own, dm_par) + attn_own + attn_par,
+        (tie(dh, send1), dm_own, dm_par) + attn_own + attn_par,
     )
     keep3, low3 = add_second(own3, got3, back3)
     parts3 = send_z(low3)
-    back2 = hop_first(add_first(turn2, got2))
-    got1 = hop_second(send1)
     keep2, low2 = add_second(own2, got2, back2)
-    parts2 = send_z(tie(low2, *parts3))
+    parts2 = send_z(tie(low2, parts3[1]))
     back1 = hop_first(add_first(tie(turn1, grad_tokens), got1))
     keep1, low1 = add_second(own1, got1, back1)
-    parts1 = send_z(tie(low1, *parts2))
+    parts1 = send_z(tie(low1, parts2[1]))
     g3 = (keep3 + parts3[0]) + (parts3[1].astype(F32) + parts3[2].astype(F32))
     g2 = (keep2 + parts2[0]) + (parts2[1].astype(F32) + parts2[2].astype(F32))
     g1, note = call(

time: 200 us -> 191 us (0.955)
  waiting for transfers between devices: 86.3 us -> 79.8 us
  Pallas kernels: 42.4 us -> 39 us
  starting transfers between devices: 58.3 us -> 60.9 us
    ppermute x7 -> x11, waiting for transfers between devices: 28.7 us -> 14.1 us  [hop_second(): lax.ppermute(value, AXES, [(i, i ^ (2 if i % 2 else 4)) for i in range(2...]
    ppermute x22, waiting for transfers between devices: 36.7 us -> 41.2 us  [hop_z(): return lax.ppermute(value, 'dp', [(i, i ^ step) for i in range(CHIPS)])]
    ppermute x7 -> x11, starting transfers between devices: 9.52 us -> 13.6 us  [hop_second(): lax.ppermute(value, AXES, [(i, i ^ (2 if i % 2 else 4)) for i in range(2...]
    ppermute x22, starting transfers between devices: 37.3 us -> 33.4 us  [hop_z(): return lax.ppermute(value, 'dp', [(i, i ^ step) for i in range(CHIPS)])]
    pallas_call x14 -> x17, Pallas kernels: 42.4 us -> 39 us  [call(): pl.pallas_call(body, out_shape=[jax.ShapeDtypeStruct(s, t) for s, t in ou...]
    ppermute x7, waiting for transfers between devices: 13.1 us -> 16.2 us  [hop_first(): lax.ppermute(value, AXES, [(i, i ^ (4 if i % 2 else 2)) for i in range(2...]
    unnamed x4 -> x0, other arithmetic: 2.9 us -> none
    convert_element_type x0 -> x4, other arithmetic: none -> 2.88 us  [the longest x1 0.98 us: tuned_device(): up_weight.T.astype(BF)]
  transfers between devices with their start and end apart: 49 -> 54, of which waited for: 24 -> 30; matrix products, arithmetic and copies ran while one was open for 2% -> 2% of each run, Pallas kernels for 18% -> 17%
where the time goes in v3:
time: 191 us
  waiting for transfers between devices  79.8 us (42%)
  starting transfers between devices  60.9 us (32%)
  Pallas kernels  39 us (20%)
  local copies, waits for them, and re-layouts  5.43 us (3%)
  other arithmetic  4.11 us (2%)
    ppermute x22, waiting for transfers between devices, hop_z(): return lax.ppermute(value, 'dp', [(i, i ^ step) for i in range(CHIPS)])  41.2 us
    pallas_call x17, Pallas kernels, call(): pl.pallas_call(body, out_shape=[jax.ShapeDtypeStruct(s, t) for s, t in ou...  39 us
    ppermute x22, starting transfers between devices, hop_z(): return lax.ppermute(value, 'dp', [(i, i ^ step) for i in range(CHIPS)])  33.4 us
    ppermute x7, waiting for transfers between devices, hop_first(): lax.ppermute(value, AXES, [(i, i ^ (4 if i % 2 else 2)) for i in range(2...  16.2 us
    ppermute x11, waiting for transfers between devices, hop_second(): lax.ppermute(value, AXES, [(i, i ^ (2 if i % 2 else 4)) for i in range(2...  14.1 us
    ppermute x11, starting transfers between devices, hop_second(): lax.ppermute(value, AXES, [(i, i ^ (2 if i % 2 else 4)) for i in range(2...  13.6 us
    ppermute x7, starting transfers between devices, hop_first(): lax.ppermute(value, AXES, [(i, i ^ (4 if i % 2 else 2)) for i in range(2...  11.9 us
    ppermute x14, waiting for transfers between devices, swap(): return lax.ppermute(value, 'fsdp', [(0, 1), (1, 0)])  8.32 us
  transfers between devices with their start and end apart: 54, of which 30 were waited for; matrix products, arithmetic and copies ran while one was open for 2% of the time, Pallas kernels for 17%

profile of v3, /device:TPU:0, one launch (start us, length us, event | category | flops | bytes accessed | tf_op | source)
XLA Modules:
  0.0 190.7 jit_solution(16476956600183616944)
XLA Ops:
  2.6 4.1 %collective-permute-start.4 = (bf16[96,768]{1,0:T(8,128)(2,1)S(1)}, bf16[96,768]{1,0:T(8,128)(2,1)S(1)}, u32[]{:S(2)}, u32[]{:S(2)}) collective-permute-start(bf16[96,768]{1,0:T(8,128)(2,1)S(1)} %pad_maximum_fusion.3), channel_id=1, source_target_pairs={{0,16},{2,18},{4,20},{6,22},{8,24},{10,26},{12,28},{14,30},{16,0},... | collective-permute-start | bytes 442376 | tf_op jit(solution)/shard_map/ppermute | solution.py:652
  12.6 2.0 %collective-permute-done.4 = bf16[96,768]{1,0:T(8,128)(2,1)S(1)} collective-permute-done((bf16[96,768]{1,0:T(8,128)(2,1)S(1)}, bf16[96,768]{1,0:T(8,128)(2,1)S(1)}, u32[]{:S(2)}, u32[]{:S(2)}) %collective-permute-start.4) | collective-permute-done | bytes 147488 | tf_op jit(solution)/shard_map/ppermute | solution.py:652
  14.7 4.9 %collective-permute-done.5 = bf16[96,768]{1,0:T(8,128)(2,1)S(1)} collective-permute-done((bf16[96,768]{1,0:T(8,128)(2,1)S(1)}, bf16[96,768]{1,0:T(8,128)(2,1)S(1)}, u32[]{:S(2)}, u32[]{:S(2)}) %collective-permute-start.5) | collective-permute-done | bytes 147488 | tf_op jit(solution)/shard_map/ppermute | solution.py:652
  21.2 2.6 %collective-permute-start.3 = (bf16[288,768]{1,0:T(8,128)(2,1)S(1)}, bf16[288,768]{1,0:T(8,128)(2,1)S(1)}, u32[]{:S(2)}, u32[]{:S(2)}) collective-permute-start(bf16[288,768]{1,0:T(8,128)(2,1)S(1)} %collective-permute-done.1.s1), channel_id=1, source_target_pairs={{0,4},{1,3},{2,6},{3,1},{4,0},{5,7},{6,2},{7,5},{8,12},{9,11},{10,... | collective-permute-start | bytes 1327112 | tf_op jit(solution)/shard_map/ppermute | solution.py:648
  23.7 2.6 %collective-permute-done.17 = bf16[96,768]{1,0:T(8,128)(2,1)S(1)} collective-permute-done((bf16[96,768]{1,0:T(8,128)(2,1)S(1)}, bf16[96,768]{1,0:T(8,128)(2,1)S(1)}, u32[]{:S(2)}, u32[]{:S(2)}) %collective-permute-start.17) | collective-permute-done | bytes 147488 | tf_op jit(solution)/shard_map/ppermute | solution.py:652
  28.1 2.5 %collective-permute-start.22 = (bf16[96,768]{1,0:T(8,128)(2,1)S(1)}, bf16[96,768]{1,0:T(8,128)(2,1)S(1)}, u32[]{:S(2)}, u32[]{:S(2)}) collective-permute-start(bf16[96,768]{1,0:T(8,128)(2,1)S(1)} %convert_element_type.78), channel_id=1, source_target_pairs={{0,16},{2,18},{4,20},{6,22},{8,24},{10,26},{12,28},{14,30},{16,0},... | collective-permute-start | bytes 442376 | tf_op jit(solution)/shard_map/ppermute | solution.py:652
  32.2 5.6 %collective-permute-done.18 = bf16[192,768]{1,0:T(8,128)(2,1)S(1)} collective-permute-done((bf16[192,768]{1,0:T(8,128)(2,1)S(1)}, bf16[192,768]{1,0:T(8,128)(2,1)S(1)}, u32[]{:S(2)}, u32[]{:S(2)}) %collective-permute-start.18) | collective-permute-done | bytes 294944 | tf_op jit(solution)/shard_map/ppermute | solution.py:652
  43.8 5.4 %collective-permute-done.23 = bf16[192,768]{1,0:T(8,128)(2,1)} collective-permute-done((bf16[192,768]{1,0:T(8,128)(2,1)S(1)}, bf16[192,768]{1,0:T(8,128)(2,1)}, u32[]{:S(2)}, u32[]{:S(2)}) %collective-permute-start.23) | collective-permute-done | bytes 294944 | tf_op jit(solution)/shard_map/ppermute | solution.py:652
  52.9 2.5 %collective-permute-start.24 = (bf16[288,768]{1,0:T(8,128)(2,1)S(1)}, bf16[288,768]{1,0:T(8,128)(2,1)S(1)}, u32[]{:S(2)}, u32[]{:S(2)}) collective-permute-start(bf16[288,768]{1,0:T(8,128)(2,1)S(1)} %constant_dynamic-update-slice_fusion.5.z0.w0), channel_id=1, source_target_pairs={{0,2},{1,5},{2,0},{3,7},{4,6},{5,1},{6,4},{7,3},{8,10},{9,13},{10,... | collective-permute-start | bytes 1327112 | tf_op jit(solution)/shard_map/ppermute | solution.py:644
  56.8 6.3 %attend_forward.1 = (f32[2304,256]{1,0:T(8,128)S(1)}, f32[768,256]{1,0:T(8,128)S(1)}, f32[16,256]{1,0:T(8,128)S(1)}, bf16[1536,256]{1,0:T(8,128)(2,1)S(1)}, bf16[1536,256]{1,0:T(8,128)(2,1)S(1)}) custom-call(s32[1,6]{1,0:T(1,128)S(1)} %copy-done.30, s32[2]{0:T(128)S(1)} %pad_add_fusion.me, bf16[256,768]{1,0:T(8,128)(2,1)S(1)} %copy-done.1, ...), custom_call_target="tpu_custom_call" | custom-call | flops 650000000 | tf_op jit(solution)/shard_map/attend_forward/pallas_call | solution.py:315
  66.4 3.5 %collective-permute-done.21.z3 = bf16[288,768]{1,0:T(8,128)(2,1)S(1)} collective-permute-done((bf16[288,768]{1,0:T(8,128)(2,1)}, bf16[288,768]{1,0:T(8,128)(2,1)S(1)}, u32[]{:S(2)}, u32[]{:S(2)}) %collective-permute-start.21) | collective-permute-done | bytes 442400 | tf_op jit(solution)/shard_map/ppermute | solution.py:648
  70.9 3.9 %attend_close.1 = (f32[256,768]{1,0:T(8,128)S(1)}, bf16[256,768]{1,0:T(8,128)(2,1)S(1)}, f32[256,768]{1,0:T(8,128)S(1)}, f32[256,1]{1,0:T(8,128)S(1)}) custom-call(bf16[256,768]{1,0:T(8,128)(2,1)S(1)} %copy-done.1, bf16[1536,256]{1,0:T(8,128)(2,1)S(1)} %get-tuple-element.95.rel_own.ata, bf16[1536,256]{1,0:T(8,128)(2,1)S(1)} %get-tuple-element.96.rel_par, ...), custom_call_target="tpu_custom_call" | custom-call | flops 360000000 | tf_op jit(solution)/shard_map/attend_close/pallas_call | solution.py:315
  76.6 2.6 %feed_up.1 = (bf16[1536,512]{1,0:T(8,128)(2,1)S(1)}, f32[1536,512]{1,0:T(8,128)S(1)}) custom-call(bf16[256,768]{1,0:T(8,128)(2,1)S(1)} %get-tuple-element.98.ya.za, bf16[256,768]{1,0:T(8,128)(2,1)S(1)} %collective-permute-done.15.yb.zb, bf16[384,768]{1,0:T(8,128)(2,1)S(1)} %copy-done.6, bf16[288,768]{1,0:T(8,128)(2,1)S(1)} %copy-done.4, ...), custom_call_target="tpu_custom_call" | custom-call | flops 250000000 | tf_op jit(solution)/shard_map/feed_up/pallas_call | solution.py:315
  80.9 2.3 %collective-permute-done.27.got = f32[256,768]{1,0:T(8,128)S(1)} collective-permute-done((f32[256,768]{1,0:T(8,128)S(1)}, f32[256,768]{1,0:T(8,128)S(1)}, u32[]{:S(2)}, u32[]{:S(2)}) %collective-permute-start.27) | collective-permute-done | bytes 786464 | tf_op jit(solution)/shard_map/ppermute | solution.py:640
  83.2 2.1 %finish_forward.1 = (bf16[256,768]{1,0:T(8,128)(2,1)}, f32[256,768]{1,0:T(8,128)S(1)}, bf16[256,768]{1,0:T(8,128)(2,1)S(1)}, f32[2,768]{1,0:T(2,128)S(1)}) custom-call(s32[1,6]{1,0:T(1,128)S(1)} %copy-done.30, f32[256,768]{1,0:T(8,128)S(1)} %get-tuple-element.97.first, f32[256,768]{1,0:T(8,128)S(1)} %get-tuple-element.111.own, ...), custom_call_target="tpu_custom_call" | custom-call | tf_op jit(solution)/shard_map/finish_forward/pallas_call | solution.py:315
  89.1 2.6 %feed_back.1 = (bf16[1536,512]{1,0:T(8,128)(2,1)S(1)}, f32[256,768]{1,0:T(8,128)S(1)}, f32[256,768]{1,0:T(8,128)S(1)}) custom-call(f32[1536,512]{1,0:T(8,128)S(1)} %get-tuple-element.115.slope, bf16[256,768]{1,0:T(8,128)(2,1)S(1)} %get-tuple-element.117.za, bf16[256,768]{1,0:T(8,128)(2,1)S(1)} %collective-permute-done.28.zb, bf16[384,768]{1,0:T(8,128)(2,1)S(1)} %copy-done.8, ...), custom_call_target="tpu_custom_call" | custom-call | tf_op jit(solution)/shard_map/feed_back/pallas_call | solution.py:315
  94.9 7.0 %attend_backward.1 = (f32[256,768]{1,0:T(8,128)S(1)}, bf16[256,768]{1,0:T(8,128)(2,1)S(1)}, f32[2,768]{1,0:T(2,128)S(1)}, bf16[1536,256]{1,0:T(8,128)(2,1)S(1)}, bf16[1536,256]{1,0:T(8,128)(2,1)S(1)}) custom-call(s32[1,6]{1,0:T(1,128)S(1)} %copy-done.30, s32[2]{0:T(128)S(1)} %pad_add_fusion.me, f32[256,768]{1,0:T(8,128)S(1)} %get-tuple-element.114.ds2, ...), custom_call_target="tpu_custom_call" | custom-call | tf_op jit(solution)/shard_map/attend_backward/pallas_call | solution.py:315
  109.1 11.5 %collective-permute-done.33 = bf16[384,768]{1,0:T(8,128)(2,1)S(1)} collective-permute-done((bf16[384,768]{1,0:T(8,128)(2,1)S(1)}, bf16[384,768]{1,0:T(8,128)(2,1)S(1)}, u32[]{:S(2)}, u32[]{:S(2)}) %collective-permute-start.33) | collective-permute-done | bytes 589856 | tf_op jit(solution)/shard_map/ppermute | solution.py:644
  124.8 4.4 %grad_input.1 = f32[256,768]{1,0:T(8,128)} custom-call(f32[256,768]{1,0:T(8,128)S(1)} %get-tuple-element.129.dh, bf16[1536,256]{1,0:T(8,128)(2,1)S(1)} %get-tuple-element.130.dma.rel_own, bf16[1536,256]{1,0:T(8,128)(2,1)S(1)} %get-tuple-element.127.rel_par, bf16[384,768]{1,0:T(8,128)(2,1)S(1)} %get-tuple-element.91.so, ...), custom_call_target="tpu_custom_call" | custom-call | tf_op jit(solution)/shard_map/grad_input/pallas_call | solution.py:315
  130.9 2.7 %collective-permute-start.45 = (bf16[96,768]{1,0:T(8,128)(2,1)S(1)}, bf16[96,768]{1,0:T(8,128)(2,1)S(1)}, u32[]{:S(2)}, u32[]{:S(2)}) collective-permute-start(bf16[96,768]{1,0:T(8,128)(2,1)S(1)} %get-tuple-element.168), channel_id=1, source_target_pairs={{0,16},{2,18},{4,20},{6,22},{8,24},{10,26},{12,28},{14,30},{16,0},... | collective-permute-start | bytes 442376 | tf_op jit(solution)/shard_map/ppermute | solution.py:652
  133.6 2.0 %collective-permute-start.46 = (bf16[96,768]{1,0:T(8,128)(2,1)S(1)}, bf16[96,768]{1,0:T(8,128)(2,1)S(1)}, u32[]{:S(2)}, u32[]{:S(2)}) collective-permute-start(bf16[96,768]{1,0:T(8,128)(2,1)S(1)} %get-tuple-element.169), channel_id=1, source_target_pairs={{0,24},{2,26},{4,28},{6,30},{8,16},{10,18},{12,20},{14,22},{16,8},... | collective-permute-start | bytes 442376 | tf_op jit(solution)/shard_map/ppermute | solution.py:652
  136.1 7.0 %collective-permute-done.34 = bf16[768,768]{1,0:T(8,128)(2,1)S(1)} collective-permute-done((bf16[768,768]{1,0:T(8,128)(2,1)S(1)}, bf16[768,768]{1,0:T(8,128)(2,1)S(1)}, u32[]{:S(2)}, u32[]{:S(2)}) %collective-permute-start.34) | collective-permute-done | bytes 1179680 | tf_op jit(solution)/shard_map/ppermute | solution.py:648
  145.1 2.7 %collective-permute-start.43 = (bf16[96,768]{1,0:T(8,128)(2,1)S(1)}, bf16[96,768]{1,0:T(8,128)(2,1)S(1)}, u32[]{:S(2)}, u32[]{:S(2)}) collective-permute-start(bf16[96,768]{1,0:T(8,128)(2,1)S(1)} %get-tuple-element.171), channel_id=1, source_target_pairs={{0,16},{2,18},{4,20},{6,22},{8,24},{10,26},{12,28},{14,30},{16,0},... | collective-permute-start | bytes 442376 | tf_op jit(solution)/shard_map/ppermute | solution.py:652
  147.8 2.0 %collective-permute-start.44 = (bf16[96,768]{1,0:T(8,128)(2,1)S(1)}, bf16[96,768]{1,0:T(8,128)(2,1)S(1)}, u32[]{:S(2)}, u32[]{:S(2)}) collective-permute-start(bf16[96,768]{1,0:T(8,128)(2,1)S(1)} %get-tuple-element.172), channel_id=1, source_target_pairs={{0,24},{2,26},{4,28},{6,30},{8,16},{10,18},{12,20},{14,22},{16,8},... | collective-permute-start | bytes 442376 | tf_op jit(solution)/shard_map/ppermute | solution.py:652
  150.4 2.8 %collective-permute-done.35 = bf16[384,768]{1,0:T(8,128)(2,1)S(1)} collective-permute-done((bf16[384,768]{1,0:T(8,128)(2,1)S(1)}, bf16[384,768]{1,0:T(8,128)(2,1)S(1)}, u32[]{:S(2)}, u32[]{:S(2)}) %collective-permute-start.35) | collective-permute-done | bytes 589856 | tf_op jit(solution)/shard_map/ppermute | solution.py:644
  153.3 4.4 %collective-permute-done.39 = bf16[96,768]{1,0:T(8,128)(2,1)S(1)} collective-permute-done((bf16[96,768]{1,0:T(8,128)(2,1)S(1)}, bf16[96,768]{1,0:T(8,128)(2,1)S(1)}, u32[]{:S(2)}, u32[]{:S(2)}) %collective-permute-start.39) | collective-permute-done | bytes 147488 | tf_op jit(solution)/shard_map/ppermute | solution.py:652
  157.8 3.2 %collective-permute-start.42 = (bf16[96,768]{1,0:T(8,128)(2,1)S(1)}, bf16[96,768]{1,0:T(8,128)(2,1)S(1)}, u32[]{:S(2)}, u32[]{:S(2)}) collective-permute-start(bf16[96,768]{1,0:T(8,128)(2,1)S(1)} %get-tuple-element.174), channel_id=1, source_target_pairs={{0,24},{2,26},{4,28},{6,30},{8,16},{10,18},{12,20},{14,22},{16,8},... | collective-permute-start | bytes 442376 | tf_op jit(solution)/shard_map/ppermute | solution.py:652
  162.5 3.8 %collective-permute-done.42.c1 = bf16[96,768]{1,0:T(8,128)(2,1)S(1)} collective-permute-done((bf16[96,768]{1,0:T(8,128)(2,1)S(1)}, bf16[96,768]{1,0:T(8,128)(2,1)S(1)}, u32[]{:S(2)}, u32[]{:S(2)}) %collective-permute-start.42) | collective-permute-done | bytes 147488 | tf_op jit(solution)/shard_map/ppermute | solution.py:652
  167.4 4.6 %collective-permute-done.40.a1 = bf16[96,768]{1,0:T(8,128)(2,1)S(1)} collective-permute-done((bf16[96,768]{1,0:T(8,128)(2,1)S(1)}, bf16[96,768]{1,0:T(8,128)(2,1)S(1)}, u32[]{:S(2)}, u32[]{:S(2)}) %collective-permute-start.40) | collective-permute-done | bytes 147488 | tf_op jit(solution)/shard_map/ppermute | solution.py:652
  180.1 3.3 %collective-permute-start.53 = (f32[8,768]{1,0:T(8,128)S(1)}, f32[8,768]{1,0:T(8,128)S(1)}, u32[]{:S(2)}, u32[]{:S(2)}) collective-permute-start(f32[8,768]{1,0:T(8,128)S(1)} %add_add_fusion.n0), channel_id=1, source_target_pairs={{0,24},{2,26},{4,28},{6,30},{8,16},{10,18},{12,20},{14,22},{16,8},... | collective-permute-start | bytes 73736 | tf_op jit(solution)/shard_map/ppermute | solution.py:652
  185.9 2.2 %collective-permute-done.52.n2 = f32[8,768]{1,0:T(8,128)S(1)} collective-permute-done((f32[8,768]{1,0:T(8,128)S(1)}, f32[8,768]{1,0:T(8,128)S(1)}, u32[]{:S(2)}, u32[]{:S(2)}) %collective-permute-start.52) | collective-permute-done | bytes 24608 | tf_op jit(solution)/shard_map/ppermute | solution.py:652
  188.2 2.3 %update.1 = (f32[1,1]{1,0:T(1,128)}, f32[72,768]{1,0:T(8,128)}, f32[24,768]{1,0:T(8,128)}, f32[96,768]{1,0:T(8,128)}, f32[96,768]{1,0:T(8,128)}, /*index=5*/f32[...) custom-call(f32[8,768]{1,0:T(8,128)S(1)} %add_add_fusion.n0, ...), custom_call_target="tpu_custom_call" | custom-call | tf_op jit(solution)/shard_map/update/pallas_call | solution.py:315
  (185 shorter events, 67.9 us)
Async XLA Ops:
  2.6 12.1 %collective-permute-start.4 = (bf16[96,768]{1,0:T(8,128)(2,1)S(1)}, bf16[96,768]{1,0:T(8,128)(2,1)S(1)}, u32[]{:S(2)}, u32[]{:S(2)}) collective-permute-start(bf16[96,768]{1,0:T(8,128)(2,1)S(1)} %pad_maximum_fusion.3), channel_id=1, source_target_pairs={{0,16},{2,18},{4,20},{6,22},{8,24},{10,26},{12,28},{14,30},{16,0},... | collective-permute-start | bytes 442376 | tf_op jit(solution)/shard_map/ppermute | solution.py:652
  7.7 12.0 %collective-permute-start.1 = (bf16[288,768]{1,0:T(8,128)(2,1)S(1)}, bf16[288,768]{1,0:T(8,128)(2,1)S(1)}, u32[]{:S(2)}, u32[]{:S(2)}) collective-permute-start(bf16[288,768]{1,0:T(8,128)(2,1)S(1)} %pad_maximum_fusion.s0), channel_id=1, source_target_pairs={{0,2},{1,5},{2,0},{3,7},{4,6},{5,1},{6,4},{7,3},{8,10},{9,13},{10,... | collective-permute-start | bytes 1327112 | tf_op jit(solution)/shard_map/ppermute | solution.py:644
  9.3 10.3 %collective-permute-start.5 = (bf16[96,768]{1,0:T(8,128)(2,1)S(1)}, bf16[96,768]{1,0:T(8,128)(2,1)S(1)}, u32[]{:S(2)}, u32[]{:S(2)}) collective-permute-start(bf16[96,768]{1,0:T(8,128)(2,1)S(1)} %pad_maximum_fusion.3), channel_id=1, source_target_pairs={{0,8},{2,10},{4,12},{6,14},{8,0},{10,2},{12,4},{14,6},{16,24},{18,... | collective-permute-start | bytes 442376 | tf_op jit(solution)/shard_map/ppermute | solution.py:652
  10.9 8.7 %collective-permute-start.6 = (bf16[96,768]{1,0:T(8,128)(2,1)S(1)}, bf16[96,768]{1,0:T(8,128)(2,1)S(1)}, u32[]{:S(2)}, u32[]{:S(2)}) collective-permute-start(bf16[96,768]{1,0:T(8,128)(2,1)S(1)} %pad_maximum_fusion.3), channel_id=1, source_target_pairs={{0,24},{2,26},{4,28},{6,30},{8,16},{10,18},{12,20},{14,22},{16,8},... | collective-permute-start | bytes 442376 | tf_op jit(solution)/shard_map/ppermute | solution.py:652
  11.1 19.5 %collective-permute-start.2 = (bf16[288,768]{1,0:T(8,128)(2,1)S(1)}, bf16[288,768]{1,0:T(8,128)(2,1)S(1)}, u32[]{:S(2)}, u32[]{:S(2)}) collective-permute-start(bf16[288,768]{1,0:T(8,128)(2,1)S(1)} %pad_maximum_fusion.s0), channel_id=1, source_target_pairs={{0,4},{1,3},{2,6},{3,1},{4,0},{5,7},{6,2},{7,5},{8,12},{9,11},{10,... | collective-permute-start | bytes 1327112 | tf_op jit(solution)/shard_map/ppermute | solution.py:648
  14.7 11.7 %collective-permute-start.17 = (bf16[96,768]{1,0:T(8,128)(2,1)S(1)}, bf16[96,768]{1,0:T(8,128)(2,1)S(1)}, u32[]{:S(2)}, u32[]{:S(2)}) collective-permute-start(bf16[96,768]{1,0:T(8,128)(2,1)S(1)} %bitcast_convert_fusion), channel_id=1, source_target_pairs={{0,16},{2,18},{4,20},{6,22},{8,24},{10,26},{12,28},{14,30},{16,0},... | collective-permute-start | bytes 442376 | tf_op jit(solution)/shard_map/ppermute | solution.py:652
  19.7 18.1 %collective-permute-start.7 = (bf16[288,768]{1,0:T(8,128)(2,1)S(1)}, bf16[288,768]{1,0:T(8,128)(2,1)S(1)}, u32[]{:S(2)}, u32[]{:S(2)}) collective-permute-start(bf16[288,768]{1,0:T(8,128)(2,1)S(1)} %constant_dynamic-update-slice_fusion.z0), channel_id=1, source_target_pairs={{0,2},{1,5},{2,0},{3,7},{4,6},{5,1},{6,4},{7,3},{8,10},{9,13},{10,... | collective-permute-start | bytes 1327112 | tf_op jit(solution)/shard_map/ppermute | solution.py:644
  21.2 17.9 %collective-permute-start.3 = (bf16[288,768]{1,0:T(8,128)(2,1)S(1)}, bf16[288,768]{1,0:T(8,128)(2,1)S(1)}, u32[]{:S(2)}, u32[]{:S(2)}) collective-permute-start(bf16[288,768]{1,0:T(8,128)(2,1)S(1)} %collective-permute-done.1.s1), channel_id=1, source_target_pairs={{0,4},{1,3},{2,6},{3,1},{4,0},{5,7},{6,2},{7,5},{8,12},{9,11},{10,... | collective-permute-start | bytes 1327112 | tf_op jit(solution)/shard_map/ppermute | solution.py:648
  26.3 11.4 %collective-permute-start.18 = (bf16[192,768]{1,0:T(8,128)(2,1)S(1)}, bf16[192,768]{1,0:T(8,128)(2,1)S(1)}, u32[]{:S(2)}, u32[]{:S(2)}) collective-permute-start(bf16[192,768]{1,0:T(8,128)(2,1)S(1)} %pad_maximum_fusion.1), channel_id=1, source_target_pairs={{0,8},{2,10},{4,12},{6,14},{8,0},{10,2},{12,4},{14,6},{16,24},{18,... | collective-permute-start | bytes 884744 | tf_op jit(solution)/shard_map/ppermute | solution.py:652
  28.1 12.6 %collective-permute-start.22 = (bf16[96,768]{1,0:T(8,128)(2,1)S(1)}, bf16[96,768]{1,0:T(8,128)(2,1)S(1)}, u32[]{:S(2)}, u32[]{:S(2)}) collective-permute-start(bf16[96,768]{1,0:T(8,128)(2,1)S(1)} %convert_element_type.78), channel_id=1, source_target_pairs={{0,16},{2,18},{4,20},{6,22},{8,24},{10,26},{12,28},{14,30},{16,0},... | collective-permute-start | bytes 442376 | tf_op jit(solution)/shard_map/ppermute | solution.py:652
  30.6 18.7 %collective-permute-start.8 = (bf16[288,768]{1,0:T(8,128)(2,1)S(1)}, bf16[288,768]{1,0:T(8,128)(2,1)S(1)}, u32[]{:S(2)}, u32[]{:S(2)}) collective-permute-start(bf16[288,768]{1,0:T(8,128)(2,1)S(1)} %constant_dynamic-update-slice_fusion.z0), channel_id=1, source_target_pairs={{0,4},{1,3},{2,6},{3,1},{4,0},{5,7},{6,2},{7,5},{8,12},{9,11},{10,... | collective-permute-start | bytes 1327112 | tf_op jit(solution)/shard_map/ppermute | solution.py:648
  37.8 12.3 %collective-permute-start.19 = (bf16[288,768]{1,0:T(8,128)(2,1)S(1)}, bf16[288,768]{1,0:T(8,128)(2,1)S(1)}, u32[]{:S(2)}, u32[]{:S(2)}) collective-permute-start(bf16[288,768]{1,0:T(8,128)(2,1)S(1)} %constant_dynamic-update-slice_fusion.3.z0), channel_id=1, source_target_pairs={{0,2},{1,5},{2,0},{3,7},{4,6},{5,1},{6,4},{7,3},{8,10},{9,13},{10,... | collective-permute-start | bytes 1327112 | tf_op jit(solution)/shard_map/ppermute | solution.py:644
  39.1 11.0 %collective-permute-start.9 = (bf16[288,768]{1,0:T(8,128)(2,1)S(1)}, bf16[288,768]{1,0:T(8,128)(2,1)S(1)}, u32[]{:S(2)}, u32[]{:S(2)}) collective-permute-start(bf16[288,768]{1,0:T(8,128)(2,1)S(1)} %collective-permute-done.7.z1), channel_id=1, source_target_pairs={{0,4},{1,3},{2,6},{3,1},{4,0},{5,7},{6,2},{7,5},{8,12},{9,11},{10,... | collective-permute-start | bytes 1327112 | tf_op jit(solution)/shard_map/ppermute | solution.py:648
  43.8 12.0 %collective-permute-start.10 = (bf16[384,768]{1,0:T(8,128)(2,1)S(1)}, bf16[384,768]{1,0:T(8,128)(2,1)S(1)}, u32[]{:S(2)}, u32[]{:S(2)}) collective-permute-start(bf16[384,768]{1,0:T(8,128)(2,1)S(1)} %get-tuple-element.91.so), channel_id=1, source_target_pairs={{0,1},{1,0},{2,3},{3,2},{4,5},{5,4},{6,7},{7,6},{8,9},{9,8},{10,11... | collective-permute-start | bytes 1769480 | tf_op jit(solution)/shard_map/ppermute | solution.py:640
  51.9 12.6 %collective-permute-start.20 = (bf16[288,768]{1,0:T(8,128)(2,1)}, bf16[288,768]{1,0:T(8,128)(2,1)S(1)}, u32[]{:S(2)}, u32[]{:S(2)}) collective-permute-start(bf16[288,768]{1,0:T(8,128)(2,1)} %copy-done.3), channel_id=1, source_target_pairs={{0,4},{1,3},{2,6},{3,1},{4,0},{5,7},{6,2},{7,5},{8,12},{9,11},{10,... | collective-permute-start | bytes 1327112 | tf_op jit(solution)/shard_map/ppermute | solution.py:648
  52.9 13.6 %collective-permute-start.24 = (bf16[288,768]{1,0:T(8,128)(2,1)S(1)}, bf16[288,768]{1,0:T(8,128)(2,1)S(1)}, u32[]{:S(2)}, u32[]{:S(2)}) collective-permute-start(bf16[288,768]{1,0:T(8,128)(2,1)S(1)} %constant_dynamic-update-slice_fusion.5.z0.w0), channel_id=1, source_target_pairs={{0,2},{1,5},{2,0},{3,7},{4,6},{5,1},{6,4},{7,3},{8,10},{9,13},{10,... | collective-permute-start | bytes 1327112 | tf_op jit(solution)/shard_map/ppermute | solution.py:644
  55.4 14.6 %collective-permute-start.21 = (bf16[288,768]{1,0:T(8,128)(2,1)}, bf16[288,768]{1,0:T(8,128)(2,1)S(1)}, u32[]{:S(2)}, u32[]{:S(2)}) collective-permute-start(bf16[288,768]{1,0:T(8,128)(2,1)} %copy-done.9), channel_id=1, source_target_pairs={{0,4},{1,3},{2,6},{3,1},{4,0},{5,7},{6,2},{7,5},{8,12},{9,11},{10,... | collective-permute-start | bytes 1327112 | tf_op jit(solution)/shard_map/ppermute | solution.py:648
  63.1 13.4 %collective-permute-start.16 = (bf16[1536,256]{1,0:T(8,128)(2,1)S(1)}, bf16[1536,256]{1,0:T(8,128)(2,1)S(1)}, u32[]{:S(2)}, u32[]{:S(2)}) collective-permute-start(bf16[1536,256]{1,0:T(8,128)(2,1)S(1)} %get-tuple-element.96.rel_par), channel_id=1, source_target_pairs={{0,1},{1,0},{2,3},{3,2},{4,5},{5,4},{6,7},{7,6},{8,9},{9,8},{10,11... | collective-permute-start | bytes 2359304 | tf_op jit(solution)/shard_map/ppermute | solution.py:640
  64.5 14.7 %collective-permute-start.25 = (bf16[288,768]{1,0:T(8,128)(2,1)S(1)}, bf16[288,768]{1,0:T(8,128)(2,1)S(1)}, u32[]{:S(2)}, u32[]{:S(2)}) collective-permute-start(bf16[288,768]{1,0:T(8,128)(2,1)S(1)} %constant_dynamic-update-slice_fusion.5.z0.w0), channel_id=1, source_target_pairs={{0,4},{1,3},{2,6},{3,1},{4,0},{5,7},{6,2},{7,5},{8,12},{9,11},{10,... | collective-permute-start | bytes 1327112 | tf_op jit(solution)/shard_map/ppermute | solution.py:648
  70.0 9.5 %collective-permute-start.26 = (bf16[288,768]{1,0:T(8,128)(2,1)S(1)}, bf16[288,768]{1,0:T(8,128)(2,1)S(1)}, u32[]{:S(2)}, u32[]{:S(2)}) collective-permute-start(bf16[288,768]{1,0:T(8,128)(2,1)S(1)} %collective-permute-done.24.z1.w1), channel_id=1, source_target_pairs={{0,4},{1,3},{2,6},{3,1},{4,0},{5,7},{6,2},{7,5},{8,12},{9,11},{10,... | collective-permute-start | bytes 1327112 | tf_op jit(solution)/shard_map/ppermute | solution.py:648
  87.8 16.3 %collective-permute-start.32 = (bf16[768,768]{1,0:T(8,128)(2,1)S(1)}, bf16[768,768]{1,0:T(8,128)(2,1)S(1)}, u32[]{:S(2)}, u32[]{:S(2)}) collective-permute-start(bf16[768,768]{1,0:T(8,128)(2,1)S(1)} %grad_down_away.1), channel_id=1, source_target_pairs={{0,4},{1,3},{2,6},{3,1},{4,0},{5,7},{6,2},{7,5},{8,12},{9,11},{10,... | collective-permute-start | bytes 3538952 | tf_op jit(solution)/shard_map/ppermute | solution.py:648
  92.9 30.2 %collective-permute-start.36 = (bf16[768,768]{1,0:T(8,128)(2,1)S(1)}, bf16[768,768]{1,0:T(8,128)(2,1)S(1)}, u32[]{:S(2)}, u32[]{:S(2)}) collective-permute-start(bf16[768,768]{1,0:T(8,128)(2,1)S(1)} %grad_up_away.1), channel_id=1, source_target_pairs={{0,4},{1,3},{2,6},{3,1},{4,0},{5,7},{6,2},{7,5},{8,12},{9,11},{10,... | collective-permute-start | bytes 3538952 | tf_op jit(solution)/shard_map/ppermute | solution.py:648
  104.2 16.3 %collective-permute-start.33 = (bf16[384,768]{1,0:T(8,128)(2,1)S(1)}, bf16[384,768]{1,0:T(8,128)(2,1)S(1)}, u32[]{:S(2)}, u32[]{:S(2)}) collective-permute-start(bf16[384,768]{1,0:T(8,128)(2,1)S(1)} %add_convert_fusion.2), channel_id=1, source_target_pairs={{0,2},{1,5},{2,0},{3,7},{4,6},{5,1},{6,4},{7,3},{8,10},{9,13},{10,... | collective-permute-start | bytes 1769480 | tf_op jit(solution)/shard_map/ppermute | solution.py:644
  120.6 22.5 %collective-permute-start.34 = (bf16[768,768]{1,0:T(8,128)(2,1)S(1)}, bf16[768,768]{1,0:T(8,128)(2,1)S(1)}, u32[]{:S(2)}, u32[]{:S(2)}) collective-permute-start(bf16[768,768]{1,0:T(8,128)(2,1)S(1)} %mix_away.1), channel_id=1, source_target_pairs={{0,4},{1,3},{2,6},{3,1},{4,0},{5,7},{6,2},{7,5},{8,12},{9,11},{10,... | collective-permute-start | bytes 3538952 | tf_op jit(solution)/shard_map/ppermute | solution.py:648
  123.2 21.7 %collective-permute-start.37 = (bf16[384,768]{1,0:T(8,128)(2,1)S(1)}, bf16[384,768]{1,0:T(8,128)(2,1)S(1)}, u32[]{:S(2)}, u32[]{:S(2)}) collective-permute-start(bf16[384,768]{1,0:T(8,128)(2,1)S(1)} %add_convert_fusion), channel_id=1, source_target_pairs={{0,2},{1,5},{2,0},{3,7},{4,6},{5,1},{6,4},{7,3},{8,10},{9,13},{10,... | collective-permute-start | bytes 1769480 | tf_op jit(solution)/shard_map/ppermute | solution.py:644
  130.9 18.9 %collective-permute-start.45 = (bf16[96,768]{1,0:T(8,128)(2,1)S(1)}, bf16[96,768]{1,0:T(8,128)(2,1)S(1)}, u32[]{:S(2)}, u32[]{:S(2)}) collective-permute-start(bf16[96,768]{1,0:T(8,128)(2,1)S(1)} %get-tuple-element.168), channel_id=1, source_target_pairs={{0,16},{2,18},{4,20},{6,22},{8,24},{10,26},{12,28},{14,30},{16,0},... | collective-permute-start | bytes 442376 | tf_op jit(solution)/shard_map/ppermute | solution.py:652
  133.6 16.7 %collective-permute-start.46 = (bf16[96,768]{1,0:T(8,128)(2,1)S(1)}, bf16[96,768]{1,0:T(8,128)(2,1)S(1)}, u32[]{:S(2)}, u32[]{:S(2)}) collective-permute-start(bf16[96,768]{1,0:T(8,128)(2,1)S(1)} %get-tuple-element.169), channel_id=1, source_target_pairs={{0,24},{2,26},{4,28},{6,30},{8,16},{10,18},{12,20},{14,22},{16,8},... | collective-permute-start | bytes 442376 | tf_op jit(solution)/shard_map/ppermute | solution.py:652
  135.6 9.5 %collective-permute-start.38 = (bf16[96,768]{1,0:T(8,128)(2,1)S(1)}, bf16[96,768]{1,0:T(8,128)(2,1)S(1)}, u32[]{:S(2)}, u32[]{:S(2)}) collective-permute-start(bf16[96,768]{1,0:T(8,128)(2,1)S(1)} %get-tuple-element.170), channel_id=1, source_target_pairs={{0,8},{2,10},{4,12},{6,14},{8,0},{10,2},{12,4},{14,6},{16,24},{18,... | collective-permute-start | bytes 442376 | tf_op jit(solution)/shard_map/ppermute | solution.py:652
  143.2 9.9 %collective-permute-start.35 = (bf16[384,768]{1,0:T(8,128)(2,1)S(1)}, bf16[384,768]{1,0:T(8,128)(2,1)S(1)}, u32[]{:S(2)}, u32[]{:S(2)}) collective-permute-start(bf16[384,768]{1,0:T(8,128)(2,1)S(1)} %add_convert_fusion.1), channel_id=1, source_target_pairs={{0,2},{1,5},{2,0},{3,7},{4,6},{5,1},{6,4},{7,3},{8,10},{9,13},{10,... | collective-permute-start | bytes 1769480 | tf_op jit(solution)/shard_map/ppermute | solution.py:644
  145.1 17.1 %collective-permute-start.43 = (bf16[96,768]{1,0:T(8,128)(2,1)S(1)}, bf16[96,768]{1,0:T(8,128)(2,1)S(1)}, u32[]{:S(2)}, u32[]{:S(2)}) collective-permute-start(bf16[96,768]{1,0:T(8,128)(2,1)S(1)} %get-tuple-element.171), channel_id=1, source_target_pairs={{0,16},{2,18},{4,20},{6,22},{8,24},{10,26},{12,28},{14,30},{16,0},... | collective-permute-start | bytes 442376 | tf_op jit(solution)/shard_map/ppermute | solution.py:652
  147.8 14.4 %collective-permute-start.44 = (bf16[96,768]{1,0:T(8,128)(2,1)S(1)}, bf16[96,768]{1,0:T(8,128)(2,1)S(1)}, u32[]{:S(2)}, u32[]{:S(2)}) collective-permute-start(bf16[96,768]{1,0:T(8,128)(2,1)S(1)} %get-tuple-element.172), channel_id=1, source_target_pairs={{0,24},{2,26},{4,28},{6,30},{8,16},{10,18},{12,20},{14,22},{16,8},... | collective-permute-start | bytes 442376 | tf_op jit(solution)/shard_map/ppermute | solution.py:652
  161.0 11.1 %collective-permute-start.40 = (bf16[96,768]{1,0:T(8,128)(2,1)S(1)}, bf16[96,768]{1,0:T(8,128)(2,1)S(1)}, u32[]{:S(2)}, u32[]{:S(2)}) collective-permute-start(bf16[96,768]{1,0:T(8,128)(2,1)S(1)} %get-tuple-element.176), channel_id=1, source_target_pairs={{0,16},{2,18},{4,20},{6,22},{8,24},{10,26},{12,28},{14,30},{16,0},... | collective-permute-start | bytes 442376 | tf_op jit(solution)/shard_map/ppermute | solution.py:652
  (53 other events, 564.7 us)

commit v4 on v3

--- a/solution.py
+++ b/solution.py
@@ -244,7 +244,9 @@
     "attend_forward": 0.65,
     "attend_close": 0.36,
     "feed_up": 0.25,
-    "feed_down": 0.15,
+    "down_away": 0.1,
+    "down_here": 0.0,
+    "turn_round": 0.0,
     "finish_forward": 0.0,
     "grad_down_away": 0.0,
     "grad_down_here": 0.0,
@@ -254,10 +256,10 @@
     "close_sums": 0.0,
     "update": 0.0,
     "grad_up_away": 0.0,
-    "grad_up_here": 1.0,
+    "grad_up_here": 0.8,
     "feed_back": 0.0,
     "mix_away": 0.0,
-    "mix_here": 2.0,
+    "mix_here": 1.5,
 }
 MB = 16
 CHIPS = 16
@@ -436,13 +438,15 @@
             )
 
 
-def feed_down(hid, s, z0, z1, z2, z3, own, other, whole):
+def down_away(hid, s, z0, z1, z2, z3, other, whole):
     for (base, size), ref in zip(PIECES, (s, z0, z1, z2, z3)):
         whole[base : base + size, :] = ref[...]
-    rows = own.shape[0]
-    w = whole[...]
-    own[...] = tn(hid[:, 0:rows], w)
-    other[...] = tn(hid[:, rows : 2 * rows], w)
+    rows = other.shape[0]
+    other[...] = tn(hid[:, rows : 2 * rows], whole[...])
+
+
+def down_here(hid, whole, own):
+    own[...] = tn(hid[:, 0 : own.shape[0]], whole[...])
 
 
 def norm_back(dy, gain, hat, scale):
@@ -454,22 +458,31 @@
     )
 
 
-def finish_forward(lengths, first, own, got, cot, norms, out, ds2, dz, terms):
-    rows = first.shape[0]
+def live_rows(lengths, rows):
     used = jnp.int32(0)
     for s in range(5):
         used = used + lengths[0, s]
-    live = jnp.where(lax.broadcasted_iota(jnp.int32, (rows, 1), 0) < used, 1.0, 0.0)
+    return jnp.where(lax.broadcasted_iota(jnp.int32, (rows, 1), 0) < used, 1.0, 0.0)
+
+
+def turn_round(lengths, first, own, got, cot, norms, ds2, dz, xhat):
     h = first[...] + (own[...] + got[...])
     centered = h - jnp.mean(h, axis=-1, keepdims=True)
     spread = jnp.mean(centered * centered, axis=-1, keepdims=True)
     scale = lax.rsqrt(spread + 1e-05)
     hat = centered * scale
-    out[...] = ((hat * norms[2:3, :] + norms[3:4, :]) * live).astype(BF)
-    dy = cot[...].astype(F32) * live
+    xhat[...] = hat
+    dy = cot[...].astype(F32) * live_rows(lengths, first.shape[0])
     back = norm_back(dy, norms[2:3, :], hat, scale)
     ds2[...] = back
     dz[...] = back.astype(BF)
+
+
+def finish_forward(lengths, xhat, cot, norms, out, terms):
+    live = live_rows(lengths, xhat.shape[0])
+    hat = xhat[...]
+    out[...] = ((hat * norms[2:3, :] + norms[3:4, :]) * live).astype(BF)
+    dy = cot[...].astype(F32) * live
     terms[0:1, :] = jnp.sum(dy * hat, axis=0, keepdims=True)
     terms[1:2, :] = jnp.sum(dy, axis=0, keepdims=True)
 
@@ -506,12 +519,12 @@
 
 
 def feed_back(
-    slope, za, zb, d, w0, w1, w2, w3, s, z0, z1, z2, z3, dup, mine, other, whole,
+    slope, za, zb, d, s, z0, z1, z2, z3, dup, mine, other, whole,
 ):
     rows = za.shape[0]
-    for (base, size), ref in zip(PIECES, (d, w0, w1, w2, w3)):
+    for base, size in PIECES:
         here = slice(base, base + size)
-        w = ref[...]
+        w = d[here, :]
         dup[here, 0:rows] = (nt(w, za[...]) * slope[here, 0:rows]).astype(BF)
         dup[here, rows:] = (nt(w, zb[...]) * slope[here, rows:]).astype(BF)
     for (base, size), ref in zip(PIECES, (s, z0, z1, z2, z3)):
@@ -702,7 +715,7 @@
     near3, joined3 = z_round(blocks[2], False, (near2[0],))
     s_third = hop_second(s_first)
     s_parts = (s_all, s_first, s_second, s_third)
-    turned1 = hop_first(tie(joined1, s_first))
+    turned1 = hop_first(tie(joined1, s_second))
     across1 = hop_second(tie(joined1, s_second))
     corner1 = hop_second(tie(turned1, s_third))
     turned2 = hop_first(tie(joined2, turned1))
@@ -734,7 +747,7 @@
         [((rows, width), F32), ((rows, width), BF), ((rows, width), F32), ((rows, 1), F32)],
         (tokens, at_own, at_par) + attn_own + attn_par + (norm_params,),
     )
-    corner3 = hop_second(tie(turned3, corner2))
+    corner3 = hop_second(tie(turned3, corner2, first_low))
     down_all = (sorted3, joined3, turned3, across3, corner3)
     at_got = swap(at_par)
     first_par = swap(first_low)
@@ -743,19 +756,24 @@
         [((HALF, 2 * rows), BF), ((HALF, 2 * rows), F32)],
         (first_low, tie(first_par, at_got)) + up_all,
     )
-    down_own, down_par = call(
-        feed_down,
-        [((rows, width), F32)] * 2,
-        (hid,) + down_all,
-        scratch=[pltpu.VMEM((HALF, width), BF)],
-    )
-    output, ds2, dz, terms_two = call(
+    down_par, down_full = call(
+        down_away, [((rows, width), F32), ((HALF, width), BF)], (hid,) + down_all
+    )
+    down_got = swap(down_par)
+    (down_own,) = call(down_here, [((rows, width), F32)], (tie(hid, down_par), down_full))
+    ds2, dz, xhat_two = call(
+        turn_round,
+        [((rows, width), F32), ((rows, width), BF), ((rows, width), F32)],
+        (lengths, first, down_own, down_got, cotangent, norm_params),
+        smem=1,
+    )
+    dz_par = swap(dz)
+    output, terms_two = call(
         finish_forward,
-        [((rows, width), BF), ((rows, width), F32), ((rows, width), BF), ((2, width), F32)],
-        (lengths, first, down_own, swap(down_par), cotangent, norm_params),
+        [((rows, width), BF), ((2, width), F32)],
+        (lengths, xhat_two, cotangent, norm_params),
         smem=1,
     )
-    dz_par = swap(dz)
     away = [((2 * PLANE, width), BF)]
     stay = [((PLANE, width), F32)] * 2
     (send3,) = call(grad_away, away, (hid, dz, dz_par), name="grad_down_away")
@@ -763,7 +781,7 @@
     dup, dy_own, dy_par = call(
         feed_back,
         [((HALF, 2 * rows), BF)] + [((rows, width), F32)] * 2,
-        (slope, tie(dz, send3), dz_par) + down_all + up_all,
+        (slope, tie(dz, send3, terms_two), dz_par, down_full) + up_all,
         scratch=[pltpu.VMEM((HALF, width), BF)],
     )
     (send2,) = call(grad_away, away, (dup, first_low, first_par), name="grad_up_away")
@@ -790,12 +808,15 @@
     )
     low_turn3 = add_first(turn3, got3)
     back3 = hop_first(low_turn3)
-    back2 = hop_first(add_first(turn2, got2))
+    low_turn2 = add_first(turn2, got2)
+    back2 = hop_first(low_turn2)
     factors = (
         dm_own, swap(dm_par), tokens, x_par, at_own, at_got,
         do, swap(do),
     )
     (send1,) = call(mix_away, away, factors)
+    keep3, low3 = add_second(own3, got3, back3)
+    parts3 = send_z(low3)
     got1 = hop_second(tie(send1, back3))
     turn1, own1 = call(mix_here, stay, (tie(dm_own, send1),) + factors[1:])
     (grad_tokens,) = call(
@@ -803,8 +824,6 @@
         [((rows, width), F32)],
         (tie(dh, send1), dm_own, dm_par) + attn_own + attn_par,
     )
-    keep3, low3 = add_second(own3, got3, back3)
-    parts3 = send_z(low3)
     keep2, low2 = add_second(own2, got2, back2)
     parts2 = send_z(tie(low2, parts3[1]))
     back1 = hop_first(add_first(tie(turn1, grad_tokens), got1))

time: 191 us -> 189 us (0.990)
  waiting for transfers between devices: 79.8 us -> 76.8 us
    ppermute x7, starting transfers between devices: 11.9 us -> 9.28 us  [hop_first(): lax.ppermute(value, AXES, [(i, i ^ (4 if i % 2 else 2)) for i in range(2...]
    pallas_call x17 -> x19, Pallas kernels: 39 us -> 39.9 us  [call(): pl.pallas_call(body, out_shape=[jax.ShapeDtypeStruct(s, t) for s, t in ou...]
  transfers between devices with their start and end apart: 54 -> 54, of which waited for: 30 -> 29; matrix products, arithmetic and copies ran while one was open for 2% -> 2% of each run, Pallas kernels for 17% -> 18%
where the time goes in v4:
time: 189 us; the launch traced here: 188 us
  waiting for transfers between devices  76.8 us (41%)
  starting transfers between devices  60.7 us (32%)
  Pallas kernels  39.9 us (21%)
  local copies, waits for them, and re-layouts  5.45 us (3%)
  other arithmetic  4.15 us (2%)
    ppermute x22, waiting for transfers between devices, hop_z(): return lax.ppermute(value, 'dp', [(i, i ^ step) for i in range(CHIPS)])  42.5 us
    pallas_call x19, Pallas kernels, call(): pl.pallas_call(body, out_shape=[jax.ShapeDtypeStruct(s, t) for s, t in ou...  39.9 us
    ppermute x22, starting transfers between devices, hop_z(): return lax.ppermute(value, 'dp', [(i, i ^ step) for i in range(CHIPS)])  34.4 us
    ppermute x11, starting transfers between devices, hop_second(): lax.ppermute(value, AXES, [(i, i ^ (2 if i % 2 else 4)) for i in range(2...  15.5 us
    ppermute x7, waiting for transfers between devices, hop_first(): lax.ppermute(value, AXES, [(i, i ^ (4 if i % 2 else 2)) for i in range(2...  14.3 us
    ppermute x11, waiting for transfers between devices, hop_second(): lax.ppermute(value, AXES, [(i, i ^ (2 if i % 2 else 4)) for i in range(2...  12.5 us
    ppermute x7, starting transfers between devices, hop_first(): lax.ppermute(value, AXES, [(i, i ^ (4 if i % 2 else 2)) for i in range(2...  9.28 us
    ppermute x14, waiting for transfers between devices, swap(): return lax.ppermute(value, 'fsdp', [(0, 1), (1, 0)])  7.48 us
  transfers between devices with their start and end apart: 54, of which 29 were waited for; matrix products, arithmetic and copies ran while one was open for 2% of the time, Pallas kernels for 18%

profile of v4, /device:TPU:0, one launch (start us, length us, event | category | flops | bytes accessed | tf_op | source)
XLA Modules:
  0.0 188.5 jit_solution(6287569366105300599)
XLA Ops:
  2.6 4.1 %collective-permute-start.4 = (bf16[96,768]{1,0:T(8,128)(2,1)S(1)}, bf16[96,768]{1,0:T(8,128)(2,1)S(1)}, u32[]{:S(2)}, u32[]{:S(2)}) collective-permute-start(bf16[96,768]{1,0:T(8,128)(2,1)S(1)} %pad_maximum_fusion.3), channel_id=1, source_target_pairs={{0,16},{2,18},{4,20},{6,22},{8,24},{10,26},{12,28},{14,30},{16,0},... | collective-permute-start | bytes 442376 | tf_op jit(solution)/shard_map/ppermute | solution.py:665
  14.3 5.4 %collective-permute-done.5 = bf16[96,768]{1,0:T(8,128)(2,1)S(1)} collective-permute-done((bf16[96,768]{1,0:T(8,128)(2,1)S(1)}, bf16[96,768]{1,0:T(8,128)(2,1)S(1)}, u32[]{:S(2)}, u32[]{:S(2)}) %collective-permute-start.5) | collective-permute-done | bytes 147488 | tf_op jit(solution)/shard_map/ppermute | solution.py:665
  22.7 4.0 %collective-permute-done.17 = bf16[96,768]{1,0:T(8,128)(2,1)S(1)} collective-permute-done((bf16[96,768]{1,0:T(8,128)(2,1)S(1)}, bf16[96,768]{1,0:T(8,128)(2,1)S(1)}, u32[]{:S(2)}, u32[]{:S(2)}) %collective-permute-start.17) | collective-permute-done | bytes 147488 | tf_op jit(solution)/shard_map/ppermute | solution.py:665
  27.5 3.1 %collective-permute-start.22 = (bf16[96,768]{1,0:T(8,128)(2,1)S(1)}, bf16[96,768]{1,0:T(8,128)(2,1)S(1)}, u32[]{:S(2)}, u32[]{:S(2)}) collective-permute-start(bf16[96,768]{1,0:T(8,128)(2,1)S(1)} %convert_element_type.78), channel_id=1, source_target_pairs={{0,16},{2,18},{4,20},{6,22},{8,24},{10,26},{12,28},{14,30},{16,0},... | collective-permute-start | bytes 442376 | tf_op jit(solution)/shard_map/ppermute | solution.py:665
  32.2 5.4 %collective-permute-done.18 = bf16[192,768]{1,0:T(8,128)(2,1)S(1)} collective-permute-done((bf16[192,768]{1,0:T(8,128)(2,1)S(1)}, bf16[192,768]{1,0:T(8,128)(2,1)S(1)}, u32[]{:S(2)}, u32[]{:S(2)}) %collective-permute-start.18) | collective-permute-done | bytes 294944 | tf_op jit(solution)/shard_map/ppermute | solution.py:665
  43.6 5.5 %collective-permute-done.23 = bf16[192,768]{1,0:T(8,128)(2,1)} collective-permute-done((bf16[192,768]{1,0:T(8,128)(2,1)S(1)}, bf16[192,768]{1,0:T(8,128)(2,1)}, u32[]{:S(2)}, u32[]{:S(2)}) %collective-permute-start.23) | collective-permute-done | bytes 294944 | tf_op jit(solution)/shard_map/ppermute | solution.py:665
  51.6 2.3 %collective-permute-start.20 = (bf16[288,768]{1,0:T(8,128)(2,1)}, bf16[288,768]{1,0:T(8,128)(2,1)S(1)}, u32[]{:S(2)}, u32[]{:S(2)}) collective-permute-start(bf16[288,768]{1,0:T(8,128)(2,1)} %copy-done.3), channel_id=1, source_target_pairs={{0,4},{1,3},{2,6},{3,1},{4,0},{5,7},{6,2},{7,5},{8,12},{9,11},{10,... | collective-permute-start | bytes 1327112 | tf_op jit(solution)/shard_map/ppermute | solution.py:661
  54.1 1.9 %collective-permute-start.21 = (bf16[288,768]{1,0:T(8,128)(2,1)}, bf16[288,768]{1,0:T(8,128)(2,1)S(1)}, u32[]{:S(2)}, u32[]{:S(2)}) collective-permute-start(bf16[288,768]{1,0:T(8,128)(2,1)} %copy-done.7), channel_id=1, source_target_pairs={{0,4},{1,3},{2,6},{3,1},{4,0},{5,7},{6,2},{7,5},{8,12},{9,11},{10,... | collective-permute-start | bytes 1327112 | tf_op jit(solution)/shard_map/ppermute | solution.py:661
  57.2 6.3 %attend_forward.1 = (f32[2304,256]{1,0:T(8,128)S(1)}, f32[768,256]{1,0:T(8,128)S(1)}, f32[16,256]{1,0:T(8,128)S(1)}, bf16[1536,256]{1,0:T(8,128)(2,1)S(1)}, bf16[1536,256]{1,0:T(8,128)(2,1)S(1)}) custom-call(s32[1,6]{1,0:T(1,128)S(1)} %copy-done.30, s32[2]{0:T(128)S(1)} %pad_add_fusion.me, bf16[256,768]{1,0:T(8,128)(2,1)S(1)} %copy-done.1, ...), custom_call_target="tpu_custom_call" | custom-call | flops 650000000 | tf_op jit(solution)/shard_map/attend_forward/pallas_call | solution.py:317
  64.3 2.4 %collective-permute-start.25 = (bf16[288,768]{1,0:T(8,128)(2,1)S(1)}, bf16[288,768]{1,0:T(8,128)(2,1)S(1)}, u32[]{:S(2)}, u32[]{:S(2)}) collective-permute-start(bf16[288,768]{1,0:T(8,128)(2,1)S(1)} %constant_dynamic-update-slice_fusion.5.z0), channel_id=1, source_target_pairs={{0,4},{1,3},{2,6},{3,1},{4,0},{5,7},{6,2},{7,5},{8,12},{9,11},{10,... | collective-permute-start | bytes 1327112 | tf_op jit(solution)/shard_map/ppermute | solution.py:661
  66.7 3.9 %attend_close.1 = (f32[256,768]{1,0:T(8,128)S(1)}, bf16[256,768]{1,0:T(8,128)(2,1)S(1)}, f32[256,768]{1,0:T(8,128)S(1)}, f32[256,1]{1,0:T(8,128)S(1)}) custom-call(bf16[256,768]{1,0:T(8,128)(2,1)S(1)} %copy-done.1, bf16[1536,256]{1,0:T(8,128)(2,1)S(1)} %get-tuple-element.95.rel_own.ata, bf16[1536,256]{1,0:T(8,128)(2,1)S(1)} %get-tuple-element.96.rel_par, ...), custom_call_target="tpu_custom_call" | custom-call | flops 360000000 | tf_op jit(solution)/shard_map/attend_close/pallas_call | solution.py:317
  71.4 1.7 collective-permute-done.15.yb.zb
  73.1 2.5 %feed_up.1 = (bf16[1536,512]{1,0:T(8,128)(2,1)S(1)}, f32[1536,512]{1,0:T(8,128)S(1)}) custom-call(bf16[256,768]{1,0:T(8,128)(2,1)S(1)} %get-tuple-element.98.ya.za, bf16[256,768]{1,0:T(8,128)(2,1)S(1)} %collective-permute-done.15.yb.zb, bf16[384,768]{1,0:T(8,128)(2,1)S(1)} %copy-done.6, bf16[288,768]{1,0:T(8,128)(2,1)S(1)} %copy-done.4, ...), custom_call_target="tpu_custom_call" | custom-call | flops 250000000 | tf_op jit(solution)/shard_map/feed_up/pallas_call | solution.py:317
  75.7 3.6 %collective-permute-done.26.z3 = bf16[288,768]{1,0:T(8,128)(2,1)S(1)} collective-permute-done((bf16[288,768]{1,0:T(8,128)(2,1)S(1)}, bf16[288,768]{1,0:T(8,128)(2,1)S(1)}, u32[]{:S(2)}, u32[]{:S(2)}) %collective-permute-start.26) | collective-permute-done | bytes 442400 | tf_op jit(solution)/shard_map/ppermute | solution.py:661
  89.3 2.6 %feed_back.1 = (bf16[1536,512]{1,0:T(8,128)(2,1)S(1)}, f32[256,768]{1,0:T(8,128)S(1)}, f32[256,768]{1,0:T(8,128)S(1)}) custom-call(f32[1536,512]{1,0:T(8,128)S(1)} %get-tuple-element.117.slope, bf16[256,768]{1,0:T(8,128)(2,1)S(1)} %get-tuple-element.120.za, bf16[256,768]{1,0:T(8,128)(2,1)S(1)} %collective-permute-done.28.zb, ...), custom_call_target="tpu_custom_call" | custom-call | tf_op jit(solution)/shard_map/feed_back/pallas_call | solution.py:317
  94.3 7.0 %attend_backward.1 = (f32[256,768]{1,0:T(8,128)S(1)}, bf16[256,768]{1,0:T(8,128)(2,1)S(1)}, f32[2,768]{1,0:T(2,128)S(1)}, bf16[1536,256]{1,0:T(8,128)(2,1)S(1)}, bf16[1536,256]{1,0:T(8,128)(2,1)S(1)}) custom-call(s32[1,6]{1,0:T(1,128)S(1)} %copy-done.30, s32[2]{0:T(128)S(1)} %pad_add_fusion.me, f32[256,768]{1,0:T(8,128)S(1)} %get-tuple-element.116.ds2, ...), custom_call_target="tpu_custom_call" | custom-call | tf_op jit(solution)/shard_map/attend_backward/pallas_call | solution.py:317
  104.3 1.7 collective-permute-done.31.dob
  107.7 11.3 %collective-permute-done.33 = bf16[384,768]{1,0:T(8,128)(2,1)S(1)} collective-permute-done((bf16[384,768]{1,0:T(8,128)(2,1)S(1)}, bf16[384,768]{1,0:T(8,128)(2,1)S(1)}, u32[]{:S(2)}, u32[]{:S(2)}) %collective-permute-start.33) | collective-permute-done | bytes 589856 | tf_op jit(solution)/shard_map/ppermute | solution.py:657
  123.2 4.4 %grad_input.1 = f32[256,768]{1,0:T(8,128)} custom-call(f32[256,768]{1,0:T(8,128)S(1)} %get-tuple-element.132.dh, bf16[1536,256]{1,0:T(8,128)(2,1)S(1)} %get-tuple-element.133.dma.rel_own, bf16[1536,256]{1,0:T(8,128)(2,1)S(1)} %get-tuple-element.130.rel_par, bf16[384,768]{1,0:T(8,128)(2,1)S(1)} %get-tuple-element.92.so, ...), custom_call_target="tpu_custom_call" | custom-call | tf_op jit(solution)/shard_map/grad_input/pallas_call | solution.py:317
  129.3 2.6 %collective-permute-start.45 = (bf16[96,768]{1,0:T(8,128)(2,1)S(1)}, bf16[96,768]{1,0:T(8,128)(2,1)S(1)}, u32[]{:S(2)}, u32[]{:S(2)}) collective-permute-start(bf16[96,768]{1,0:T(8,128)(2,1)S(1)} %get-tuple-element.170), channel_id=1, source_target_pairs={{0,16},{2,18},{4,20},{6,22},{8,24},{10,26},{12,28},{14,30},{16,0},... | collective-permute-start | bytes 442376 | tf_op jit(solution)/shard_map/ppermute | solution.py:665
  131.9 2.0 %collective-permute-start.46 = (bf16[96,768]{1,0:T(8,128)(2,1)S(1)}, bf16[96,768]{1,0:T(8,128)(2,1)S(1)}, u32[]{:S(2)}, u32[]{:S(2)}) collective-permute-start(bf16[96,768]{1,0:T(8,128)(2,1)S(1)} %get-tuple-element.171), channel_id=1, source_target_pairs={{0,24},{2,26},{4,28},{6,30},{8,16},{10,18},{12,20},{14,22},{16,8},... | collective-permute-start | bytes 442376 | tf_op jit(solution)/shard_map/ppermute | solution.py:665
  134.4 7.1 %collective-permute-done.34 = bf16[768,768]{1,0:T(8,128)(2,1)S(1)} collective-permute-done((bf16[768,768]{1,0:T(8,128)(2,1)S(1)}, bf16[768,768]{1,0:T(8,128)(2,1)S(1)}, u32[]{:S(2)}, u32[]{:S(2)}) %collective-permute-start.34) | collective-permute-done | bytes 1179680 | tf_op jit(solution)/shard_map/ppermute | solution.py:661
  143.5 2.6 %collective-permute-start.43 = (bf16[96,768]{1,0:T(8,128)(2,1)S(1)}, bf16[96,768]{1,0:T(8,128)(2,1)S(1)}, u32[]{:S(2)}, u32[]{:S(2)}) collective-permute-start(bf16[96,768]{1,0:T(8,128)(2,1)S(1)} %get-tuple-element.173), channel_id=1, source_target_pairs={{0,16},{2,18},{4,20},{6,22},{8,24},{10,26},{12,28},{14,30},{16,0},... | collective-permute-start | bytes 442376 | tf_op jit(solution)/shard_map/ppermute | solution.py:665
  146.1 2.0 %collective-permute-start.44 = (bf16[96,768]{1,0:T(8,128)(2,1)S(1)}, bf16[96,768]{1,0:T(8,128)(2,1)S(1)}, u32[]{:S(2)}, u32[]{:S(2)}) collective-permute-start(bf16[96,768]{1,0:T(8,128)(2,1)S(1)} %get-tuple-element.174), channel_id=1, source_target_pairs={{0,24},{2,26},{4,28},{6,30},{8,16},{10,18},{12,20},{14,22},{16,8},... | collective-permute-start | bytes 442376 | tf_op jit(solution)/shard_map/ppermute | solution.py:665
  148.7 2.9 %collective-permute-done.35 = bf16[384,768]{1,0:T(8,128)(2,1)S(1)} collective-permute-done((bf16[384,768]{1,0:T(8,128)(2,1)S(1)}, bf16[384,768]{1,0:T(8,128)(2,1)S(1)}, u32[]{:S(2)}, u32[]{:S(2)}) %collective-permute-start.35) | collective-permute-done | bytes 589856 | tf_op jit(solution)/shard_map/ppermute | solution.py:657
  151.7 4.4 %collective-permute-done.39 = bf16[96,768]{1,0:T(8,128)(2,1)S(1)} collective-permute-done((bf16[96,768]{1,0:T(8,128)(2,1)S(1)}, bf16[96,768]{1,0:T(8,128)(2,1)S(1)}, u32[]{:S(2)}, u32[]{:S(2)}) %collective-permute-start.39) | collective-permute-done | bytes 147488 | tf_op jit(solution)/shard_map/ppermute | solution.py:665
  156.2 3.2 %collective-permute-start.42 = (bf16[96,768]{1,0:T(8,128)(2,1)S(1)}, bf16[96,768]{1,0:T(8,128)(2,1)S(1)}, u32[]{:S(2)}, u32[]{:S(2)}) collective-permute-start(bf16[96,768]{1,0:T(8,128)(2,1)S(1)} %get-tuple-element.176), channel_id=1, source_target_pairs={{0,24},{2,26},{4,28},{6,30},{8,16},{10,18},{12,20},{14,22},{16,8},... | collective-permute-start | bytes 442376 | tf_op jit(solution)/shard_map/ppermute | solution.py:665
  160.9 3.9 %collective-permute-done.42.c1 = bf16[96,768]{1,0:T(8,128)(2,1)S(1)} collective-permute-done((bf16[96,768]{1,0:T(8,128)(2,1)S(1)}, bf16[96,768]{1,0:T(8,128)(2,1)S(1)}, u32[]{:S(2)}, u32[]{:S(2)}) %collective-permute-start.42) | collective-permute-done | bytes 147488 | tf_op jit(solution)/shard_map/ppermute | solution.py:665
  166.0 4.5 %collective-permute-done.40.a1 = bf16[96,768]{1,0:T(8,128)(2,1)S(1)} collective-permute-done((bf16[96,768]{1,0:T(8,128)(2,1)S(1)}, bf16[96,768]{1,0:T(8,128)(2,1)S(1)}, u32[]{:S(2)}, u32[]{:S(2)}) %collective-permute-start.40) | collective-permute-done | bytes 147488 | tf_op jit(solution)/shard_map/ppermute | solution.py:665
  177.8 3.3 %collective-permute-start.53 = (f32[8,768]{1,0:T(8,128)S(1)}, f32[8,768]{1,0:T(8,128)S(1)}, u32[]{:S(2)}, u32[]{:S(2)}) collective-permute-start(f32[8,768]{1,0:T(8,128)S(1)} %add_add_fusion.n0), channel_id=1, source_target_pairs={{0,24},{2,26},{4,28},{6,30},{8,16},{10,18},{12,20},{14,22},{16,8},... | collective-permute-start | bytes 73736 | tf_op jit(solution)/shard_map/ppermute | solution.py:665
  183.6 2.2 %collective-permute-done.52.n2 = f32[8,768]{1,0:T(8,128)S(1)} collective-permute-done((f32[8,768]{1,0:T(8,128)S(1)}, f32[8,768]{1,0:T(8,128)S(1)}, u32[]{:S(2)}, u32[]{:S(2)}) %collective-permute-start.52) | collective-permute-done | bytes 24608 | tf_op jit(solution)/shard_map/ppermute | solution.py:665
  186.0 2.3 %update.1 = (f32[1,1]{1,0:T(1,128)}, f32[72,768]{1,0:T(8,128)}, f32[24,768]{1,0:T(8,128)}, f32[96,768]{1,0:T(8,128)}, f32[96,768]{1,0:T(8,128)}, /*index=5*/f32[...) custom-call(f32[8,768]{1,0:T(8,128)S(1)} %add_add_fusion.n0, ...), custom_call_target="tpu_custom_call" | custom-call | tf_op jit(solution)/shard_map/update/pallas_call | solution.py:317
  (187 shorter events, 64.6 us)
Async XLA Ops:
  2.6 11.2 %collective-permute-start.4 = (bf16[96,768]{1,0:T(8,128)(2,1)S(1)}, bf16[96,768]{1,0:T(8,128)(2,1)S(1)}, u32[]{:S(2)}, u32[]{:S(2)}) collective-permute-start(bf16[96,768]{1,0:T(8,128)(2,1)S(1)} %pad_maximum_fusion.3), channel_id=1, source_target_pairs={{0,16},{2,18},{4,20},{6,22},{8,24},{10,26},{12,28},{14,30},{16,0},... | collective-permute-start | bytes 442376 | tf_op jit(solution)/shard_map/ppermute | solution.py:665
  7.7 12.9 %collective-permute-start.2 = (bf16[288,768]{1,0:T(8,128)(2,1)S(1)}, bf16[288,768]{1,0:T(8,128)(2,1)S(1)}, u32[]{:S(2)}, u32[]{:S(2)}) collective-permute-start(bf16[288,768]{1,0:T(8,128)(2,1)S(1)} %pad_maximum_fusion.s0), channel_id=1, source_target_pairs={{0,4},{1,3},{2,6},{3,1},{4,0},{5,7},{6,2},{7,5},{8,12},{9,11},{10,... | collective-permute-start | bytes 1327112 | tf_op jit(solution)/shard_map/ppermute | solution.py:661
  9.3 12.3 %collective-permute-start.1 = (bf16[288,768]{1,0:T(8,128)(2,1)S(1)}, bf16[288,768]{1,0:T(8,128)(2,1)S(1)}, u32[]{:S(2)}, u32[]{:S(2)}) collective-permute-start(bf16[288,768]{1,0:T(8,128)(2,1)S(1)} %pad_maximum_fusion.s0), channel_id=1, source_target_pairs={{0,2},{1,5},{2,0},{3,7},{4,6},{5,1},{6,4},{7,3},{8,10},{9,13},{10,... | collective-permute-start | bytes 1327112 | tf_op jit(solution)/shard_map/ppermute | solution.py:657
  10.8 8.9 %collective-permute-start.5 = (bf16[96,768]{1,0:T(8,128)(2,1)S(1)}, bf16[96,768]{1,0:T(8,128)(2,1)S(1)}, u32[]{:S(2)}, u32[]{:S(2)}) collective-permute-start(bf16[96,768]{1,0:T(8,128)(2,1)S(1)} %pad_maximum_fusion.3), channel_id=1, source_target_pairs={{0,8},{2,10},{4,12},{6,14},{8,0},{10,2},{12,4},{14,6},{16,24},{18,... | collective-permute-start | bytes 442376 | tf_op jit(solution)/shard_map/ppermute | solution.py:665
  13.8 13.0 %collective-permute-start.17 = (bf16[96,768]{1,0:T(8,128)(2,1)S(1)}, bf16[96,768]{1,0:T(8,128)(2,1)S(1)}, u32[]{:S(2)}, u32[]{:S(2)}) collective-permute-start(bf16[96,768]{1,0:T(8,128)(2,1)S(1)} %bitcast_convert_fusion), channel_id=1, source_target_pairs={{0,16},{2,18},{4,20},{6,22},{8,24},{10,26},{12,28},{14,30},{16,0},... | collective-permute-start | bytes 442376 | tf_op jit(solution)/shard_map/ppermute | solution.py:665
  20.7 17.0 %collective-permute-start.7 = (bf16[288,768]{1,0:T(8,128)(2,1)S(1)}, bf16[288,768]{1,0:T(8,128)(2,1)S(1)}, u32[]{:S(2)}, u32[]{:S(2)}) collective-permute-start(bf16[288,768]{1,0:T(8,128)(2,1)S(1)} %constant_dynamic-update-slice_fusion.z0), channel_id=1, source_target_pairs={{0,2},{1,5},{2,0},{3,7},{4,6},{5,1},{6,4},{7,3},{8,10},{9,13},{10,... | collective-permute-start | bytes 1327112 | tf_op jit(solution)/shard_map/ppermute | solution.py:657
  21.6 17.6 %collective-permute-start.3 = (bf16[288,768]{1,0:T(8,128)(2,1)S(1)}, bf16[288,768]{1,0:T(8,128)(2,1)S(1)}, u32[]{:S(2)}, u32[]{:S(2)}) collective-permute-start(bf16[288,768]{1,0:T(8,128)(2,1)S(1)} %collective-permute-done.1.s1), channel_id=1, source_target_pairs={{0,4},{1,3},{2,6},{3,1},{4,0},{5,7},{6,2},{7,5},{8,12},{9,11},{10,... | collective-permute-start | bytes 1327112 | tf_op jit(solution)/shard_map/ppermute | solution.py:661
  26.8 10.8 %collective-permute-start.18 = (bf16[192,768]{1,0:T(8,128)(2,1)S(1)}, bf16[192,768]{1,0:T(8,128)(2,1)S(1)}, u32[]{:S(2)}, u32[]{:S(2)}) collective-permute-start(bf16[192,768]{1,0:T(8,128)(2,1)S(1)} %pad_maximum_fusion.1), channel_id=1, source_target_pairs={{0,8},{2,10},{4,12},{6,14},{8,0},{10,2},{12,4},{14,6},{16,24},{18,... | collective-permute-start | bytes 884744 | tf_op jit(solution)/shard_map/ppermute | solution.py:665
  27.5 11.8 %collective-permute-start.22 = (bf16[96,768]{1,0:T(8,128)(2,1)S(1)}, bf16[96,768]{1,0:T(8,128)(2,1)S(1)}, u32[]{:S(2)}, u32[]{:S(2)}) collective-permute-start(bf16[96,768]{1,0:T(8,128)(2,1)S(1)} %convert_element_type.78), channel_id=1, source_target_pairs={{0,16},{2,18},{4,20},{6,22},{8,24},{10,26},{12,28},{14,30},{16,0},... | collective-permute-start | bytes 442376 | tf_op jit(solution)/shard_map/ppermute | solution.py:665
  30.6 18.5 %collective-permute-start.8 = (bf16[288,768]{1,0:T(8,128)(2,1)S(1)}, bf16[288,768]{1,0:T(8,128)(2,1)S(1)}, u32[]{:S(2)}, u32[]{:S(2)}) collective-permute-start(bf16[288,768]{1,0:T(8,128)(2,1)S(1)} %constant_dynamic-update-slice_fusion.z0), channel_id=1, source_target_pairs={{0,4},{1,3},{2,6},{3,1},{4,0},{5,7},{6,2},{7,5},{8,12},{9,11},{10,... | collective-permute-start | bytes 1327112 | tf_op jit(solution)/shard_map/ppermute | solution.py:661
  37.6 12.1 %collective-permute-start.19 = (bf16[288,768]{1,0:T(8,128)(2,1)S(1)}, bf16[288,768]{1,0:T(8,128)(2,1)S(1)}, u32[]{:S(2)}, u32[]{:S(2)}) collective-permute-start(bf16[288,768]{1,0:T(8,128)(2,1)S(1)} %constant_dynamic-update-slice_fusion.3.z0), channel_id=1, source_target_pairs={{0,2},{1,5},{2,0},{3,7},{4,6},{5,1},{6,4},{7,3},{8,10},{9,13},{10,... | collective-permute-start | bytes 1327112 | tf_op jit(solution)/shard_map/ppermute | solution.py:657
  39.2 10.5 %collective-permute-start.9 = (bf16[288,768]{1,0:T(8,128)(2,1)S(1)}, bf16[288,768]{1,0:T(8,128)(2,1)S(1)}, u32[]{:S(2)}, u32[]{:S(2)}) collective-permute-start(bf16[288,768]{1,0:T(8,128)(2,1)S(1)} %collective-permute-done.7.z1), channel_id=1, source_target_pairs={{0,4},{1,3},{2,6},{3,1},{4,0},{5,7},{6,2},{7,5},{8,12},{9,11},{10,... | collective-permute-start | bytes 1327112 | tf_op jit(solution)/shard_map/ppermute | solution.py:661
  39.4 9.7 %collective-permute-start.23 = (bf16[192,768]{1,0:T(8,128)(2,1)S(1)}, bf16[192,768]{1,0:T(8,128)(2,1)}, u32[]{:S(2)}, u32[]{:S(2)}) collective-permute-start(bf16[192,768]{1,0:T(8,128)(2,1)S(1)} %pad_maximum_fusion.2), channel_id=1, source_target_pairs={{0,8},{2,10},{4,12},{6,14},{8,0},{10,2},{12,4},{14,6},{16,24},{18,... | collective-permute-start | bytes 884744 | tf_op jit(solution)/shard_map/ppermute | solution.py:665
  43.5 12.6 %collective-permute-start.10 = (bf16[384,768]{1,0:T(8,128)(2,1)S(1)}, bf16[384,768]{1,0:T(8,128)(2,1)S(1)}, u32[]{:S(2)}, u32[]{:S(2)}) collective-permute-start(bf16[384,768]{1,0:T(8,128)(2,1)S(1)} %get-tuple-element.92.so), channel_id=1, source_target_pairs={{0,1},{1,0},{2,3},{3,2},{4,5},{5,4},{6,7},{7,6},{8,9},{9,8},{10,11... | collective-permute-start | bytes 1769480 | tf_op jit(solution)/shard_map/ppermute | solution.py:653
  51.6 12.7 %collective-permute-start.20 = (bf16[288,768]{1,0:T(8,128)(2,1)}, bf16[288,768]{1,0:T(8,128)(2,1)S(1)}, u32[]{:S(2)}, u32[]{:S(2)}) collective-permute-start(bf16[288,768]{1,0:T(8,128)(2,1)} %copy-done.3), channel_id=1, source_target_pairs={{0,4},{1,3},{2,6},{3,1},{4,0},{5,7},{6,2},{7,5},{8,12},{9,11},{10,... | collective-permute-start | bytes 1327112 | tf_op jit(solution)/shard_map/ppermute | solution.py:661
  53.9 16.7 %collective-permute-start.24 = (bf16[288,768]{1,0:T(8,128)(2,1)S(1)}, bf16[288,768]{1,0:T(8,128)(2,1)S(1)}, u32[]{:S(2)}, u32[]{:S(2)}) collective-permute-start(bf16[288,768]{1,0:T(8,128)(2,1)S(1)} %constant_dynamic-update-slice_fusion.5.z0), channel_id=1, source_target_pairs={{0,2},{1,5},{2,0},{3,7},{4,6},{5,1},{6,4},{7,3},{8,10},{9,13},{10,... | collective-permute-start | bytes 1327112 | tf_op jit(solution)/shard_map/ppermute | solution.py:657
  54.1 16.4 %collective-permute-start.21 = (bf16[288,768]{1,0:T(8,128)(2,1)}, bf16[288,768]{1,0:T(8,128)(2,1)S(1)}, u32[]{:S(2)}, u32[]{:S(2)}) collective-permute-start(bf16[288,768]{1,0:T(8,128)(2,1)} %copy-done.7), channel_id=1, source_target_pairs={{0,4},{1,3},{2,6},{3,1},{4,0},{5,7},{6,2},{7,5},{8,12},{9,11},{10,... | collective-permute-start | bytes 1327112 | tf_op jit(solution)/shard_map/ppermute | solution.py:661
  63.5 9.7 %collective-permute-start.16 = (bf16[1536,256]{1,0:T(8,128)(2,1)S(1)}, bf16[1536,256]{1,0:T(8,128)(2,1)S(1)}, u32[]{:S(2)}, u32[]{:S(2)}) collective-permute-start(bf16[1536,256]{1,0:T(8,128)(2,1)S(1)} %get-tuple-element.96.rel_par), channel_id=1, source_target_pairs={{0,1},{1,0},{2,3},{3,2},{4,5},{5,4},{6,7},{7,6},{8,9},{9,8},{10,11... | collective-permute-start | bytes 2359304 | tf_op jit(solution)/shard_map/ppermute | solution.py:653
  64.3 11.4 %collective-permute-start.25 = (bf16[288,768]{1,0:T(8,128)(2,1)S(1)}, bf16[288,768]{1,0:T(8,128)(2,1)S(1)}, u32[]{:S(2)}, u32[]{:S(2)}) collective-permute-start(bf16[288,768]{1,0:T(8,128)(2,1)S(1)} %constant_dynamic-update-slice_fusion.5.z0), channel_id=1, source_target_pairs={{0,4},{1,3},{2,6},{3,1},{4,0},{5,7},{6,2},{7,5},{8,12},{9,11},{10,... | collective-permute-start | bytes 1327112 | tf_op jit(solution)/shard_map/ppermute | solution.py:661
  70.6 8.8 %collective-permute-start.26 = (bf16[288,768]{1,0:T(8,128)(2,1)S(1)}, bf16[288,768]{1,0:T(8,128)(2,1)S(1)}, u32[]{:S(2)}, u32[]{:S(2)}) collective-permute-start(bf16[288,768]{1,0:T(8,128)(2,1)S(1)} %collective-permute-done.24.z1), channel_id=1, source_target_pairs={{0,4},{1,3},{2,6},{3,1},{4,0},{5,7},{6,2},{7,5},{8,12},{9,11},{10,... | collective-permute-start | bytes 1327112 | tf_op jit(solution)/shard_map/ppermute | solution.py:661
  86.2 16.3 %collective-permute-start.32 = (bf16[768,768]{1,0:T(8,128)(2,1)S(1)}, bf16[768,768]{1,0:T(8,128)(2,1)S(1)}, u32[]{:S(2)}, u32[]{:S(2)}) collective-permute-start(bf16[768,768]{1,0:T(8,128)(2,1)S(1)} %grad_down_away.1), channel_id=1, source_target_pairs={{0,4},{1,3},{2,6},{3,1},{4,0},{5,7},{6,2},{7,5},{8,12},{9,11},{10,... | collective-permute-start | bytes 3538952 | tf_op jit(solution)/shard_map/ppermute | solution.py:661
  92.8 28.6 %collective-permute-start.36 = (bf16[768,768]{1,0:T(8,128)(2,1)S(1)}, bf16[768,768]{1,0:T(8,128)(2,1)S(1)}, u32[]{:S(2)}, u32[]{:S(2)}) collective-permute-start(bf16[768,768]{1,0:T(8,128)(2,1)S(1)} %grad_up_away.1), channel_id=1, source_target_pairs={{0,4},{1,3},{2,6},{3,1},{4,0},{5,7},{6,2},{7,5},{8,12},{9,11},{10,... | collective-permute-start | bytes 3538952 | tf_op jit(solution)/shard_map/ppermute | solution.py:661
  102.6 16.3 %collective-permute-start.33 = (bf16[384,768]{1,0:T(8,128)(2,1)S(1)}, bf16[384,768]{1,0:T(8,128)(2,1)S(1)}, u32[]{:S(2)}, u32[]{:S(2)}) collective-permute-start(bf16[384,768]{1,0:T(8,128)(2,1)S(1)} %add_convert_fusion.2), channel_id=1, source_target_pairs={{0,2},{1,5},{2,0},{3,7},{4,6},{5,1},{6,4},{7,3},{8,10},{9,13},{10,... | collective-permute-start | bytes 1769480 | tf_op jit(solution)/shard_map/ppermute | solution.py:657
  119.0 22.5 %collective-permute-start.34 = (bf16[768,768]{1,0:T(8,128)(2,1)S(1)}, bf16[768,768]{1,0:T(8,128)(2,1)S(1)}, u32[]{:S(2)}, u32[]{:S(2)}) collective-permute-start(bf16[768,768]{1,0:T(8,128)(2,1)S(1)} %mix_away.1), channel_id=1, source_target_pairs={{0,4},{1,3},{2,6},{3,1},{4,0},{5,7},{6,2},{7,5},{8,12},{9,11},{10,... | collective-permute-start | bytes 3538952 | tf_op jit(solution)/shard_map/ppermute | solution.py:661
  121.6 21.7 %collective-permute-start.37 = (bf16[384,768]{1,0:T(8,128)(2,1)S(1)}, bf16[384,768]{1,0:T(8,128)(2,1)S(1)}, u32[]{:S(2)}, u32[]{:S(2)}) collective-permute-start(bf16[384,768]{1,0:T(8,128)(2,1)S(1)} %add_convert_fusion), channel_id=1, source_target_pairs={{0,2},{1,5},{2,0},{3,7},{4,6},{5,1},{6,4},{7,3},{8,10},{9,13},{10,... | collective-permute-start | bytes 1769480 | tf_op jit(solution)/shard_map/ppermute | solution.py:657
  129.3 18.8 %collective-permute-start.45 = (bf16[96,768]{1,0:T(8,128)(2,1)S(1)}, bf16[96,768]{1,0:T(8,128)(2,1)S(1)}, u32[]{:S(2)}, u32[]{:S(2)}) collective-permute-start(bf16[96,768]{1,0:T(8,128)(2,1)S(1)} %get-tuple-element.170), channel_id=1, source_target_pairs={{0,16},{2,18},{4,20},{6,22},{8,24},{10,26},{12,28},{14,30},{16,0},... | collective-permute-start | bytes 442376 | tf_op jit(solution)/shard_map/ppermute | solution.py:665
  131.9 16.7 %collective-permute-start.46 = (bf16[96,768]{1,0:T(8,128)(2,1)S(1)}, bf16[96,768]{1,0:T(8,128)(2,1)S(1)}, u32[]{:S(2)}, u32[]{:S(2)}) collective-permute-start(bf16[96,768]{1,0:T(8,128)(2,1)S(1)} %get-tuple-element.171), channel_id=1, source_target_pairs={{0,24},{2,26},{4,28},{6,30},{8,16},{10,18},{12,20},{14,22},{16,8},... | collective-permute-start | bytes 442376 | tf_op jit(solution)/shard_map/ppermute | solution.py:665
  133.9 9.6 %collective-permute-start.38 = (bf16[96,768]{1,0:T(8,128)(2,1)S(1)}, bf16[96,768]{1,0:T(8,128)(2,1)S(1)}, u32[]{:S(2)}, u32[]{:S(2)}) collective-permute-start(bf16[96,768]{1,0:T(8,128)(2,1)S(1)} %get-tuple-element.172), channel_id=1, source_target_pairs={{0,8},{2,10},{4,12},{6,14},{8,0},{10,2},{12,4},{14,6},{16,24},{18,... | collective-permute-start | bytes 442376 | tf_op jit(solution)/shard_map/ppermute | solution.py:665
  141.6 9.9 %collective-permute-start.35 = (bf16[384,768]{1,0:T(8,128)(2,1)S(1)}, bf16[384,768]{1,0:T(8,128)(2,1)S(1)}, u32[]{:S(2)}, u32[]{:S(2)}) collective-permute-start(bf16[384,768]{1,0:T(8,128)(2,1)S(1)} %add_convert_fusion.1), channel_id=1, source_target_pairs={{0,2},{1,5},{2,0},{3,7},{4,6},{5,1},{6,4},{7,3},{8,10},{9,13},{10,... | collective-permute-start | bytes 1769480 | tf_op jit(solution)/shard_map/ppermute | solution.py:657
  143.5 17.1 %collective-permute-start.43 = (bf16[96,768]{1,0:T(8,128)(2,1)S(1)}, bf16[96,768]{1,0:T(8,128)(2,1)S(1)}, u32[]{:S(2)}, u32[]{:S(2)}) collective-permute-start(bf16[96,768]{1,0:T(8,128)(2,1)S(1)} %get-tuple-element.173), channel_id=1, source_target_pairs={{0,16},{2,18},{4,20},{6,22},{8,24},{10,26},{12,28},{14,30},{16,0},... | collective-permute-start | bytes 442376 | tf_op jit(solution)/shard_map/ppermute | solution.py:665
  146.1 14.5 %collective-permute-start.44 = (bf16[96,768]{1,0:T(8,128)(2,1)S(1)}, bf16[96,768]{1,0:T(8,128)(2,1)S(1)}, u32[]{:S(2)}, u32[]{:S(2)}) collective-permute-start(bf16[96,768]{1,0:T(8,128)(2,1)S(1)} %get-tuple-element.174), channel_id=1, source_target_pairs={{0,24},{2,26},{4,28},{6,30},{8,16},{10,18},{12,20},{14,22},{16,8},... | collective-permute-start | bytes 442376 | tf_op jit(solution)/shard_map/ppermute | solution.py:665
  159.4 11.1 %collective-permute-start.40 = (bf16[96,768]{1,0:T(8,128)(2,1)S(1)}, bf16[96,768]{1,0:T(8,128)(2,1)S(1)}, u32[]{:S(2)}, u32[]{:S(2)}) collective-permute-start(bf16[96,768]{1,0:T(8,128)(2,1)S(1)} %get-tuple-element.178), channel_id=1, source_target_pairs={{0,16},{2,18},{4,20},{6,22},{8,24},{10,26},{12,28},{14,30},{16,0},... | collective-permute-start | bytes 442376 | tf_op jit(solution)/shard_map/ppermute | solution.py:665
  (53 other events, 555.6 us)

commit v5 on v4

--- a/solution.py
+++ b/solution.py
@@ -257,8 +257,8 @@
     "update": 0.0,
     "grad_up_away": 0.0,
     "grad_up_here": 0.8,
-    "feed_back": 0.0,
-    "mix_away": 0.0,
+    "feed_back": 1.0,
+    "mix_away": 0.4,
     "mix_here": 1.5,
 }
 MB = 16
@@ -711,16 +711,16 @@
     s_first = hop_first(s_all)
     s_second = hop_second(s_all)
     near1, joined1 = z_round(blocks[0], True, ())
-    near2, joined2 = z_round(blocks[1], False, (near1[0],))
+    near2, joined2 = z_round(blocks[1], False, (near1[2],))
     near3, joined3 = z_round(blocks[2], False, (near2[0],))
     s_third = hop_second(s_first)
     s_parts = (s_all, s_first, s_second, s_third)
-    turned1 = hop_first(tie(joined1, s_second))
+    turned1 = hop_first(tie(joined1, s_first, s_second))
     across1 = hop_second(tie(joined1, s_second))
     corner1 = hop_second(tie(turned1, s_third))
-    turned2 = hop_first(tie(joined2, turned1))
+    turned2 = hop_first(tie(joined2, turned1, across1))
     across2 = hop_second(tie(joined2, across1))
-    corner2 = hop_second(tie(turned2, corner1))
+    corner2 = hop_second(tie(turned2, corner1, across2))
     sorted1, sorted2, sorted3 = call(
         sort_near,
         [((PLANE, width), BF)] * 3,
@@ -741,7 +741,7 @@
         smem=2,
     )
     turned3 = hop_first(tie(joined3, turned2))
-    across3 = hop_second(tie(joined3, across2))
+    across3 = hop_second(tie(joined3, across2, den))
     first, first_low, xhat, rstd = call(
         attend_close,
         [((rows, width), F32), ((rows, width), BF), ((rows, width), F32), ((rows, 1), F32)],

time: 189 us -> 187 us (0.989)
  starting transfers between devices: 60.7 us -> 56.4 us
  waiting for transfers between devices: 76.8 us -> 79.5 us
    ppermute x22, waiting for transfers between devices: 42.5 us -> 36.3 us  [hop_z(): return lax.ppermute(value, 'dp', [(i, i ^ step) for i in range(CHIPS)])]
    ppermute x11, waiting for transfers between devices: 12.5 us -> 17 us  [hop_second(): lax.ppermute(value, AXES, [(i, i ^ (2 if i % 2 else 4)) for i in range(2...]
    ppermute x7, waiting for transfers between devices: 14.3 us -> 18.7 us  [hop_first(): lax.ppermute(value, AXES, [(i, i ^ (4 if i % 2 else 2)) for i in range(2...]
    ppermute x11, starting transfers between devices: 15.5 us -> 12.9 us  [hop_second(): lax.ppermute(value, AXES, [(i, i ^ (2 if i % 2 else 4)) for i in range(2...]
    unnamed x66 -> x70, local copies, waits for them, and re-layouts: 4.32 us -> 4.31 us
  transfers between devices with their start and end apart: 54 -> 54, of which waited for: 29 -> 24; matrix products, arithmetic and copies ran while one was open for 2% -> 2% of each run, Pallas kernels for 18% -> 19%
where the time goes in v5:
time: 187 us
  waiting for transfers between devices  79.5 us (43%)
  starting transfers between devices  56.4 us (30%)
  Pallas kernels  40 us (21%)
  local copies, waits for them, and re-layouts  5.44 us (3%)
  other arithmetic  4.2 us (2%)
    pallas_call x19, Pallas kernels, call(): pl.pallas_call(body, out_shape=[jax.ShapeDtypeStruct(s, t) for s, t in ou...  40 us
    ppermute x22, waiting for transfers between devices, hop_z(): return lax.ppermute(value, 'dp', [(i, i ^ step) for i in range(CHIPS)])  36.3 us
    ppermute x22, starting transfers between devices, hop_z(): return lax.ppermute(value, 'dp', [(i, i ^ step) for i in range(CHIPS)])  34.6 us
    ppermute x7, waiting for transfers between devices, hop_first(): lax.ppermute(value, AXES, [(i, i ^ (4 if i % 2 else 2)) for i in range(2...  18.7 us
    ppermute x11, waiting for transfers between devices, hop_second(): lax.ppermute(value, AXES, [(i, i ^ (2 if i % 2 else 4)) for i in range(2...  17 us
    ppermute x11, starting transfers between devices, hop_second(): lax.ppermute(value, AXES, [(i, i ^ (2 if i % 2 else 4)) for i in range(2...  12.9 us
    ppermute x7, starting transfers between devices, hop_first(): lax.ppermute(value, AXES, [(i, i ^ (4 if i % 2 else 2)) for i in range(2...  7.88 us
    ppermute x14, waiting for transfers between devices, swap(): return lax.ppermute(value, 'fsdp', [(0, 1), (1, 0)])  7.48 us
  transfers between devices with their start and end apart: 54, of which 24 were waited for; matrix products, arithmetic and copies ran while one was open for 2% of the time, Pallas kernels for 19%

profile of v5, /device:TPU:0, one launch (start us, length us, event | category | flops | bytes accessed | tf_op | source)
XLA Modules:
  0.0 187.1 jit_solution(12012346130470654222)
XLA Ops:
  2.6 5.1 %collective-permute-start.6 = (bf16[96,768]{1,0:T(8,128)(2,1)S(1)}, bf16[96,768]{1,0:T(8,128)(2,1)S(1)}, u32[]{:S(2)}, u32[]{:S(2)}) collective-permute-start(bf16[96,768]{1,0:T(8,128)(2,1)S(1)} %pad_maximum_fusion.3), channel_id=1, source_target_pairs={{0,24},{2,26},{4,28},{6,30},{8,16},{10,18},{12,20},{14,22},{16,8},... | collective-permute-start | bytes 442376 | tf_op jit(solution)/shard_map/ppermute | solution.py:665
  12.6 7.4 %collective-permute-start.17 = (bf16[96,768]{1,0:T(8,128)(2,1)S(1)}, bf16[96,768]{1,0:T(8,128)(2,1)S(1)}, u32[]{:S(2)}, u32[]{:S(2)}) collective-permute-start(bf16[96,768]{1,0:T(8,128)(2,1)S(1)} %bitcast_convert_fusion), channel_id=1, source_target_pairs={{0,16},{2,18},{4,20},{6,22},{8,24},{10,26},{12,28},{14,30},{16,0},... | collective-permute-start | bytes 442376 | tf_op jit(solution)/shard_map/ppermute | solution.py:665
  20.0 4.3 %collective-permute-done.4 = bf16[96,768]{1,0:T(8,128)(2,1)S(1)} collective-permute-done((bf16[96,768]{1,0:T(8,128)(2,1)S(1)}, bf16[96,768]{1,0:T(8,128)(2,1)S(1)}, u32[]{:S(2)}, u32[]{:S(2)}) %collective-permute-start.4) | collective-permute-done | bytes 147488 | tf_op jit(solution)/shard_map/ppermute | solution.py:665
  28.1 1.6 collective-permute-start.22
  29.7 8.1 %collective-permute-done.18 = bf16[192,768]{1,0:T(8,128)(2,1)S(1)} collective-permute-done((bf16[192,768]{1,0:T(8,128)(2,1)S(1)}, bf16[192,768]{1,0:T(8,128)(2,1)S(1)}, u32[]{:S(2)}, u32[]{:S(2)}) %collective-permute-start.18) | collective-permute-done | bytes 294944 | tf_op jit(solution)/shard_map/ppermute | solution.py:665
  44.1 6.4 %collective-permute-done.23 = bf16[192,768]{1,0:T(8,128)(2,1)} collective-permute-done((bf16[192,768]{1,0:T(8,128)(2,1)S(1)}, bf16[192,768]{1,0:T(8,128)(2,1)}, u32[]{:S(2)}, u32[]{:S(2)}) %collective-permute-start.23) | collective-permute-done | bytes 294944 | tf_op jit(solution)/shard_map/ppermute | solution.py:665
  52.6 3.1 %collective-permute-done.9.z3 = bf16[288,768]{1,0:T(8,128)(2,1)S(1)} collective-permute-done((bf16[288,768]{1,0:T(8,128)(2,1)S(1)}, bf16[288,768]{1,0:T(8,128)(2,1)S(1)}, u32[]{:S(2)}, u32[]{:S(2)}) %collective-permute-start.9) | collective-permute-done | bytes 442400 | tf_op jit(solution)/shard_map/ppermute | solution.py:661
  60.9 6.3 %attend_forward.1 = (f32[2304,256]{1,0:T(8,128)S(1)}, f32[768,256]{1,0:T(8,128)S(1)}, f32[16,256]{1,0:T(8,128)S(1)}, bf16[1536,256]{1,0:T(8,128)(2,1)S(1)}, bf16[1536,256]{1,0:T(8,128)(2,1)S(1)}) custom-call(s32[1,6]{1,0:T(1,128)S(1)} %copy-done.32, s32[2]{0:T(128)S(1)} %pad_add_fusion.me, bf16[256,768]{1,0:T(8,128)(2,1)S(1)} %copy-done.1, ...), custom_call_target="tpu_custom_call" | custom-call | flops 650000000 | tf_op jit(solution)/shard_map/attend_forward/pallas_call | solution.py:317
  67.9 3.9 %attend_close.1 = (f32[256,768]{1,0:T(8,128)S(1)}, bf16[256,768]{1,0:T(8,128)(2,1)S(1)}, f32[256,768]{1,0:T(8,128)S(1)}, f32[256,1]{1,0:T(8,128)S(1)}) custom-call(bf16[256,768]{1,0:T(8,128)(2,1)S(1)} %copy-done.1, bf16[1536,256]{1,0:T(8,128)(2,1)S(1)} %get-tuple-element.97.rel_own.ata, bf16[1536,256]{1,0:T(8,128)(2,1)S(1)} %get-tuple-element.98.rel_par, ...), custom_call_target="tpu_custom_call" | custom-call | flops 360000000 | tf_op jit(solution)/shard_map/attend_close/pallas_call | solution.py:317
  71.8 1.6 collective-permute-start.26
  73.4 1.7 collective-permute-done.15.yb.zb
  75.1 2.5 %feed_up.1 = (bf16[1536,512]{1,0:T(8,128)(2,1)S(1)}, f32[1536,512]{1,0:T(8,128)S(1)}) custom-call(bf16[256,768]{1,0:T(8,128)(2,1)S(1)} %get-tuple-element.100.ya.za, bf16[256,768]{1,0:T(8,128)(2,1)S(1)} %collective-permute-done.15.yb.zb, bf16[384,768]{1,0:T(8,128)(2,1)S(1)} %copy-done.6, bf16[288,768]{1,0:T(8,128)(2,1)S(1)} %copy-done.4, ...), custom_call_target="tpu_custom_call" | custom-call | flops 250000000 | tf_op jit(solution)/shard_map/feed_up/pallas_call | solution.py:317
  77.7 2.7 %collective-permute-done.26.z3 = bf16[288,768]{1,0:T(8,128)(2,1)S(1)} collective-permute-done((bf16[288,768]{1,0:T(8,128)(2,1)S(1)}, bf16[288,768]{1,0:T(8,128)(2,1)S(1)}, u32[]{:S(2)}, u32[]{:S(2)}) %collective-permute-start.26) | collective-permute-done | bytes 442400 | tf_op jit(solution)/shard_map/ppermute | solution.py:661
  84.9 1.6 collective-permute-done.28.zb
  90.1 2.6 %feed_back.1 = (bf16[1536,512]{1,0:T(8,128)(2,1)S(1)}, f32[256,768]{1,0:T(8,128)S(1)}, f32[256,768]{1,0:T(8,128)S(1)}) custom-call(f32[1536,512]{1,0:T(8,128)S(1)} %get-tuple-element.120.slope, bf16[256,768]{1,0:T(8,128)(2,1)S(1)} %get-tuple-element.123.za, bf16[256,768]{1,0:T(8,128)(2,1)S(1)} %collective-permute-done.28.zb, ...), custom_call_target="tpu_custom_call" | custom-call | flops 1000000000 | tf_op jit(solution)/shard_map/feed_back/pallas_call | solution.py:317
  95.2 7.0 %attend_backward.1 = (f32[256,768]{1,0:T(8,128)S(1)}, bf16[256,768]{1,0:T(8,128)(2,1)S(1)}, f32[2,768]{1,0:T(2,128)S(1)}, bf16[1536,256]{1,0:T(8,128)(2,1)S(1)}, bf16[1536,256]{1,0:T(8,128)(2,1)S(1)}) custom-call(s32[1,6]{1,0:T(1,128)S(1)} %copy-done.32, s32[2]{0:T(128)S(1)} %pad_add_fusion.me, f32[256,768]{1,0:T(8,128)S(1)} %get-tuple-element.119.ds2, ...), custom_call_target="tpu_custom_call" | custom-call | tf_op jit(solution)/shard_map/attend_backward/pallas_call | solution.py:317
  104.3 1.7 collective-permute-done.31.dob
  106.0 1.6 mix_away.1
  107.6 12.4 %collective-permute-done.33 = bf16[384,768]{1,0:T(8,128)(2,1)S(1)} collective-permute-done((bf16[384,768]{1,0:T(8,128)(2,1)S(1)}, bf16[384,768]{1,0:T(8,128)(2,1)S(1)}, u32[]{:S(2)}, u32[]{:S(2)}) %collective-permute-start.33) | collective-permute-done | bytes 589856 | tf_op jit(solution)/shard_map/ppermute | solution.py:657
  123.2 4.4 %grad_input.1 = f32[256,768]{1,0:T(8,128)} custom-call(f32[256,768]{1,0:T(8,128)S(1)} %get-tuple-element.134.dh, bf16[1536,256]{1,0:T(8,128)(2,1)S(1)} %get-tuple-element.135.dma.rel_own, bf16[1536,256]{1,0:T(8,128)(2,1)S(1)} %get-tuple-element.132.rel_par, bf16[384,768]{1,0:T(8,128)(2,1)S(1)} %get-tuple-element.93.so, ...), custom_call_target="tpu_custom_call" | custom-call | tf_op jit(solution)/shard_map/grad_input/pallas_call | solution.py:317
  129.7 2.0 %collective-permute-start.46 = (bf16[96,768]{1,0:T(8,128)(2,1)S(1)}, bf16[96,768]{1,0:T(8,128)(2,1)S(1)}, u32[]{:S(2)}, u32[]{:S(2)}) collective-permute-start(bf16[96,768]{1,0:T(8,128)(2,1)S(1)} %get-tuple-element.173), channel_id=1, source_target_pairs={{0,24},{2,26},{4,28},{6,30},{8,16},{10,18},{12,20},{14,22},{16,8},... | collective-permute-start | bytes 442376 | tf_op jit(solution)/shard_map/ppermute | solution.py:665
  132.8 9.7 %collective-permute-done.34 = bf16[768,768]{1,0:T(8,128)(2,1)S(1)} collective-permute-done((bf16[768,768]{1,0:T(8,128)(2,1)S(1)}, bf16[768,768]{1,0:T(8,128)(2,1)S(1)}, u32[]{:S(2)}, u32[]{:S(2)}) %collective-permute-start.34) | collective-permute-done | bytes 1179680 | tf_op jit(solution)/shard_map/ppermute | solution.py:661
  144.0 2.0 %collective-permute-start.44 = (bf16[96,768]{1,0:T(8,128)(2,1)S(1)}, bf16[96,768]{1,0:T(8,128)(2,1)S(1)}, u32[]{:S(2)}, u32[]{:S(2)}) collective-permute-start(bf16[96,768]{1,0:T(8,128)(2,1)S(1)} %get-tuple-element.176), channel_id=1, source_target_pairs={{0,24},{2,26},{4,28},{6,30},{8,16},{10,18},{12,20},{14,22},{16,8},... | collective-permute-start | bytes 442376 | tf_op jit(solution)/shard_map/ppermute | solution.py:665
  147.2 5.5 %collective-permute-done.35 = bf16[384,768]{1,0:T(8,128)(2,1)S(1)} collective-permute-done((bf16[384,768]{1,0:T(8,128)(2,1)S(1)}, bf16[384,768]{1,0:T(8,128)(2,1)S(1)}, u32[]{:S(2)}, u32[]{:S(2)}) %collective-permute-start.35) | collective-permute-done | bytes 589856 | tf_op jit(solution)/shard_map/ppermute | solution.py:657
  152.8 3.5 %collective-permute-done.39 = bf16[96,768]{1,0:T(8,128)(2,1)S(1)} collective-permute-done((bf16[96,768]{1,0:T(8,128)(2,1)S(1)}, bf16[96,768]{1,0:T(8,128)(2,1)S(1)}, u32[]{:S(2)}, u32[]{:S(2)}) %collective-permute-start.39) | collective-permute-done | bytes 147488 | tf_op jit(solution)/shard_map/ppermute | solution.py:665
  156.4 1.7 collective-permute-start.42
  158.0 2.8 %collective-permute-start.40 = (bf16[96,768]{1,0:T(8,128)(2,1)S(1)}, bf16[96,768]{1,0:T(8,128)(2,1)S(1)}, u32[]{:S(2)}, u32[]{:S(2)}) collective-permute-start(bf16[96,768]{1,0:T(8,128)(2,1)S(1)} %get-tuple-element.180), channel_id=1, source_target_pairs={{0,16},{2,18},{4,20},{6,22},{8,24},{10,26},{12,28},{14,30},{16,0},... | collective-permute-start | bytes 442376 | tf_op jit(solution)/shard_map/ppermute | solution.py:665
  161.1 3.9 %collective-permute-done.42.c1 = bf16[96,768]{1,0:T(8,128)(2,1)S(1)} collective-permute-done((bf16[96,768]{1,0:T(8,128)(2,1)S(1)}, bf16[96,768]{1,0:T(8,128)(2,1)S(1)}, u32[]{:S(2)}, u32[]{:S(2)}) %collective-permute-start.42) | collective-permute-done | bytes 147488 | tf_op jit(solution)/shard_map/ppermute | solution.py:665
  166.2 4.5 %collective-permute-done.40.a1 = bf16[96,768]{1,0:T(8,128)(2,1)S(1)} collective-permute-done((bf16[96,768]{1,0:T(8,128)(2,1)S(1)}, bf16[96,768]{1,0:T(8,128)(2,1)S(1)}, u32[]{:S(2)}, u32[]{:S(2)}) %collective-permute-start.40) | collective-permute-done | bytes 147488 | tf_op jit(solution)/shard_map/ppermute | solution.py:665
  178.0 1.7 collective-permute-start.53
  179.7 2.8 %collective-permute-start.51 = (f32[8,768]{1,0:T(8,128)S(1)}, f32[8,768]{1,0:T(8,128)S(1)}, u32[]{:S(2)}, u32[]{:S(2)}) collective-permute-start(f32[8,768]{1,0:T(8,128)S(1)} %add_add_fusion.n0), channel_id=1, source_target_pairs={{0,8},{2,10},{4,12},{6,14},{8,0},{10,2},{12,4},{14,6},{16,24},{18,... | collective-permute-start | bytes 73736 | tf_op jit(solution)/shard_map/ppermute | solution.py:665
  184.6 2.3 %update.1 = (f32[1,1]{1,0:T(1,128)}, f32[72,768]{1,0:T(8,128)}, f32[24,768]{1,0:T(8,128)}, f32[96,768]{1,0:T(8,128)}, f32[96,768]{1,0:T(8,128)}, /*index=5*/f32[...) custom-call(f32[8,768]{1,0:T(8,128)S(1)} %add_add_fusion.n0, ...), custom_call_target="tpu_custom_call" | custom-call | tf_op jit(solution)/shard_map/update/pallas_call | solution.py:317
  (191 shorter events, 57.1 us)
Async XLA Ops:
  2.6 10.0 %collective-permute-start.6 = (bf16[96,768]{1,0:T(8,128)(2,1)S(1)}, bf16[96,768]{1,0:T(8,128)(2,1)S(1)}, u32[]{:S(2)}, u32[]{:S(2)}) collective-permute-start(bf16[96,768]{1,0:T(8,128)(2,1)S(1)} %pad_maximum_fusion.3), channel_id=1, source_target_pairs={{0,24},{2,26},{4,28},{6,30},{8,16},{10,18},{12,20},{14,22},{16,8},... | collective-permute-start | bytes 442376 | tf_op jit(solution)/shard_map/ppermute | solution.py:665
  7.7 16.6 %collective-permute-start.4 = (bf16[96,768]{1,0:T(8,128)(2,1)S(1)}, bf16[96,768]{1,0:T(8,128)(2,1)S(1)}, u32[]{:S(2)}, u32[]{:S(2)}) collective-permute-start(bf16[96,768]{1,0:T(8,128)(2,1)S(1)} %pad_maximum_fusion.3), channel_id=1, source_target_pairs={{0,16},{2,18},{4,20},{6,22},{8,24},{10,26},{12,28},{14,30},{16,0},... | collective-permute-start | bytes 442376 | tf_op jit(solution)/shard_map/ppermute | solution.py:665
  8.8 15.6 %collective-permute-start.2 = (bf16[288,768]{1,0:T(8,128)(2,1)S(1)}, bf16[288,768]{1,0:T(8,128)(2,1)S(1)}, u32[]{:S(2)}, u32[]{:S(2)}) collective-permute-start(bf16[288,768]{1,0:T(8,128)(2,1)S(1)} %pad_maximum_fusion.s0), channel_id=1, source_target_pairs={{0,4},{1,3},{2,6},{3,1},{4,0},{5,7},{6,2},{7,5},{8,12},{9,11},{10,... | collective-permute-start | bytes 1327112 | tf_op jit(solution)/shard_map/ppermute | solution.py:661
  10.3 15.6 %collective-permute-start.1 = (bf16[288,768]{1,0:T(8,128)(2,1)S(1)}, bf16[288,768]{1,0:T(8,128)(2,1)S(1)}, u32[]{:S(2)}, u32[]{:S(2)}) collective-permute-start(bf16[288,768]{1,0:T(8,128)(2,1)S(1)} %pad_maximum_fusion.s0), channel_id=1, source_target_pairs={{0,2},{1,5},{2,0},{3,7},{4,6},{5,1},{6,4},{7,3},{8,10},{9,13},{10,... | collective-permute-start | bytes 1327112 | tf_op jit(solution)/shard_map/ppermute | solution.py:657
  11.8 12.5 %collective-permute-start.5 = (bf16[96,768]{1,0:T(8,128)(2,1)S(1)}, bf16[96,768]{1,0:T(8,128)(2,1)S(1)}, u32[]{:S(2)}, u32[]{:S(2)}) collective-permute-start(bf16[96,768]{1,0:T(8,128)(2,1)S(1)} %pad_maximum_fusion.3), channel_id=1, source_target_pairs={{0,8},{2,10},{4,12},{6,14},{8,0},{10,2},{12,4},{14,6},{16,24},{18,... | collective-permute-start | bytes 442376 | tf_op jit(solution)/shard_map/ppermute | solution.py:665
  12.6 15.3 %collective-permute-start.17 = (bf16[96,768]{1,0:T(8,128)(2,1)S(1)}, bf16[96,768]{1,0:T(8,128)(2,1)S(1)}, u32[]{:S(2)}, u32[]{:S(2)}) collective-permute-start(bf16[96,768]{1,0:T(8,128)(2,1)S(1)} %bitcast_convert_fusion), channel_id=1, source_target_pairs={{0,16},{2,18},{4,20},{6,22},{8,24},{10,26},{12,28},{14,30},{16,0},... | collective-permute-start | bytes 442376 | tf_op jit(solution)/shard_map/ppermute | solution.py:665
  24.4 13.5 %collective-permute-start.8 = (bf16[288,768]{1,0:T(8,128)(2,1)S(1)}, bf16[288,768]{1,0:T(8,128)(2,1)S(1)}, u32[]{:S(2)}, u32[]{:S(2)}) collective-permute-start(bf16[288,768]{1,0:T(8,128)(2,1)S(1)} %constant_dynamic-update-slice_fusion.z0), channel_id=1, source_target_pairs={{0,4},{1,3},{2,6},{3,1},{4,0},{5,7},{6,2},{7,5},{8,12},{9,11},{10,... | collective-permute-start | bytes 1327112 | tf_op jit(solution)/shard_map/ppermute | solution.py:661
  26.0 13.5 %collective-permute-start.7 = (bf16[288,768]{1,0:T(8,128)(2,1)S(1)}, bf16[288,768]{1,0:T(8,128)(2,1)S(1)}, u32[]{:S(2)}, u32[]{:S(2)}) collective-permute-start(bf16[288,768]{1,0:T(8,128)(2,1)S(1)} %constant_dynamic-update-slice_fusion.z0), channel_id=1, source_target_pairs={{0,2},{1,5},{2,0},{3,7},{4,6},{5,1},{6,4},{7,3},{8,10},{9,13},{10,... | collective-permute-start | bytes 1327112 | tf_op jit(solution)/shard_map/ppermute | solution.py:657
  27.4 13.6 %collective-permute-start.3 = (bf16[288,768]{1,0:T(8,128)(2,1)S(1)}, bf16[288,768]{1,0:T(8,128)(2,1)S(1)}, u32[]{:S(2)}, u32[]{:S(2)}) collective-permute-start(bf16[288,768]{1,0:T(8,128)(2,1)S(1)} %collective-permute-done.1.s1), channel_id=1, source_target_pairs={{0,4},{1,3},{2,6},{3,1},{4,0},{5,7},{6,2},{7,5},{8,12},{9,11},{10,... | collective-permute-start | bytes 1327112 | tf_op jit(solution)/shard_map/ppermute | solution.py:661
  28.0 9.8 %collective-permute-start.18 = (bf16[192,768]{1,0:T(8,128)(2,1)S(1)}, bf16[192,768]{1,0:T(8,128)(2,1)S(1)}, u32[]{:S(2)}, u32[]{:S(2)}) collective-permute-start(bf16[192,768]{1,0:T(8,128)(2,1)S(1)} %pad_maximum_fusion.1), channel_id=1, source_target_pairs={{0,8},{2,10},{4,12},{6,14},{8,0},{10,2},{12,4},{14,6},{16,24},{18,... | collective-permute-start | bytes 884744 | tf_op jit(solution)/shard_map/ppermute | solution.py:665
  28.1 13.5 %collective-permute-start.22 = (bf16[96,768]{1,0:T(8,128)(2,1)S(1)}, bf16[96,768]{1,0:T(8,128)(2,1)S(1)}, u32[]{:S(2)}, u32[]{:S(2)}) collective-permute-start(bf16[96,768]{1,0:T(8,128)(2,1)S(1)} %convert_element_type.78), channel_id=1, source_target_pairs={{0,16},{2,18},{4,20},{6,22},{8,24},{10,26},{12,28},{14,30},{16,0},... | collective-permute-start | bytes 442376 | tf_op jit(solution)/shard_map/ppermute | solution.py:665
  37.8 12.7 %collective-permute-start.20 = (bf16[288,768]{1,0:T(8,128)(2,1)S(1)}, bf16[288,768]{1,0:T(8,128)(2,1)S(1)}, u32[]{:S(2)}, u32[]{:S(2)}) collective-permute-start(bf16[288,768]{1,0:T(8,128)(2,1)S(1)} %constant_dynamic-update-slice_fusion.3.z0), channel_id=1, source_target_pairs={{0,4},{1,3},{2,6},{3,1},{4,0},{5,7},{6,2},{7,5},{8,12},{9,11},{10,... | collective-permute-start | bytes 1327112 | tf_op jit(solution)/shard_map/ppermute | solution.py:661
  39.4 13.2 %collective-permute-start.19 = (bf16[288,768]{1,0:T(8,128)(2,1)S(1)}, bf16[288,768]{1,0:T(8,128)(2,1)S(1)}, u32[]{:S(2)}, u32[]{:S(2)}) collective-permute-start(bf16[288,768]{1,0:T(8,128)(2,1)S(1)} %constant_dynamic-update-slice_fusion.3.z0), channel_id=1, source_target_pairs={{0,2},{1,5},{2,0},{3,7},{4,6},{5,1},{6,4},{7,3},{8,10},{9,13},{10,... | collective-permute-start | bytes 1327112 | tf_op jit(solution)/shard_map/ppermute | solution.py:657
  41.0 14.7 %collective-permute-start.9 = (bf16[288,768]{1,0:T(8,128)(2,1)S(1)}, bf16[288,768]{1,0:T(8,128)(2,1)S(1)}, u32[]{:S(2)}, u32[]{:S(2)}) collective-permute-start(bf16[288,768]{1,0:T(8,128)(2,1)S(1)} %collective-permute-done.7.z1), channel_id=1, source_target_pairs={{0,4},{1,3},{2,6},{3,1},{4,0},{5,7},{6,2},{7,5},{8,12},{9,11},{10,... | collective-permute-start | bytes 1327112 | tf_op jit(solution)/shard_map/ppermute | solution.py:661
  41.5 9.0 %collective-permute-start.23 = (bf16[192,768]{1,0:T(8,128)(2,1)S(1)}, bf16[192,768]{1,0:T(8,128)(2,1)}, u32[]{:S(2)}, u32[]{:S(2)}) collective-permute-start(bf16[192,768]{1,0:T(8,128)(2,1)S(1)} %pad_maximum_fusion.2), channel_id=1, source_target_pairs={{0,8},{2,10},{4,12},{6,14},{8,0},{10,2},{12,4},{14,6},{16,24},{18,... | collective-permute-start | bytes 884744 | tf_op jit(solution)/shard_map/ppermute | solution.py:665
  44.1 15.7 %collective-permute-start.10 = (bf16[384,768]{1,0:T(8,128)(2,1)S(1)}, bf16[384,768]{1,0:T(8,128)(2,1)S(1)}, u32[]{:S(2)}, u32[]{:S(2)}) collective-permute-start(bf16[384,768]{1,0:T(8,128)(2,1)S(1)} %get-tuple-element.93.so), channel_id=1, source_target_pairs={{0,1},{1,0},{2,3},{3,2},{4,5},{5,4},{6,7},{7,6},{8,9},{9,8},{10,11... | collective-permute-start | bytes 1769480 | tf_op jit(solution)/shard_map/ppermute | solution.py:653
  56.7 15.1 %collective-permute-start.24 = (bf16[288,768]{1,0:T(8,128)(2,1)S(1)}, bf16[288,768]{1,0:T(8,128)(2,1)S(1)}, u32[]{:S(2)}, u32[]{:S(2)}) collective-permute-start(bf16[288,768]{1,0:T(8,128)(2,1)S(1)} %constant_dynamic-update-slice_fusion.5.z0), channel_id=1, source_target_pairs={{0,2},{1,5},{2,0},{3,7},{4,6},{5,1},{6,4},{7,3},{8,10},{9,13},{10,... | collective-permute-start | bytes 1327112 | tf_op jit(solution)/shard_map/ppermute | solution.py:657
  58.3 13.5 %collective-permute-start.21 = (bf16[288,768]{1,0:T(8,128)(2,1)}, bf16[288,768]{1,0:T(8,128)(2,1)S(1)}, u32[]{:S(2)}, u32[]{:S(2)}) collective-permute-start(bf16[288,768]{1,0:T(8,128)(2,1)} %copy-done.9), channel_id=1, source_target_pairs={{0,4},{1,3},{2,6},{3,1},{4,0},{5,7},{6,2},{7,5},{8,12},{9,11},{10,... | collective-permute-start | bytes 1327112 | tf_op jit(solution)/shard_map/ppermute | solution.py:661
  67.3 10.4 %collective-permute-start.25 = (bf16[288,768]{1,0:T(8,128)(2,1)S(1)}, bf16[288,768]{1,0:T(8,128)(2,1)S(1)}, u32[]{:S(2)}, u32[]{:S(2)}) collective-permute-start(bf16[288,768]{1,0:T(8,128)(2,1)S(1)} %constant_dynamic-update-slice_fusion.5.z0), channel_id=1, source_target_pairs={{0,4},{1,3},{2,6},{3,1},{4,0},{5,7},{6,2},{7,5},{8,12},{9,11},{10,... | collective-permute-start | bytes 1327112 | tf_op jit(solution)/shard_map/ppermute | solution.py:661
  87.3 16.3 %collective-permute-start.32 = (bf16[768,768]{1,0:T(8,128)(2,1)S(1)}, bf16[768,768]{1,0:T(8,128)(2,1)S(1)}, u32[]{:S(2)}, u32[]{:S(2)}) collective-permute-start(bf16[768,768]{1,0:T(8,128)(2,1)S(1)} %grad_down_away.1), channel_id=1, source_target_pairs={{0,4},{1,3},{2,6},{3,1},{4,0},{5,7},{6,2},{7,5},{8,12},{9,11},{10,... | collective-permute-start | bytes 3538952 | tf_op jit(solution)/shard_map/ppermute | solution.py:661
  93.7 28.8 %collective-permute-start.36 = (bf16[768,768]{1,0:T(8,128)(2,1)S(1)}, bf16[768,768]{1,0:T(8,128)(2,1)S(1)}, u32[]{:S(2)}, u32[]{:S(2)}) collective-permute-start(bf16[768,768]{1,0:T(8,128)(2,1)S(1)} %grad_up_away.1), channel_id=1, source_target_pairs={{0,4},{1,3},{2,6},{3,1},{4,0},{5,7},{6,2},{7,5},{8,12},{9,11},{10,... | collective-permute-start | bytes 3538952 | tf_op jit(solution)/shard_map/ppermute | solution.py:661
  103.7 16.3 %collective-permute-start.33 = (bf16[384,768]{1,0:T(8,128)(2,1)S(1)}, bf16[384,768]{1,0:T(8,128)(2,1)S(1)}, u32[]{:S(2)}, u32[]{:S(2)}) collective-permute-start(bf16[384,768]{1,0:T(8,128)(2,1)S(1)} %add_convert_fusion.2), channel_id=1, source_target_pairs={{0,2},{1,5},{2,0},{3,7},{4,6},{5,1},{6,4},{7,3},{8,10},{9,13},{10,... | collective-permute-start | bytes 1769480 | tf_op jit(solution)/shard_map/ppermute | solution.py:657
  120.0 22.5 %collective-permute-start.34 = (bf16[768,768]{1,0:T(8,128)(2,1)S(1)}, bf16[768,768]{1,0:T(8,128)(2,1)S(1)}, u32[]{:S(2)}, u32[]{:S(2)}) collective-permute-start(bf16[768,768]{1,0:T(8,128)(2,1)S(1)} %mix_away.1), channel_id=1, source_target_pairs={{0,4},{1,3},{2,6},{3,1},{4,0},{5,7},{6,2},{7,5},{8,12},{9,11},{10,... | collective-permute-start | bytes 3538952 | tf_op jit(solution)/shard_map/ppermute | solution.py:661
  122.6 20.6 %collective-permute-start.37 = (bf16[384,768]{1,0:T(8,128)(2,1)S(1)}, bf16[384,768]{1,0:T(8,128)(2,1)S(1)}, u32[]{:S(2)}, u32[]{:S(2)}) collective-permute-start(bf16[384,768]{1,0:T(8,128)(2,1)S(1)} %add_convert_fusion), channel_id=1, source_target_pairs={{0,2},{1,5},{2,0},{3,7},{4,6},{5,1},{6,4},{7,3},{8,10},{9,13},{10,... | collective-permute-start | bytes 1769480 | tf_op jit(solution)/shard_map/ppermute | solution.py:657
  129.3 16.7 %collective-permute-start.45 = (bf16[96,768]{1,0:T(8,128)(2,1)S(1)}, bf16[96,768]{1,0:T(8,128)(2,1)S(1)}, u32[]{:S(2)}, u32[]{:S(2)}) collective-permute-start(bf16[96,768]{1,0:T(8,128)(2,1)S(1)} %get-tuple-element.172), channel_id=1, source_target_pairs={{0,16},{2,18},{4,20},{6,22},{8,24},{10,26},{12,28},{14,30},{16,0},... | collective-permute-start | bytes 442376 | tf_op jit(solution)/shard_map/ppermute | solution.py:665
  129.7 17.4 %collective-permute-start.46 = (bf16[96,768]{1,0:T(8,128)(2,1)S(1)}, bf16[96,768]{1,0:T(8,128)(2,1)S(1)}, u32[]{:S(2)}, u32[]{:S(2)}) collective-permute-start(bf16[96,768]{1,0:T(8,128)(2,1)S(1)} %get-tuple-element.173), channel_id=1, source_target_pairs={{0,24},{2,26},{4,28},{6,30},{8,16},{10,18},{12,20},{14,22},{16,8},... | collective-permute-start | bytes 442376 | tf_op jit(solution)/shard_map/ppermute | solution.py:665
  131.7 11.8 %collective-permute-start.38 = (bf16[96,768]{1,0:T(8,128)(2,1)S(1)}, bf16[96,768]{1,0:T(8,128)(2,1)S(1)}, u32[]{:S(2)}, u32[]{:S(2)}) collective-permute-start(bf16[96,768]{1,0:T(8,128)(2,1)S(1)} %get-tuple-element.174), channel_id=1, source_target_pairs={{0,8},{2,10},{4,12},{6,14},{8,0},{10,2},{12,4},{14,6},{16,24},{18,... | collective-permute-start | bytes 442376 | tf_op jit(solution)/shard_map/ppermute | solution.py:665
  142.7 9.9 %collective-permute-start.35 = (bf16[384,768]{1,0:T(8,128)(2,1)S(1)}, bf16[384,768]{1,0:T(8,128)(2,1)S(1)}, u32[]{:S(2)}, u32[]{:S(2)}) collective-permute-start(bf16[384,768]{1,0:T(8,128)(2,1)S(1)} %add_convert_fusion.1), channel_id=1, source_target_pairs={{0,2},{1,5},{2,0},{3,7},{4,6},{5,1},{6,4},{7,3},{8,10},{9,13},{10,... | collective-permute-start | bytes 1769480 | tf_op jit(solution)/shard_map/ppermute | solution.py:657
  143.5 17.3 %collective-permute-start.43 = (bf16[96,768]{1,0:T(8,128)(2,1)S(1)}, bf16[96,768]{1,0:T(8,128)(2,1)S(1)}, u32[]{:S(2)}, u32[]{:S(2)}) collective-permute-start(bf16[96,768]{1,0:T(8,128)(2,1)S(1)} %get-tuple-element.175), channel_id=1, source_target_pairs={{0,16},{2,18},{4,20},{6,22},{8,24},{10,26},{12,28},{14,30},{16,0},... | collective-permute-start | bytes 442376 | tf_op jit(solution)/shard_map/ppermute | solution.py:665
  144.0 16.9 %collective-permute-start.44 = (bf16[96,768]{1,0:T(8,128)(2,1)S(1)}, bf16[96,768]{1,0:T(8,128)(2,1)S(1)}, u32[]{:S(2)}, u32[]{:S(2)}) collective-permute-start(bf16[96,768]{1,0:T(8,128)(2,1)S(1)} %get-tuple-element.176), channel_id=1, source_target_pairs={{0,24},{2,26},{4,28},{6,30},{8,16},{10,18},{12,20},{14,22},{16,8},... | collective-permute-start | bytes 442376 | tf_op jit(solution)/shard_map/ppermute | solution.py:665
  146.0 10.4 %collective-permute-start.39 = (bf16[96,768]{1,0:T(8,128)(2,1)S(1)}, bf16[96,768]{1,0:T(8,128)(2,1)S(1)}, u32[]{:S(2)}, u32[]{:S(2)}) collective-permute-start(bf16[96,768]{1,0:T(8,128)(2,1)S(1)} %get-tuple-element.177), channel_id=1, source_target_pairs={{0,8},{2,10},{4,12},{6,14},{8,0},{10,2},{12,4},{14,6},{16,24},{18,... | collective-permute-start | bytes 442376 | tf_op jit(solution)/shard_map/ppermute | solution.py:665
  158.0 12.6 %collective-permute-start.40 = (bf16[96,768]{1,0:T(8,128)(2,1)S(1)}, bf16[96,768]{1,0:T(8,128)(2,1)S(1)}, u32[]{:S(2)}, u32[]{:S(2)}) collective-permute-start(bf16[96,768]{1,0:T(8,128)(2,1)S(1)} %get-tuple-element.180), channel_id=1, source_target_pairs={{0,16},{2,18},{4,20},{6,22},{8,24},{10,26},{12,28},{14,30},{16,0},... | collective-permute-start | bytes 442376 | tf_op jit(solution)/shard_map/ppermute | solution.py:665
  (55 other events, 552.4 us)

commit v6 on v5

--- a/solution.py
+++ b/solution.py
@@ -442,7 +442,7 @@
     for (base, size), ref in zip(PIECES, (s, z0, z1, z2, z3)):
         whole[base : base + size, :] = ref[...]
     rows = other.shape[0]
-    other[...] = tn(hid[:, rows : 2 * rows], whole[...])
+    other[...] = tn(hid[:, rows : 2 * rows], whole[...]).astype(other.dtype)
 
 
 def down_here(hid, whole, own):
@@ -466,7 +466,7 @@
 
 
 def turn_round(lengths, first, own, got, cot, norms, ds2, dz, xhat):
-    h = first[...] + (own[...] + got[...])
+    h = first[...] + (own[...] + got[...].astype(F32))
     centered = h - jnp.mean(h, axis=-1, keepdims=True)
     spread = jnp.mean(centered * centered, axis=-1, keepdims=True)
     scale = lax.rsqrt(spread + 1e-05)
@@ -757,7 +757,7 @@
         (first_low, tie(first_par, at_got)) + up_all,
     )
     down_par, down_full = call(
-        down_away, [((rows, width), F32), ((HALF, width), BF)], (hid,) + down_all
+        down_away, [((rows, width), BF), ((HALF, width), BF)], (hid,) + down_all
     )
     down_got = swap(down_par)
     (down_own,) = call(down_here, [((rows, width), F32)], (tie(hid, down_par), down_full))

time: 187 us -> 187 us (level)
  no operation moved by 1% of the time
where the time goes in v6:
time: 187 us
  waiting for transfers between devices  78.9 us (42%)
  starting transfers between devices  56.5 us (30%)
  Pallas kernels  40 us (21%)
  local copies, waits for them, and re-layouts  5.44 us (3%)
  other arithmetic  4.2 us (2%)
    pallas_call x19, Pallas kernels, call(): pl.pallas_call(body, out_shape=[jax.ShapeDtypeStruct(s, t) for s, t in ou...  40 us
    ppermute x22, waiting for transfers between devices, hop_z(): return lax.ppermute(value, 'dp', [(i, i ^ step) for i in range(CHIPS)])  36.3 us
    ppermute x22, starting transfers between devices, hop_z(): return lax.ppermute(value, 'dp', [(i, i ^ step) for i in range(CHIPS)])  34.6 us
    ppermute x7, waiting for transfers between devices, hop_first(): lax.ppermute(value, AXES, [(i, i ^ (4 if i % 2 else 2)) for i in range(2...  18.7 us
    ppermute x11, waiting for transfers between devices, hop_second(): lax.ppermute(value, AXES, [(i, i ^ (2 if i % 2 else 4)) for i in range(2...  17 us
    ppermute x11, starting transfers between devices, hop_second(): lax.ppermute(value, AXES, [(i, i ^ (2 if i % 2 else 4)) for i in range(2...  12.9 us
    ppermute x7, starting transfers between devices, hop_first(): lax.ppermute(value, AXES, [(i, i ^ (4 if i % 2 else 2)) for i in range(2...  7.88 us
    ppermute x14, waiting for transfers between devices, swap(): return lax.ppermute(value, 'fsdp', [(0, 1), (1, 0)])  6.91 us
  transfers between devices with their start and end apart: 54, of which 24 were waited for; matrix products, arithmetic and copies ran while one was open for 2% of the time, Pallas kernels for 19%

profile of v6, /device:TPU:0, one launch (start us, length us, event | category | flops | bytes accessed | tf_op | source)
XLA Modules:
  0.0 186.6 jit_solution(3473698071643080764)
XLA Ops:
  2.6 5.1 %collective-permute-start.6 = (bf16[96,768]{1,0:T(8,128)(2,1)S(1)}, bf16[96,768]{1,0:T(8,128)(2,1)S(1)}, u32[]{:S(2)}, u32[]{:S(2)}) collective-permute-start(bf16[96,768]{1,0:T(8,128)(2,1)S(1)} %pad_maximum_fusion.3), channel_id=1, source_target_pairs={{0,24},{2,26},{4,28},{6,30},{8,16},{10,18},{12,20},{14,22},{16,8},... | collective-permute-start | bytes 442376 | tf_op jit(solution)/shard_map/ppermute | solution.py:665
  12.6 7.4 %collective-permute-start.17 = (bf16[96,768]{1,0:T(8,128)(2,1)S(1)}, bf16[96,768]{1,0:T(8,128)(2,1)S(1)}, u32[]{:S(2)}, u32[]{:S(2)}) collective-permute-start(bf16[96,768]{1,0:T(8,128)(2,1)S(1)} %bitcast_convert_fusion), channel_id=1, source_target_pairs={{0,16},{2,18},{4,20},{6,22},{8,24},{10,26},{12,28},{14,30},{16,0},... | collective-permute-start | bytes 442376 | tf_op jit(solution)/shard_map/ppermute | solution.py:665
  20.0 4.3 %collective-permute-done.4 = bf16[96,768]{1,0:T(8,128)(2,1)S(1)} collective-permute-done((bf16[96,768]{1,0:T(8,128)(2,1)S(1)}, bf16[96,768]{1,0:T(8,128)(2,1)S(1)}, u32[]{:S(2)}, u32[]{:S(2)}) %collective-permute-start.4) | collective-permute-done | bytes 147488 | tf_op jit(solution)/shard_map/ppermute | solution.py:665
  28.1 1.6 collective-permute-start.22
  29.7 8.1 %collective-permute-done.18 = bf16[192,768]{1,0:T(8,128)(2,1)S(1)} collective-permute-done((bf16[192,768]{1,0:T(8,128)(2,1)S(1)}, bf16[192,768]{1,0:T(8,128)(2,1)S(1)}, u32[]{:S(2)}, u32[]{:S(2)}) %collective-permute-start.18) | collective-permute-done | bytes 294944 | tf_op jit(solution)/shard_map/ppermute | solution.py:665
  44.1 6.4 %collective-permute-done.23 = bf16[192,768]{1,0:T(8,128)(2,1)} collective-permute-done((bf16[192,768]{1,0:T(8,128)(2,1)S(1)}, bf16[192,768]{1,0:T(8,128)(2,1)}, u32[]{:S(2)}, u32[]{:S(2)}) %collective-permute-start.23) | collective-permute-done | bytes 294944 | tf_op jit(solution)/shard_map/ppermute | solution.py:665
  52.6 3.1 %collective-permute-done.9.z3 = bf16[288,768]{1,0:T(8,128)(2,1)S(1)} collective-permute-done((bf16[288,768]{1,0:T(8,128)(2,1)S(1)}, bf16[288,768]{1,0:T(8,128)(2,1)S(1)}, u32[]{:S(2)}, u32[]{:S(2)}) %collective-permute-start.9) | collective-permute-done | bytes 442400 | tf_op jit(solution)/shard_map/ppermute | solution.py:661
  60.9 6.3 %attend_forward.1 = (f32[2304,256]{1,0:T(8,128)S(1)}, f32[768,256]{1,0:T(8,128)S(1)}, f32[16,256]{1,0:T(8,128)S(1)}, bf16[1536,256]{1,0:T(8,128)(2,1)S(1)}, bf16[1536,256]{1,0:T(8,128)(2,1)S(1)}) custom-call(s32[1,6]{1,0:T(1,128)S(1)} %copy-done.32, s32[2]{0:T(128)S(1)} %pad_add_fusion.me, bf16[256,768]{1,0:T(8,128)(2,1)S(1)} %copy-done.1, ...), custom_call_target="tpu_custom_call" | custom-call | flops 650000000 | tf_op jit(solution)/shard_map/attend_forward/pallas_call | solution.py:317
  67.9 3.9 %attend_close.1 = (f32[256,768]{1,0:T(8,128)S(1)}, bf16[256,768]{1,0:T(8,128)(2,1)S(1)}, f32[256,768]{1,0:T(8,128)S(1)}, f32[256,1]{1,0:T(8,128)S(1)}) custom-call(bf16[256,768]{1,0:T(8,128)(2,1)S(1)} %copy-done.1, bf16[1536,256]{1,0:T(8,128)(2,1)S(1)} %get-tuple-element.97.rel_own.ata, bf16[1536,256]{1,0:T(8,128)(2,1)S(1)} %get-tuple-element.98.rel_par, ...), custom_call_target="tpu_custom_call" | custom-call | flops 360000000 | tf_op jit(solution)/shard_map/attend_close/pallas_call | solution.py:317
  71.8 1.6 collective-permute-start.26
  73.4 1.7 collective-permute-done.15.yb.zb
  75.1 2.5 %feed_up.1 = (bf16[1536,512]{1,0:T(8,128)(2,1)S(1)}, f32[1536,512]{1,0:T(8,128)S(1)}) custom-call(bf16[256,768]{1,0:T(8,128)(2,1)S(1)} %get-tuple-element.100.ya.za, bf16[256,768]{1,0:T(8,128)(2,1)S(1)} %collective-permute-done.15.yb.zb, bf16[384,768]{1,0:T(8,128)(2,1)S(1)} %copy-done.6, bf16[288,768]{1,0:T(8,128)(2,1)S(1)} %copy-done.4, ...), custom_call_target="tpu_custom_call" | custom-call | flops 250000000 | tf_op jit(solution)/shard_map/feed_up/pallas_call | solution.py:317
  77.7 2.7 %collective-permute-done.26.z3 = bf16[288,768]{1,0:T(8,128)(2,1)S(1)} collective-permute-done((bf16[288,768]{1,0:T(8,128)(2,1)S(1)}, bf16[288,768]{1,0:T(8,128)(2,1)S(1)}, u32[]{:S(2)}, u32[]{:S(2)}) %collective-permute-start.26) | collective-permute-done | bytes 442400 | tf_op jit(solution)/shard_map/ppermute | solution.py:661
  84.3 1.6 collective-permute-done.28.zb
  89.6 2.6 %feed_back.1 = (bf16[1536,512]{1,0:T(8,128)(2,1)S(1)}, f32[256,768]{1,0:T(8,128)S(1)}, f32[256,768]{1,0:T(8,128)S(1)}) custom-call(f32[1536,512]{1,0:T(8,128)S(1)} %get-tuple-element.120.slope, bf16[256,768]{1,0:T(8,128)(2,1)S(1)} %get-tuple-element.123.za, bf16[256,768]{1,0:T(8,128)(2,1)S(1)} %collective-permute-done.28.zb, ...), custom_call_target="tpu_custom_call" | custom-call | flops 1000000000 | tf_op jit(solution)/shard_map/feed_back/pallas_call | solution.py:317
  94.7 7.0 %attend_backward.1 = (f32[256,768]{1,0:T(8,128)S(1)}, bf16[256,768]{1,0:T(8,128)(2,1)S(1)}, f32[2,768]{1,0:T(2,128)S(1)}, bf16[1536,256]{1,0:T(8,128)(2,1)S(1)}, bf16[1536,256]{1,0:T(8,128)(2,1)S(1)}) custom-call(s32[1,6]{1,0:T(1,128)S(1)} %copy-done.32, s32[2]{0:T(128)S(1)} %pad_add_fusion.me, f32[256,768]{1,0:T(8,128)S(1)} %get-tuple-element.119.ds2, ...), custom_call_target="tpu_custom_call" | custom-call | tf_op jit(solution)/shard_map/attend_backward/pallas_call | solution.py:317
  103.7 1.7 collective-permute-done.31.dob
  105.5 1.6 mix_away.1
  107.1 12.4 %collective-permute-done.33 = bf16[384,768]{1,0:T(8,128)(2,1)S(1)} collective-permute-done((bf16[384,768]{1,0:T(8,128)(2,1)S(1)}, bf16[384,768]{1,0:T(8,128)(2,1)S(1)}, u32[]{:S(2)}, u32[]{:S(2)}) %collective-permute-start.33) | collective-permute-done | bytes 589856 | tf_op jit(solution)/shard_map/ppermute | solution.py:657
  122.6 4.4 %grad_input.1 = f32[256,768]{1,0:T(8,128)} custom-call(f32[256,768]{1,0:T(8,128)S(1)} %get-tuple-element.134.dh, bf16[1536,256]{1,0:T(8,128)(2,1)S(1)} %get-tuple-element.135.dma.rel_own, bf16[1536,256]{1,0:T(8,128)(2,1)S(1)} %get-tuple-element.132.rel_par, bf16[384,768]{1,0:T(8,128)(2,1)S(1)} %get-tuple-element.93.so, ...), custom_call_target="tpu_custom_call" | custom-call | tf_op jit(solution)/shard_map/grad_input/pallas_call | solution.py:317
  129.1 2.0 %collective-permute-start.46 = (bf16[96,768]{1,0:T(8,128)(2,1)S(1)}, bf16[96,768]{1,0:T(8,128)(2,1)S(1)}, u32[]{:S(2)}, u32[]{:S(2)}) collective-permute-start(bf16[96,768]{1,0:T(8,128)(2,1)S(1)} %get-tuple-element.173), channel_id=1, source_target_pairs={{0,24},{2,26},{4,28},{6,30},{8,16},{10,18},{12,20},{14,22},{16,8},... | collective-permute-start | bytes 442376 | tf_op jit(solution)/shard_map/ppermute | solution.py:665
  132.3 9.7 %collective-permute-done.34 = bf16[768,768]{1,0:T(8,128)(2,1)S(1)} collective-permute-done((bf16[768,768]{1,0:T(8,128)(2,1)S(1)}, bf16[768,768]{1,0:T(8,128)(2,1)S(1)}, u32[]{:S(2)}, u32[]{:S(2)}) %collective-permute-start.34) | collective-permute-done | bytes 1179680 | tf_op jit(solution)/shard_map/ppermute | solution.py:661
  143.4 2.0 %collective-permute-start.44 = (bf16[96,768]{1,0:T(8,128)(2,1)S(1)}, bf16[96,768]{1,0:T(8,128)(2,1)S(1)}, u32[]{:S(2)}, u32[]{:S(2)}) collective-permute-start(bf16[96,768]{1,0:T(8,128)(2,1)S(1)} %get-tuple-element.176), channel_id=1, source_target_pairs={{0,24},{2,26},{4,28},{6,30},{8,16},{10,18},{12,20},{14,22},{16,8},... | collective-permute-start | bytes 442376 | tf_op jit(solution)/shard_map/ppermute | solution.py:665
  146.6 5.5 %collective-permute-done.35 = bf16[384,768]{1,0:T(8,128)(2,1)S(1)} collective-permute-done((bf16[384,768]{1,0:T(8,128)(2,1)S(1)}, bf16[384,768]{1,0:T(8,128)(2,1)S(1)}, u32[]{:S(2)}, u32[]{:S(2)}) %collective-permute-start.35) | collective-permute-done | bytes 589856 | tf_op jit(solution)/shard_map/ppermute | solution.py:657
  152.2 3.5 %collective-permute-done.39 = bf16[96,768]{1,0:T(8,128)(2,1)S(1)} collective-permute-done((bf16[96,768]{1,0:T(8,128)(2,1)S(1)}, bf16[96,768]{1,0:T(8,128)(2,1)S(1)}, u32[]{:S(2)}, u32[]{:S(2)}) %collective-permute-start.39) | collective-permute-done | bytes 147488 | tf_op jit(solution)/shard_map/ppermute | solution.py:665
  155.8 1.7 collective-permute-start.42
  157.5 2.8 %collective-permute-start.40 = (bf16[96,768]{1,0:T(8,128)(2,1)S(1)}, bf16[96,768]{1,0:T(8,128)(2,1)S(1)}, u32[]{:S(2)}, u32[]{:S(2)}) collective-permute-start(bf16[96,768]{1,0:T(8,128)(2,1)S(1)} %get-tuple-element.180), channel_id=1, source_target_pairs={{0,16},{2,18},{4,20},{6,22},{8,24},{10,26},{12,28},{14,30},{16,0},... | collective-permute-start | bytes 442376 | tf_op jit(solution)/shard_map/ppermute | solution.py:665
  160.5 3.9 %collective-permute-done.42.c1 = bf16[96,768]{1,0:T(8,128)(2,1)S(1)} collective-permute-done((bf16[96,768]{1,0:T(8,128)(2,1)S(1)}, bf16[96,768]{1,0:T(8,128)(2,1)S(1)}, u32[]{:S(2)}, u32[]{:S(2)}) %collective-permute-start.42) | collective-permute-done | bytes 147488 | tf_op jit(solution)/shard_map/ppermute | solution.py:665
  165.6 4.5 %collective-permute-done.40.a1 = bf16[96,768]{1,0:T(8,128)(2,1)S(1)} collective-permute-done((bf16[96,768]{1,0:T(8,128)(2,1)S(1)}, bf16[96,768]{1,0:T(8,128)(2,1)S(1)}, u32[]{:S(2)}, u32[]{:S(2)}) %collective-permute-start.40) | collective-permute-done | bytes 147488 | tf_op jit(solution)/shard_map/ppermute | solution.py:665
  177.4 1.7 collective-permute-start.53
  179.1 2.8 %collective-permute-start.51 = (f32[8,768]{1,0:T(8,128)S(1)}, f32[8,768]{1,0:T(8,128)S(1)}, u32[]{:S(2)}, u32[]{:S(2)}) collective-permute-start(f32[8,768]{1,0:T(8,128)S(1)} %add_add_fusion.n0), channel_id=1, source_target_pairs={{0,8},{2,10},{4,12},{6,14},{8,0},{10,2},{12,4},{14,6},{16,24},{18,... | collective-permute-start | bytes 73736 | tf_op jit(solution)/shard_map/ppermute | solution.py:665
  184.0 2.3 %update.1 = (f32[1,1]{1,0:T(1,128)}, f32[72,768]{1,0:T(8,128)}, f32[24,768]{1,0:T(8,128)}, f32[96,768]{1,0:T(8,128)}, f32[96,768]{1,0:T(8,128)}, /*index=5*/f32[...) custom-call(f32[8,768]{1,0:T(8,128)S(1)} %add_add_fusion.n0, ...), custom_call_target="tpu_custom_call" | custom-call | tf_op jit(solution)/shard_map/update/pallas_call | solution.py:317
  (191 shorter events, 56.6 us)
Async XLA Ops:
  2.6 10.0 %collective-permute-start.6 = (bf16[96,768]{1,0:T(8,128)(2,1)S(1)}, bf16[96,768]{1,0:T(8,128)(2,1)S(1)}, u32[]{:S(2)}, u32[]{:S(2)}) collective-permute-start(bf16[96,768]{1,0:T(8,128)(2,1)S(1)} %pad_maximum_fusion.3), channel_id=1, source_target_pairs={{0,24},{2,26},{4,28},{6,30},{8,16},{10,18},{12,20},{14,22},{16,8},... | collective-permute-start | bytes 442376 | tf_op jit(solution)/shard_map/ppermute | solution.py:665
  7.7 16.6 %collective-permute-start.4 = (bf16[96,768]{1,0:T(8,128)(2,1)S(1)}, bf16[96,768]{1,0:T(8,128)(2,1)S(1)}, u32[]{:S(2)}, u32[]{:S(2)}) collective-permute-start(bf16[96,768]{1,0:T(8,128)(2,1)S(1)} %pad_maximum_fusion.3), channel_id=1, source_target_pairs={{0,16},{2,18},{4,20},{6,22},{8,24},{10,26},{12,28},{14,30},{16,0},... | collective-permute-start | bytes 442376 | tf_op jit(solution)/shard_map/ppermute | solution.py:665
  8.8 15.6 %collective-permute-start.2 = (bf16[288,768]{1,0:T(8,128)(2,1)S(1)}, bf16[288,768]{1,0:T(8,128)(2,1)S(1)}, u32[]{:S(2)}, u32[]{:S(2)}) collective-permute-start(bf16[288,768]{1,0:T(8,128)(2,1)S(1)} %pad_maximum_fusion.s0), channel_id=1, source_target_pairs={{0,4},{1,3},{2,6},{3,1},{4,0},{5,7},{6,2},{7,5},{8,12},{9,11},{10,... | collective-permute-start | bytes 1327112 | tf_op jit(solution)/shard_map/ppermute | solution.py:661
  10.3 15.6 %collective-permute-start.1 = (bf16[288,768]{1,0:T(8,128)(2,1)S(1)}, bf16[288,768]{1,0:T(8,128)(2,1)S(1)}, u32[]{:S(2)}, u32[]{:S(2)}) collective-permute-start(bf16[288,768]{1,0:T(8,128)(2,1)S(1)} %pad_maximum_fusion.s0), channel_id=1, source_target_pairs={{0,2},{1,5},{2,0},{3,7},{4,6},{5,1},{6,4},{7,3},{8,10},{9,13},{10,... | collective-permute-start | bytes 1327112 | tf_op jit(solution)/shard_map/ppermute | solution.py:657
  11.8 12.5 %collective-permute-start.5 = (bf16[96,768]{1,0:T(8,128)(2,1)S(1)}, bf16[96,768]{1,0:T(8,128)(2,1)S(1)}, u32[]{:S(2)}, u32[]{:S(2)}) collective-permute-start(bf16[96,768]{1,0:T(8,128)(2,1)S(1)} %pad_maximum_fusion.3), channel_id=1, source_target_pairs={{0,8},{2,10},{4,12},{6,14},{8,0},{10,2},{12,4},{14,6},{16,24},{18,... | collective-permute-start | bytes 442376 | tf_op jit(solution)/shard_map/ppermute | solution.py:665
  12.6 15.3 %collective-permute-start.17 = (bf16[96,768]{1,0:T(8,128)(2,1)S(1)}, bf16[96,768]{1,0:T(8,128)(2,1)S(1)}, u32[]{:S(2)}, u32[]{:S(2)}) collective-permute-start(bf16[96,768]{1,0:T(8,128)(2,1)S(1)} %bitcast_convert_fusion), channel_id=1, source_target_pairs={{0,16},{2,18},{4,20},{6,22},{8,24},{10,26},{12,28},{14,30},{16,0},... | collective-permute-start | bytes 442376 | tf_op jit(solution)/shard_map/ppermute | solution.py:665
  24.4 13.5 %collective-permute-start.8 = (bf16[288,768]{1,0:T(8,128)(2,1)S(1)}, bf16[288,768]{1,0:T(8,128)(2,1)S(1)}, u32[]{:S(2)}, u32[]{:S(2)}) collective-permute-start(bf16[288,768]{1,0:T(8,128)(2,1)S(1)} %constant_dynamic-update-slice_fusion.z0), channel_id=1, source_target_pairs={{0,4},{1,3},{2,6},{3,1},{4,0},{5,7},{6,2},{7,5},{8,12},{9,11},{10,... | collective-permute-start | bytes 1327112 | tf_op jit(solution)/shard_map/ppermute | solution.py:661
  26.0 13.5 %collective-permute-start.7 = (bf16[288,768]{1,0:T(8,128)(2,1)S(1)}, bf16[288,768]{1,0:T(8,128)(2,1)S(1)}, u32[]{:S(2)}, u32[]{:S(2)}) collective-permute-start(bf16[288,768]{1,0:T(8,128)(2,1)S(1)} %constant_dynamic-update-slice_fusion.z0), channel_id=1, source_target_pairs={{0,2},{1,5},{2,0},{3,7},{4,6},{5,1},{6,4},{7,3},{8,10},{9,13},{10,... | collective-permute-start | bytes 1327112 | tf_op jit(solution)/shard_map/ppermute | solution.py:657
  27.4 13.6 %collective-permute-start.3 = (bf16[288,768]{1,0:T(8,128)(2,1)S(1)}, bf16[288,768]{1,0:T(8,128)(2,1)S(1)}, u32[]{:S(2)}, u32[]{:S(2)}) collective-permute-start(bf16[288,768]{1,0:T(8,128)(2,1)S(1)} %collective-permute-done.1.s1), channel_id=1, source_target_pairs={{0,4},{1,3},{2,6},{3,1},{4,0},{5,7},{6,2},{7,5},{8,12},{9,11},{10,... | collective-permute-start | bytes 1327112 | tf_op jit(solution)/shard_map/ppermute | solution.py:661
  28.0 9.8 %collective-permute-start.18 = (bf16[192,768]{1,0:T(8,128)(2,1)S(1)}, bf16[192,768]{1,0:T(8,128)(2,1)S(1)}, u32[]{:S(2)}, u32[]{:S(2)}) collective-permute-start(bf16[192,768]{1,0:T(8,128)(2,1)S(1)} %pad_maximum_fusion.1), channel_id=1, source_target_pairs={{0,8},{2,10},{4,12},{6,14},{8,0},{10,2},{12,4},{14,6},{16,24},{18,... | collective-permute-start | bytes 884744 | tf_op jit(solution)/shard_map/ppermute | solution.py:665
  28.1 13.5 %collective-permute-start.22 = (bf16[96,768]{1,0:T(8,128)(2,1)S(1)}, bf16[96,768]{1,0:T(8,128)(2,1)S(1)}, u32[]{:S(2)}, u32[]{:S(2)}) collective-permute-start(bf16[96,768]{1,0:T(8,128)(2,1)S(1)} %convert_element_type.78), channel_id=1, source_target_pairs={{0,16},{2,18},{4,20},{6,22},{8,24},{10,26},{12,28},{14,30},{16,0},... | collective-permute-start | bytes 442376 | tf_op jit(solution)/shard_map/ppermute | solution.py:665
  37.8 12.7 %collective-permute-start.20 = (bf16[288,768]{1,0:T(8,128)(2,1)S(1)}, bf16[288,768]{1,0:T(8,128)(2,1)S(1)}, u32[]{:S(2)}, u32[]{:S(2)}) collective-permute-start(bf16[288,768]{1,0:T(8,128)(2,1)S(1)} %constant_dynamic-update-slice_fusion.3.z0), channel_id=1, source_target_pairs={{0,4},{1,3},{2,6},{3,1},{4,0},{5,7},{6,2},{7,5},{8,12},{9,11},{10,... | collective-permute-start | bytes 1327112 | tf_op jit(solution)/shard_map/ppermute | solution.py:661
  39.4 13.2 %collective-permute-start.19 = (bf16[288,768]{1,0:T(8,128)(2,1)S(1)}, bf16[288,768]{1,0:T(8,128)(2,1)S(1)}, u32[]{:S(2)}, u32[]{:S(2)}) collective-permute-start(bf16[288,768]{1,0:T(8,128)(2,1)S(1)} %constant_dynamic-update-slice_fusion.3.z0), channel_id=1, source_target_pairs={{0,2},{1,5},{2,0},{3,7},{4,6},{5,1},{6,4},{7,3},{8,10},{9,13},{10,... | collective-permute-start | bytes 1327112 | tf_op jit(solution)/shard_map/ppermute | solution.py:657
  41.0 14.7 %collective-permute-start.9 = (bf16[288,768]{1,0:T(8,128)(2,1)S(1)}, bf16[288,768]{1,0:T(8,128)(2,1)S(1)}, u32[]{:S(2)}, u32[]{:S(2)}) collective-permute-start(bf16[288,768]{1,0:T(8,128)(2,1)S(1)} %collective-permute-done.7.z1), channel_id=1, source_target_pairs={{0,4},{1,3},{2,6},{3,1},{4,0},{5,7},{6,2},{7,5},{8,12},{9,11},{10,... | collective-permute-start | bytes 1327112 | tf_op jit(solution)/shard_map/ppermute | solution.py:661
  41.5 9.0 %collective-permute-start.23 = (bf16[192,768]{1,0:T(8,128)(2,1)S(1)}, bf16[192,768]{1,0:T(8,128)(2,1)}, u32[]{:S(2)}, u32[]{:S(2)}) collective-permute-start(bf16[192,768]{1,0:T(8,128)(2,1)S(1)} %pad_maximum_fusion.2), channel_id=1, source_target_pairs={{0,8},{2,10},{4,12},{6,14},{8,0},{10,2},{12,4},{14,6},{16,24},{18,... | collective-permute-start | bytes 884744 | tf_op jit(solution)/shard_map/ppermute | solution.py:665
  44.1 15.7 %collective-permute-start.10 = (bf16[384,768]{1,0:T(8,128)(2,1)S(1)}, bf16[384,768]{1,0:T(8,128)(2,1)S(1)}, u32[]{:S(2)}, u32[]{:S(2)}) collective-permute-start(bf16[384,768]{1,0:T(8,128)(2,1)S(1)} %get-tuple-element.93.so), channel_id=1, source_target_pairs={{0,1},{1,0},{2,3},{3,2},{4,5},{5,4},{6,7},{7,6},{8,9},{9,8},{10,11... | collective-permute-start | bytes 1769480 | tf_op jit(solution)/shard_map/ppermute | solution.py:653
  56.7 15.1 %collective-permute-start.24 = (bf16[288,768]{1,0:T(8,128)(2,1)S(1)}, bf16[288,768]{1,0:T(8,128)(2,1)S(1)}, u32[]{:S(2)}, u32[]{:S(2)}) collective-permute-start(bf16[288,768]{1,0:T(8,128)(2,1)S(1)} %constant_dynamic-update-slice_fusion.5.z0), channel_id=1, source_target_pairs={{0,2},{1,5},{2,0},{3,7},{4,6},{5,1},{6,4},{7,3},{8,10},{9,13},{10,... | collective-permute-start | bytes 1327112 | tf_op jit(solution)/shard_map/ppermute | solution.py:657
  58.3 13.5 %collective-permute-start.21 = (bf16[288,768]{1,0:T(8,128)(2,1)}, bf16[288,768]{1,0:T(8,128)(2,1)S(1)}, u32[]{:S(2)}, u32[]{:S(2)}) collective-permute-start(bf16[288,768]{1,0:T(8,128)(2,1)} %copy-done.9), channel_id=1, source_target_pairs={{0,4},{1,3},{2,6},{3,1},{4,0},{5,7},{6,2},{7,5},{8,12},{9,11},{10,... | collective-permute-start | bytes 1327112 | tf_op jit(solution)/shard_map/ppermute | solution.py:661
  67.3 10.4 %collective-permute-start.25 = (bf16[288,768]{1,0:T(8,128)(2,1)S(1)}, bf16[288,768]{1,0:T(8,128)(2,1)S(1)}, u32[]{:S(2)}, u32[]{:S(2)}) collective-permute-start(bf16[288,768]{1,0:T(8,128)(2,1)S(1)} %constant_dynamic-update-slice_fusion.5.z0), channel_id=1, source_target_pairs={{0,4},{1,3},{2,6},{3,1},{4,0},{5,7},{6,2},{7,5},{8,12},{9,11},{10,... | collective-permute-start | bytes 1327112 | tf_op jit(solution)/shard_map/ppermute | solution.py:661
  86.7 16.3 %collective-permute-start.32 = (bf16[768,768]{1,0:T(8,128)(2,1)S(1)}, bf16[768,768]{1,0:T(8,128)(2,1)S(1)}, u32[]{:S(2)}, u32[]{:S(2)}) collective-permute-start(bf16[768,768]{1,0:T(8,128)(2,1)S(1)} %grad_down_away.1), channel_id=1, source_target_pairs={{0,4},{1,3},{2,6},{3,1},{4,0},{5,7},{6,2},{7,5},{8,12},{9,11},{10,... | collective-permute-start | bytes 3538952 | tf_op jit(solution)/shard_map/ppermute | solution.py:661
  93.1 28.8 %collective-permute-start.36 = (bf16[768,768]{1,0:T(8,128)(2,1)S(1)}, bf16[768,768]{1,0:T(8,128)(2,1)S(1)}, u32[]{:S(2)}, u32[]{:S(2)}) collective-permute-start(bf16[768,768]{1,0:T(8,128)(2,1)S(1)} %grad_up_away.1), channel_id=1, source_target_pairs={{0,4},{1,3},{2,6},{3,1},{4,0},{5,7},{6,2},{7,5},{8,12},{9,11},{10,... | collective-permute-start | bytes 3538952 | tf_op jit(solution)/shard_map/ppermute | solution.py:661
  103.1 16.3 %collective-permute-start.33 = (bf16[384,768]{1,0:T(8,128)(2,1)S(1)}, bf16[384,768]{1,0:T(8,128)(2,1)S(1)}, u32[]{:S(2)}, u32[]{:S(2)}) collective-permute-start(bf16[384,768]{1,0:T(8,128)(2,1)S(1)} %add_convert_fusion.2), channel_id=1, source_target_pairs={{0,2},{1,5},{2,0},{3,7},{4,6},{5,1},{6,4},{7,3},{8,10},{9,13},{10,... | collective-permute-start | bytes 1769480 | tf_op jit(solution)/shard_map/ppermute | solution.py:657
  119.5 22.5 %collective-permute-start.34 = (bf16[768,768]{1,0:T(8,128)(2,1)S(1)}, bf16[768,768]{1,0:T(8,128)(2,1)S(1)}, u32[]{:S(2)}, u32[]{:S(2)}) collective-permute-start(bf16[768,768]{1,0:T(8,128)(2,1)S(1)} %mix_away.1), channel_id=1, source_target_pairs={{0,4},{1,3},{2,6},{3,1},{4,0},{5,7},{6,2},{7,5},{8,12},{9,11},{10,... | collective-permute-start | bytes 3538952 | tf_op jit(solution)/shard_map/ppermute | solution.py:661
  122.0 20.6 %collective-permute-start.37 = (bf16[384,768]{1,0:T(8,128)(2,1)S(1)}, bf16[384,768]{1,0:T(8,128)(2,1)S(1)}, u32[]{:S(2)}, u32[]{:S(2)}) collective-permute-start(bf16[384,768]{1,0:T(8,128)(2,1)S(1)} %add_convert_fusion), channel_id=1, source_target_pairs={{0,2},{1,5},{2,0},{3,7},{4,6},{5,1},{6,4},{7,3},{8,10},{9,13},{10,... | collective-permute-start | bytes 1769480 | tf_op jit(solution)/shard_map/ppermute | solution.py:657
  128.7 16.7 %collective-permute-start.45 = (bf16[96,768]{1,0:T(8,128)(2,1)S(1)}, bf16[96,768]{1,0:T(8,128)(2,1)S(1)}, u32[]{:S(2)}, u32[]{:S(2)}) collective-permute-start(bf16[96,768]{1,0:T(8,128)(2,1)S(1)} %get-tuple-element.172), channel_id=1, source_target_pairs={{0,16},{2,18},{4,20},{6,22},{8,24},{10,26},{12,28},{14,30},{16,0},... | collective-permute-start | bytes 442376 | tf_op jit(solution)/shard_map/ppermute | solution.py:665
  129.1 17.4 %collective-permute-start.46 = (bf16[96,768]{1,0:T(8,128)(2,1)S(1)}, bf16[96,768]{1,0:T(8,128)(2,1)S(1)}, u32[]{:S(2)}, u32[]{:S(2)}) collective-permute-start(bf16[96,768]{1,0:T(8,128)(2,1)S(1)} %get-tuple-element.173), channel_id=1, source_target_pairs={{0,24},{2,26},{4,28},{6,30},{8,16},{10,18},{12,20},{14,22},{16,8},... | collective-permute-start | bytes 442376 | tf_op jit(solution)/shard_map/ppermute | solution.py:665
  131.1 11.8 %collective-permute-start.38 = (bf16[96,768]{1,0:T(8,128)(2,1)S(1)}, bf16[96,768]{1,0:T(8,128)(2,1)S(1)}, u32[]{:S(2)}, u32[]{:S(2)}) collective-permute-start(bf16[96,768]{1,0:T(8,128)(2,1)S(1)} %get-tuple-element.174), channel_id=1, source_target_pairs={{0,8},{2,10},{4,12},{6,14},{8,0},{10,2},{12,4},{14,6},{16,24},{18,... | collective-permute-start | bytes 442376 | tf_op jit(solution)/shard_map/ppermute | solution.py:665
  142.1 9.9 %collective-permute-start.35 = (bf16[384,768]{1,0:T(8,128)(2,1)S(1)}, bf16[384,768]{1,0:T(8,128)(2,1)S(1)}, u32[]{:S(2)}, u32[]{:S(2)}) collective-permute-start(bf16[384,768]{1,0:T(8,128)(2,1)S(1)} %add_convert_fusion.1), channel_id=1, source_target_pairs={{0,2},{1,5},{2,0},{3,7},{4,6},{5,1},{6,4},{7,3},{8,10},{9,13},{10,... | collective-permute-start | bytes 1769480 | tf_op jit(solution)/shard_map/ppermute | solution.py:657
  143.0 17.3 %collective-permute-start.43 = (bf16[96,768]{1,0:T(8,128)(2,1)S(1)}, bf16[96,768]{1,0:T(8,128)(2,1)S(1)}, u32[]{:S(2)}, u32[]{:S(2)}) collective-permute-start(bf16[96,768]{1,0:T(8,128)(2,1)S(1)} %get-tuple-element.175), channel_id=1, source_target_pairs={{0,16},{2,18},{4,20},{6,22},{8,24},{10,26},{12,28},{14,30},{16,0},... | collective-permute-start | bytes 442376 | tf_op jit(solution)/shard_map/ppermute | solution.py:665
  143.4 16.9 %collective-permute-start.44 = (bf16[96,768]{1,0:T(8,128)(2,1)S(1)}, bf16[96,768]{1,0:T(8,128)(2,1)S(1)}, u32[]{:S(2)}, u32[]{:S(2)}) collective-permute-start(bf16[96,768]{1,0:T(8,128)(2,1)S(1)} %get-tuple-element.176), channel_id=1, source_target_pairs={{0,24},{2,26},{4,28},{6,30},{8,16},{10,18},{12,20},{14,22},{16,8},... | collective-permute-start | bytes 442376 | tf_op jit(solution)/shard_map/ppermute | solution.py:665
  145.4 10.4 %collective-permute-start.39 = (bf16[96,768]{1,0:T(8,128)(2,1)S(1)}, bf16[96,768]{1,0:T(8,128)(2,1)S(1)}, u32[]{:S(2)}, u32[]{:S(2)}) collective-permute-start(bf16[96,768]{1,0:T(8,128)(2,1)S(1)} %get-tuple-element.177), channel_id=1, source_target_pairs={{0,8},{2,10},{4,12},{6,14},{8,0},{10,2},{12,4},{14,6},{16,24},{18,... | collective-permute-start | bytes 442376 | tf_op jit(solution)/shard_map/ppermute | solution.py:665
  157.5 12.6 %collective-permute-start.40 = (bf16[96,768]{1,0:T(8,128)(2,1)S(1)}, bf16[96,768]{1,0:T(8,128)(2,1)S(1)}, u32[]{:S(2)}, u32[]{:S(2)}) collective-permute-start(bf16[96,768]{1,0:T(8,128)(2,1)S(1)} %get-tuple-element.180), channel_id=1, source_target_pairs={{0,16},{2,18},{4,20},{6,22},{8,24},{10,26},{12,28},{14,30},{16,0},... | collective-permute-start | bytes 442376 | tf_op jit(solution)/shard_map/ppermute | solution.py:665
  (55 other events, 551.3 us)
